TPU v7x, 128 devices: a whole 4x4x4 slice. The times are simulated.
128 devices in a mesh: lon: 32 (over x_hi, y, z), lat: 4 (over x_lo, core).
Axes of the slice: x: 4 (x_hi: 2, x_lo: 2; x = x_hi * 2 + x_lo), y: 4, z: 4, core: 2. Of those that a mesh axis runs over, the one named last changes fastest.
Arguments:
- background: float32 [32, 512, 69], P('lat', 'lon'), may hold values from -6 to 6
- direction: float32 [32, 512, 69], P('lat', 'lon'), may hold values from -6 to 6
- obs_owner: int32 [65536, 1], P(('lon', 'lat')), may hold values from 0 to 127; in each aligned block of 512 rows (0 to 511, 512 to 1023, ...) at most 8 rows name the same one
- obs_site: int32 [65536], P(('lon', 'lat')), may hold values from 0 to 7658, as said below
- obs_weights: float32 [65536, 4], P(('lon', 'lat')), as said below
- obs_precision: float32 [65536], P(('lon', 'lat')), may hold values from 0.5 to 4
- embed_weight: bfloat16 [69, 1024], replicated, may hold values from -0.75 to 0.75
- attn_gain: float32 [1024], replicated, may hold values from 0.5 to 1.5
- qkv_weight: bfloat16 [1024, 3072], replicated, may hold values from -0.1875 to 0.1875
- logit_scale: float32 [16], replicated, may hold values from 2 to 10
- out_weight: bfloat16 [1024, 1024], replicated, may hold values from -0.1875 to 0.1875
- decode_gain: float32 [1024], replicated, may hold values from 0.5 to 1.5
- decode_weight: bfloat16 [1024, 69], replicated, may hold values from -0.1875 to 0.1875
Outputs:
- hvp: float32 [32, 512, 69], P('lat', 'lon')
- obs_increment: float32 [65536], P(('lon', 'lat'))
Inputs may be any that keep to these rules, and one draw needn't show every extreme that they name: `obs_owner`: devices are numbered lon index times the lat axis' size plus lat index; among the 512 rows of one device no owner is named more than 8 times. `obs_site`: A base cell has row under 8 - 1 and column under 16 - 1 of the owner's block, so all four corners lie in that block. `obs_weights`: the four weights of a row are nonnegative and sum to one.
All inputs are finite; a program needn't handle non-finite values.
Results may differ from a plain program's by a relative error of at most 0.02.
Values may be sent and summed in bfloat16 or wider, within the bound.
No kernel may reach another device: no remote copies, remote signals or barrier semaphores. Data moves between devices by JAX's collectives and lax.ppermute only.
A program may use at most 128 MiB of HBM per device.

v0:
```python
import jax
import jax.numpy as jnp
from jax import lax
from jax.experimental import pallas as pl
from jax.experimental.pallas import tpu as pltpu
from jax.sharding import PartitionSpec as P

HEADS = 16
WLAT = 8
WLON = 16
CELLS = WLAT * WLON
HALF_LAT = WLAT // 2
HALF_LON = WLON // 2
QUARTER = HALF_LAT * HALF_LON
SLOTS = 8
PIECES = 3

eps_norm = 1e-05
eps_head = 1e-06

f32 = jnp.float32
bf16 = jnp.bfloat16

NN = ((1,), (0,))
NT = ((1,), (1,))
TN = ((0,), (0,))

VMEM = pl.BlockSpec(memory_space=pltpu.VMEM)
SMEM = pl.BlockSpec(memory_space=pltpu.SMEM)
ANY = pl.BlockSpec(memory_space=pl.ANY)


def product(left, right, dims):
    return lax.dot_general(left, right, (dims, ((), ())), preferred_element_type=f32)


def parts_of(value, count):
    parts = []
    for _ in range(count):
        part = value.astype(bf16)
        parts.append(part)
        value = value - part.astype(f32)
    return parts


def quadrants(own, lat_piece, lon_piece, far_piece):
    rows = []
    for left, right in ((own, lon_piece), (lat_piece, far_piece)):
        for i in range(HALF_LAT):
            rows.append(left[i * HALF_LON : (i + 1) * HALF_LON])
            rows.append(right[i * HALF_LON : (i + 1) * HALF_LON])
    return jnp.concatenate(rows, axis=0)


def quadrant_of(cells, row, col):
    return jnp.concatenate(
        [cells[(row + i) * WLON + col : (row + i) * WLON + col + HALF_LON] for i in range(HALF_LAT)], axis=0
    )


def centred_rows(values):
    centred = values - jnp.mean(values, axis=-1, keepdims=True)
    scale = lax.rsqrt(jnp.mean(centred * centred, axis=-1, keepdims=True) + eps_norm)
    return centred * scale, scale


def norm_tangent(unit, scale, tangent):
    moved = tangent - jnp.mean(tangent, axis=-1, keepdims=True)
    return scale * (moved - unit * jnp.mean(unit * moved, axis=-1, keepdims=True))


def strips_kernel(background_ref, direction_ref, lat_ref, lon_ref, far_ref):
    for out_ref, row, col in ((lat_ref, 0, HALF_LON), (lon_ref, HALF_LAT, 0), (far_ref, 0, 0)):
        pieces = []
        for source in (background_ref, direction_ref):
            for i in range(HALF_LAT):
                pieces.append(source[row + i, col : col + HALF_LON, :])
        out_ref[...] = jnp.concatenate(pieces, axis=0).astype(bf16)


def slots_of(owners, rows, devices):
    owner_hot = (lax.broadcasted_iota(jnp.int32, (devices, rows), 0) == owners).astype(f32)
    upper = (
        lax.broadcasted_iota(jnp.int32, (rows, rows), 0) <= lax.broadcasted_iota(jnp.int32, (rows, rows), 1)
    ).astype(bf16)
    counted = product(owner_hot.astype(bf16), upper, NN)
    slots = jnp.sum(counted * owner_hot, axis=0, keepdims=True) - 1.0
    return owner_hot, slots


def pack_kernel(owner_ref, site_ref, weights_ref, precision_ref, out_ref, slots_ref):
    rows = owner_ref.shape[1]
    devices = out_ref.shape[0]
    owner_hot, slots = slots_of(owner_ref[...], rows, devices)
    slots_ref[...] = slots
    payload = jnp.concatenate(
        [weights_ref[...], precision_ref[...], site_ref[...].astype(f32), jnp.zeros((2, rows), f32)], axis=0
    )
    owner_hot = owner_hot.astype(bf16)
    spread = jnp.concatenate([jnp.where(slots == float(k), payload, 0.0) for k in range(SLOTS)], axis=0)
    out = jnp.zeros((devices, SLOTS * 8), f32)
    for part in parts_of(spread, PIECES):
        out = out + product(owner_hot, part, NT)
    out_ref[...] = out


def unpack_kernel(owner_ref, slots_ref, returned_ref, out_ref):
    rows = owner_ref.shape[1]
    devices = returned_ref.shape[0]
    owner_hot = (lax.broadcasted_iota(jnp.int32, (devices, rows), 0) == owner_ref[...]).astype(bf16)
    picked = jnp.zeros((SLOTS, rows), f32)
    for part in parts_of(returned_ref[...], PIECES):
        picked = picked + product(part, owner_hot, TN)
    slot_hot = lax.broadcasted_iota(jnp.int32, (SLOTS, rows), 0).astype(f32) == slots_ref[...]
    out_ref[...] = jnp.sum(jnp.where(slot_hot, picked, 0.0), axis=0, keepdims=True)


def forward_kernel(
    lat_ref,
    logit_ref,
    background_ref,
    direction_ref,
    lat_piece,
    lon_piece,
    far_piece,
    embed_ref,
    gain_ref,
    decode_gain_ref,
    decode_ref,
    qkv_hbm,
    outw_hbm,
    lat_out,
    lon_out,
    far_out,
    own_out,
    hidden_out,
    block_out,
    unit_q_out,
    unit_k_out,
    scale_q_out,
    scale_k_out,
    value_out,
    probs_out,
    qkv_ref,
    outw_ref,
    packed_ref,
    mixed_ref,
    sems,
):
    width = embed_ref.shape[1]
    chunk = 512
    copies = []
    chunks = []
    for group in range(width // chunk):
        for third in range(3):
            columns = pl.ds(third * width + group * chunk, chunk)
            chunks.append(columns)
            copies.append(
                pltpu.make_async_copy(qkv_hbm.at[:, columns], qkv_ref.at[:, columns], sems.at[len(copies)])
            )
    copies.append(pltpu.make_async_copy(outw_hbm, outw_ref, sems.at[len(copies)]))
    for copy in copies:
        copy.start()

    states = []
    for number, source in enumerate((background_ref, direction_ref)):
        own = jnp.concatenate([source[HALF_LAT + i, HALF_LON:, :] for i in range(HALF_LAT)], axis=0)
        part = slice(number * QUARTER, (number + 1) * QUARTER)
        received = [piece[part, :].astype(f32) for piece in (lat_piece, lon_piece, far_piece)]
        states.append(quadrants(own, *received))
    states = jnp.concatenate(states, axis=0).astype(bf16)
    hidden = product(states, embed_ref[...], NN).astype(bf16)
    hidden_out[...] = hidden[:CELLS]
    hidden = hidden.astype(f32)
    unit, scale = centred_rows(hidden[:CELLS])
    moved = norm_tangent(unit, scale, hidden[CELLS:])
    gain = gain_ref[...]
    normed = jnp.concatenate([unit * gain, moved * gain], axis=0).astype(bf16)

    lane = lax.broadcasted_iota(jnp.int32, (1, 128), 1)
    first = lane < 64
    same_head = (
        (lax.broadcasted_iota(jnp.int32, (128, 128), 0) < 64) == (lax.broadcasted_iota(jnp.int32, (128, 128), 1) < 64)
    ).astype(bf16)
    low_q = lax.broadcasted_iota(jnp.int32, (CELLS, CELLS), 0) < CELLS // 2
    low_k = lax.broadcasted_iota(jnp.int32, (CELLS, CELLS), 1) < CELLS // 2
    allowed = jnp.logical_or(low_q == low_k, lat_ref[0] == 0).astype(f32)

    for group in range(width // chunk):
        for third in range(3):
            number = group * 3 + third
            copies[number].wait()
            packed_ref[:, chunks[number]] = product(normed, qkv_ref[:, chunks[number]], NN)
        for pair in range(group * chunk // 128, (group + 1) * chunk // 128):
            here = pl.ds(pair * 128, 128)
            units = []
            for third, unit_out, scale_out in ((0, unit_q_out, scale_q_out), (1, unit_k_out, scale_k_out)):
                both = packed_ref[:, pl.ds(third * width + pair * 128, 128)]
                raw, raw_tan = both[:CELLS], both[CELLS:]
                head_scale = lax.rsqrt(product((raw * raw).astype(bf16), same_head, NN) + eps_head)
                unit = raw * head_scale
                along = product((unit * raw_tan).astype(bf16), same_head, NN)
                unit_tan = head_scale * (raw_tan - unit * along)
                scale_out[:, here] = head_scale
                unit = unit.astype(bf16)
                unit_out[:, here] = unit
                units.append((unit, unit_tan.astype(bf16)))
            (query, query_tan), (key, key_tan) = units
            both = packed_ref[:, pl.ds(2 * width + pair * 128, 128)].astype(bf16)
            value, value_tan = both[:CELLS], both[CELLS:]
            value_out[:, here] = value
            stacked = jnp.concatenate([value, value_tan], axis=0)
            crossed = jnp.concatenate([key_tan, key], axis=1)
            results = []
            for side in range(2):
                head = pair * 2 + side
                mine = first if side == 0 else jnp.logical_not(first)
                zero = jnp.zeros((), bf16)
                query_here = jnp.where(mine, query, zero)
                query_tan_here = jnp.where(mine, query_tan, zero)
                logit = logit_ref[head]
                scores = product(query_here, key, NT)
                scores_tan = product(jnp.concatenate([query_here, query_tan_here], axis=1), crossed, NT) * logit
                weights = jnp.exp(scores * logit) * allowed
                probs = weights * (1.0 / jnp.sum(weights, axis=-1, keepdims=True))
                probs_tan = probs * (scores_tan - jnp.sum(probs * scores_tan, axis=-1, keepdims=True))
                probs = probs.astype(bf16)
                probs_out[head] = probs
                results.append(
                    (
                        product(probs, value, NN),
                        product(jnp.concatenate([probs_tan.astype(bf16), probs], axis=1), stacked, NN),
                    )
                )
            for number, rows in ((0, pl.ds(0, CELLS)), (1, pl.ds(CELLS, CELLS))):
                mixed_ref[rows, here] = jnp.where(first, results[0][number], results[1][number]).astype(bf16)

    copies[-1].wait()
    update = product(mixed_ref[...], outw_ref[...], NN)
    block = (hidden + update).astype(bf16)
    block_out[...] = block[:CELLS]
    block = block.astype(f32)
    unit, scale = centred_rows(block[:CELLS])
    moved = norm_tangent(unit, scale, block[CELLS:])
    change = product((moved * decode_gain_ref[...]).astype(bf16), decode_ref[...], NT)
    lat_out[...] = quadrant_of(change, HALF_LAT, 0).astype(bf16)
    lon_out[...] = quadrant_of(change, 0, HALF_LON).astype(bf16)
    far_out[...] = quadrant_of(change, HALF_LAT, HALF_LON).astype(bf16)
    own_out[...] = quadrant_of(change, 0, 0).astype(bf16)


def observe_kernel(
    direction_ref,
    own_piece,
    lat_piece,
    lon_piece,
    far_piece,
    arrived_ref,
    at_obs_out,
    adjoint_out,
    own_out,
    lat_out,
    lon_out,
    far_out,
):
    var_count = direction_ref.shape[2]
    devices = arrived_ref.shape[0]
    pieces = [piece[...].astype(f32) for piece in (far_piece, lon_piece, lat_piece, own_piece)]
    moved = quadrants(*pieces)
    tangent = jnp.concatenate([direction_ref[i] for i in range(WLAT)], axis=0) + moved
    arrived = jnp.transpose(arrived_ref[...])
    cell_ids = lax.broadcasted_iota(jnp.int32, (CELLS, devices), 0).astype(f32)
    var_ids = lax.broadcasted_iota(jnp.int32, (var_count, devices), 0).astype(f32)
    selectors, var_hots, precisions = [], [], []
    for k in range(SLOTS):
        row = arrived[k * 8 : (k + 1) * 8]
        site = row[5:6]
        cell = jnp.floor((site + 0.5) * (1.0 / var_count))
        variable = site - cell * var_count
        selector = jnp.zeros((CELLS, devices), f32)
        for corner, offset in enumerate((0, 1, WLON, WLON + 1)):
            selector = selector + jnp.where(cell_ids == cell + float(offset), row[corner : corner + 1], 0.0)
        selectors.append(selector)
        var_hots.append((var_ids == variable).astype(f32))
        precisions.append(row[4:5])
    selector = jnp.concatenate(selectors, axis=1)
    var_hot = jnp.concatenate(var_hots, axis=1)
    precision = jnp.concatenate(precisions, axis=1)
    selector_parts = parts_of(selector, 2)
    tangent_parts = parts_of(tangent, 3)
    picked = product(tangent_parts[0], selector_parts[0], TN)
    for left, right in ((1, 0), (0, 1), (2, 0)):
        picked = picked + product(tangent_parts[left], selector_parts[right], TN)
    at_obs = jnp.sum(picked * var_hot, axis=0, keepdims=True)
    at_obs_out[...] = jnp.transpose(
        jnp.concatenate([at_obs[:, k * devices : (k + 1) * devices] for k in range(SLOTS)], axis=0)
    )
    spread_parts = parts_of(var_hot * (at_obs * precision), 2)
    adjoint = product(selector_parts[0], spread_parts[0], NT)
    for left, right in ((1, 0), (0, 1)):
        adjoint = adjoint + product(selector_parts[left], spread_parts[right], NT)
    for i in range(WLAT):
        adjoint_out[i] = adjoint[i * WLON : (i + 1) * WLON]
    own_out[...] = quadrant_of(adjoint, HALF_LAT, HALF_LON).astype(bf16)
    lat_out[...] = quadrant_of(adjoint, 0, HALF_LON).astype(bf16)
    lon_out[...] = quadrant_of(adjoint, HALF_LAT, 0).astype(bf16)
    far_out[...] = quadrant_of(adjoint, 0, 0).astype(bf16)


def adjoint_kernel(
    logit_ref,
    own_piece,
    lat_piece,
    lon_piece,
    far_piece,
    embed_ref,
    gain_ref,
    decode_gain_ref,
    decode_ref,
    hidden_ref,
    block_ref,
    unit_q_ref,
    unit_k_ref,
    scale_q_ref,
    scale_k_ref,
    value_ref,
    probs_ref,
    qkv_hbm,
    outw_hbm,
    own_out,
    lat_out,
    lon_out,
    far_out,
    qkv_ref,
    outw_ref,
    packed_ref,
    sems,
):
    width = embed_ref.shape[1]
    out_copy = pltpu.make_async_copy(outw_hbm, outw_ref, sems.at[0])
    qkv_copy = pltpu.make_async_copy(qkv_hbm, qkv_ref, sems.at[1])
    out_copy.start()
    qkv_copy.start()

    change = quadrants(*[piece[...].astype(f32) for piece in (own_piece, lat_piece, lon_piece, far_piece)])
    unit, scale = centred_rows(block_ref[...].astype(f32))
    normed_ct = product(change.astype(bf16), decode_ref[...], NN).astype(bf16).astype(f32) * decode_gain_ref[...]
    block_ct = norm_tangent(unit, scale, normed_ct).astype(bf16)
    out_copy.wait()
    mixed_ct = product(block_ct, outw_ref[...], NT).astype(bf16)

    lane = lax.broadcasted_iota(jnp.int32, (1, 128), 1)
    first = lane < 64
    same_head = (
        (lax.broadcasted_iota(jnp.int32, (128, 128), 0) < 64) == (lax.broadcasted_iota(jnp.int32, (128, 128), 1) < 64)
    ).astype(bf16)
    for pair in range(width // 128):
        here = pl.ds(pair * 128, 128)
        query, key, value = unit_q_ref[:, here], unit_k_ref[:, here], value_ref[:, here]
        mixed_here = mixed_ct[:, pair * 128 : (pair + 1) * 128]
        results = []
        for side in range(2):
            head = pair * 2 + side
            mine = first if side == 0 else jnp.logical_not(first)
            probs = probs_ref[head]
            probs_ct = product(jnp.where(mine, mixed_here, jnp.zeros((), bf16)), value, NT)
            probs_wide = probs.astype(f32)
            scores_ct = probs_wide * (probs_ct - jnp.sum(probs_wide * probs_ct, axis=-1, keepdims=True))
            scores_ct = (scores_ct * logit_ref[head]).astype(bf16)
            results.append(
                (product(scores_ct, key, NN), product(scores_ct, query, TN), product(probs, mixed_here, TN))
            )
        for third, unit_ref, scale_ref in ((0, unit_q_ref, scale_q_ref), (1, unit_k_ref, scale_k_ref)):
            unit_ct = jnp.where(first, results[0][third], results[1][third])
            unit_here = unit_ref[:, here].astype(f32)
            along = product((unit_here * unit_ct).astype(bf16), same_head, NN)
            packed_ref[:, pl.ds(third * width + pair * 128, 128)] = (
                scale_ref[:, here] * (unit_ct - unit_here * along)
            ).astype(bf16)
        packed_ref[:, pl.ds(2 * width + pair * 128, 128)] = jnp.where(first, results[0][2], results[1][2]).astype(bf16)

    qkv_copy.wait()
    normed_ct = product(packed_ref[...], qkv_ref[...], NT).astype(bf16).astype(f32) * gain_ref[...]
    unit, scale = centred_rows(hidden_ref[...].astype(f32))
    hidden_ct = (norm_tangent(unit, scale, normed_ct) + block_ct.astype(f32)).astype(bf16)
    state = product(hidden_ct, embed_ref[...], NT)
    lat_out[...] = quadrant_of(state, HALF_LAT, 0).astype(bf16)
    lon_out[...] = quadrant_of(state, 0, HALF_LON).astype(bf16)
    far_out[...] = quadrant_of(state, HALF_LAT, HALF_LON).astype(bf16)
    own_out[...] = quadrant_of(state, 0, 0).astype(bf16)


def finish_kernel(adjoint_ref, own_piece, lat_piece, lon_piece, far_piece, out_ref):
    pieces = [piece[...].astype(f32) for piece in (far_piece, lon_piece, lat_piece, own_piece)]
    moved = quadrants(*pieces)
    for i in range(WLAT):
        out_ref[i] = adjoint_ref[i] + moved[i * WLON : (i + 1) * WLON]


def shape(dims, dtype):
    return jax.ShapeDtypeStruct(dims, dtype)


def exchanged(lat_piece, lon_piece, far_piece, steps):
    lat_count, lon_count = lax.axis_size("lat"), lax.axis_size("lon")
    lat_piece = lax.ppermute(lat_piece, "lat", [(i, (i + steps) % lat_count) for i in range(lat_count)])
    lon_piece = lax.ppermute(lon_piece, "lon", [(i, (i + steps) % lon_count) for i in range(lon_count)])
    pairs = [
        (i * lat_count + j, ((i + steps) % lon_count) * lat_count + (j + steps) % lat_count)
        for i in range(lon_count)
        for j in range(lat_count)
    ]
    far_piece = lax.ppermute(far_piece, ("lon", "lat"), pairs)
    return lat_piece, lon_piece, far_piece


def per_device(
    background,
    direction,
    obs_owner,
    obs_site,
    obs_weights,
    obs_precision,
    embed_weight,
    attn_gain,
    qkv_weight,
    logit_scale,
    out_weight,
    decode_gain,
    decode_weight,
):
    var_count = background.shape[2]
    width = embed_weight.shape[1]
    devices = lax.axis_size("lat") * lax.axis_size("lon")
    obs_rows = obs_site.shape[0]
    last_band = (lax.axis_index("lat") == lax.axis_size("lat") - 1).astype(jnp.int32).reshape(1)
    gain = attn_gain.reshape(1, width)
    decode_gain = decode_gain.reshape(1, width)
    decode_rows = decode_weight.T
    params = pltpu.CompilerParams(vmem_limit_bytes=40 * 1024 * 1024)
    quarter = shape((QUARTER, var_count), bf16)

    strips = pl.pallas_call(
        strips_kernel,
        out_shape=[shape((2 * QUARTER, var_count), bf16)] * 3,
        in_specs=[VMEM] * 2,
        out_specs=[VMEM] * 3,
        name="strips",
    )(background, direction)
    strips = exchanged(*strips, -1)

    owners = obs_owner.reshape(1, obs_rows)
    outgoing, slots = pl.pallas_call(
        pack_kernel,
        out_shape=[shape((devices, SLOTS * 8), f32), shape((1, obs_rows), f32)],
        in_specs=[VMEM] * 4,
        out_specs=[VMEM] * 2,
        name="pack",
    )(owners, obs_site.reshape(1, obs_rows), obs_weights.T, obs_precision.reshape(1, obs_rows))
    arrived = lax.all_to_all(outgoing, ("lon", "lat"), split_axis=0, concat_axis=0, tiled=True)

    wide = shape((CELLS, width), bf16)
    wide_long = shape((CELLS, width), f32)
    lat_piece, lon_piece, far_piece, own_piece, *kept = pl.pallas_call(
        forward_kernel,
        out_shape=[quarter] * 4
        + [wide, wide, wide, wide, wide_long, wide_long, wide, shape((HEADS, CELLS, CELLS), bf16)],
        in_specs=[SMEM] * 2 + [VMEM] * 9 + [ANY] * 2,
        out_specs=[VMEM] * 12,
        scratch_shapes=[
            pltpu.VMEM((width, 3 * width), bf16),
            pltpu.VMEM((width, width), bf16),
            pltpu.VMEM((2 * CELLS, 3 * width), f32),
            pltpu.VMEM((2 * CELLS, width), bf16),
            pltpu.SemaphoreType.DMA((3 * (width // 512) + 1,)),
        ],
        compiler_params=params,
        cost_estimate=pl.CostEstimate(flops=2_500_000_000, bytes_accessed=10_000_000, transcendentals=300_000),
        name="forward",
    )(
        last_band,
        logit_scale,
        background,
        direction,
        *strips,
        embed_weight,
        gain,
        decode_gain,
        decode_rows,
        qkv_weight,
        out_weight,
    )
    lat_piece, lon_piece, far_piece = exchanged(lat_piece, lon_piece, far_piece, 1)

    at_obs, adjoint_field, own_piece, lat_piece, lon_piece, far_piece = pl.pallas_call(
        observe_kernel,
        out_shape=[shape((devices, SLOTS), f32), shape(background.shape, f32)] + [quarter] * 4,
        in_specs=[VMEM] * 6,
        out_specs=[VMEM] * 6,
        name="observe",
    )(direction, own_piece, lat_piece, lon_piece, far_piece, arrived)
    lat_piece, lon_piece, far_piece = exchanged(lat_piece, lon_piece, far_piece, -1)
    returned = lax.all_to_all(at_obs, ("lon", "lat"), split_axis=0, concat_axis=0, tiled=True)

    own_piece, lat_piece, lon_piece, far_piece = pl.pallas_call(
        adjoint_kernel,
        out_shape=[quarter] * 4,
        in_specs=[SMEM] + [VMEM] * 16 + [ANY] * 2,
        out_specs=[VMEM] * 4,
        scratch_shapes=[
            pltpu.VMEM((width, 3 * width), bf16),
            pltpu.VMEM((width, width), bf16),
            pltpu.VMEM((CELLS, 3 * width), bf16),
            pltpu.SemaphoreType.DMA((2,)),
        ],
        compiler_params=params,
        cost_estimate=pl.CostEstimate(flops=1_500_000_000, bytes_accessed=10_000_000, transcendentals=300_000),
        name="adjoint",
    )(
        logit_scale,
        own_piece,
        lat_piece,
        lon_piece,
        far_piece,
        embed_weight,
        gain,
        decode_gain,
        decode_rows,
        *kept,
        qkv_weight,
        out_weight,
    )
    lat_piece, lon_piece, far_piece = exchanged(lat_piece, lon_piece, far_piece, 1)

    hvp = pl.pallas_call(
        finish_kernel,
        out_shape=shape(background.shape, f32),
        in_specs=[VMEM] * 5,
        out_specs=VMEM,
        name="finish",
    )(adjoint_field, own_piece, lat_piece, lon_piece, far_piece)
    obs_increment = pl.pallas_call(
        unpack_kernel,
        out_shape=shape((1, obs_rows), f32),
        in_specs=[VMEM] * 3,
        out_specs=VMEM,
        name="unpack",
    )(owners, slots, returned)
    return (hvp, obs_increment.reshape(obs_rows))


def solution(mesh):
    in_specs = (
        P("lat", "lon", None),
        P("lat", "lon", None),
        P(("lon", "lat"), None),
        P(("lon", "lat")),
        P(("lon", "lat"), None),
        P(("lon", "lat")),
        P(),
        P(),
        P(),
        P(),
        P(),
        P(),
        P(),
    )
    out_specs = (P("lat", "lon", None), P(("lon", "lat")))
    return jax.shard_map(
        per_device, mesh=mesh, in_specs=in_specs, out_specs=out_specs, check_vma=False
    )
```

profile of v0, /device:TPU:1, one launch (start us, length us, event | category | flops | bytes accessed | tf_op | source)
XLA Modules:
  0.0 116.3 jit_solution(336279899403564328)
XLA Ops:
  0.6 1.5 %strips.1 = (bf16[64,69]{1,0:T(8,128)(2,1)}, bf16[64,69]{1,0:T(8,128)(2,1)}, bf16[64,69]{1,0:T(8,128)(2,1)}) custom-call(f32[8,16,69]{2,1,0:T(8,128)} %background_ref.3, f32[8,16,69]{2,1,0:T(8,128)} %direction_ref.5), custom_call_target="tpu_custom_call" | custom-call | tf_op jit(solution)/shard_map/strips/pallas_call | solution.py:443
  2.2 1.4 %collective-permute-start = (bf16[64,69]{1,0:T(8,128)(2,1)}, bf16[64,69]{1,0:T(8,128)(2,1)S(1)}, u32[]{:S(2)}, u32[]{:S(2)}) collective-permute-start(bf16[64,69]{1,0:T(8,128)(2,1)} %get-tuple-element.29), channel_id=1, source_target_pairs={{0,3},{1,0},{2,1},{3,2},{4,7},{5,4},{6,5},{7,6},{8,11},{9,8},{10,9... | collective-permute-start | bytes 26504 | tf_op jit(solution)/shard_map/ppermute | solution.py:406
  3.6 8.8 %collective-permute-start.1 = (bf16[64,69]{1,0:T(8,128)(2,1)}, bf16[64,69]{1,0:T(8,128)(2,1)S(1)}, u32[]{:S(2)}, u32[]{:S(2)}) collective-permute-start(bf16[64,69]{1,0:T(8,128)(2,1)} %get-tuple-element.30), channel_id=1, source_target_pairs={{0,124},{4,0},{8,4},{12,8},{16,12},{20,16},{24,20},{28,24},{32,28}... | collective-permute-start | bytes 26504 | tf_op jit(solution)/shard_map/ppermute | solution.py:407
  12.3 0.9 collective-permute-start.2
  13.3 1.9 %pack.1 = (f32[128,64]{1,0:T(8,128)}, f32[1,512]{1,0:T(1,128)}) custom-call(s32[1,512]{1,0:T(1,128)} %bitcast.26, s32[1,512]{1,0:T(1,128)} %bitcast.29, f32[4,512]{1,0:T(4,128)} %bitcast.28, f32[1,512]{1,0:T(1,128)} %bitcast.30), custom_call_target="tpu_custom_call" | custom-call | tf_op jit(solution)/shard_map/pack/pallas_call | solution.py:453
  15.2 4.6 %all-to-all-start = ((f32[128,1,64]{2,1,0:T(1,128)}), f32[128,1,64]{2,1,0:T(1,128)}, u32[]{:S(2)}, u32[]{:S(2)}) async-start(f32[128,1,64]{2,1,0:T(1,128)} %bitcast.24), calls=%async_computation | async-start | bytes 131072 | tf_op jit(solution)/shard_map/all_to_all | solution.py:460
  21.7 2.8 %copy-done = bf16[1024,3072]{1,0:T(8,128)(2,1)S(1)} copy-done((bf16[1024,3072]{1,0:T(8,128)(2,1)S(1)}, bf16[1024,3072]{1,0:T(8,128)(2,1)}, u32[]{:S(2)}) %copy-start) | copy-done | bytes 6291480
  24.5 1.6 %copy-done.2 = bf16[1024,1024]{1,0:T(8,128)(2,1)S(1)} copy-done((bf16[1024,1024]{1,0:T(8,128)(2,1)S(1)}, bf16[1024,1024]{1,0:T(8,128)(2,1)}, u32[]{:S(2)}) %copy-start.2) | copy-done | bytes 2097176
  26.1 0.8 copy-done.14
  26.9 0.9 copy-done.15
  27.8 0.9 copy-done.17
  28.7 0.8 copy-done.19
  29.6 0.7 copy-done.23
  30.2 0.7 copy-done.25
  30.9 0.7 copy-done.27
  31.6 0.7 copy-done.30
  32.3 0.7 copy-done.32
  33.0 0.7 copy-done.34
  33.7 11.5 %forward.1 = (bf16[32,69]{1,0:T(8,128)(2,1)S(1)}, bf16[32,69]{1,0:T(8,128)(2,1)S(1)}, bf16[32,69]{1,0:T(8,128)(2,1)S(1)}, bf16[32,69]{1,0:T(8,128)(2,1)S(1)}, bf...) custom-call(s32[1]{0:T(128)} %bitcast.lat_ref, ...), custom_call_target="tpu_custom_call" | custom-call | flops 2500000000 | bytes 10000000 | tf_op jit(solution)/shard_map/forward/pallas_call | solution.py:464
  45.3 0.8 copy-done.4
  46.1 0.7 copy-done.6
  46.8 0.7 copy-done.8
  47.5 0.7 copy-done.10
  48.2 0.7 copy-done.12
  49.5 1.4 %collective-permute-start.3 = (bf16[32,69]{1,0:T(8,128)(2,1)S(1)}, bf16[32,69]{1,0:T(8,128)(2,1)S(1)}, u32[]{:S(2)}, u32[]{:S(2)}) collective-permute-start(bf16[32,69]{1,0:T(8,128)(2,1)S(1)} %get-tuple-element.33), channel_id=1, source_target_pairs={{0,1},{1,2},{2,3},{3,0},{4,5},{5,6},{6,7},{7,4},{8,9},{9,10},{10,1... | collective-permute-start | bytes 13256 | tf_op jit(solution)/shard_map/ppermute | solution.py:406
  50.8 1.5 %collective-permute-start.4 = (bf16[32,69]{1,0:T(8,128)(2,1)S(1)}, bf16[32,69]{1,0:T(8,128)(2,1)S(1)}, u32[]{:S(2)}, u32[]{:S(2)}) collective-permute-start(bf16[32,69]{1,0:T(8,128)(2,1)S(1)} %get-tuple-element.34), channel_id=1, source_target_pairs={{0,4},{4,8},{8,12},{12,16},{16,20},{20,24},{24,28},{28,32},{32,36}... | collective-permute-start | bytes 13256 | tf_op jit(solution)/shard_map/ppermute | solution.py:407
  52.3 1.6 %collective-permute-start.5 = (bf16[32,69]{1,0:T(8,128)(2,1)S(1)}, bf16[32,69]{1,0:T(8,128)(2,1)}, u32[]{:S(2)}, u32[]{:S(2)}) collective-permute-start(bf16[32,69]{1,0:T(8,128)(2,1)S(1)} %get-tuple-element.35), channel_id=1, source_target_pairs={{0,5},{1,6},{2,7},{3,4},{4,9},{5,10},{6,11},{7,8},{8,13},{9,14},{1... | collective-permute-start | bytes 13256 | tf_op jit(solution)/shard_map/ppermute | solution.py:413
  53.9 5.7 %collective-permute-done.4.lon_piece = bf16[32,69]{1,0:T(8,128)(2,1)S(1)} collective-permute-done((bf16[32,69]{1,0:T(8,128)(2,1)S(1)}, bf16[32,69]{1,0:T(8,128)(2,1)S(1)}, u32[]{:S(2)}, u32[]{:S(2)}) %collective-permute-start.4) | collective-permute-done | bytes 4448 | tf_op jit(solution)/shard_map/ppermute | solution.py:407
  60.2 1.0 collective-permute-done.5.far_piece
  61.2 2.5 %observe.1 = (f32[128,8]{1,0:T(8,128)}, f32[8,16,69]{2,1,0:T(8,128)}, bf16[32,69]{1,0:T(8,128)(2,1)}, bf16[32,69]{1,0:T(8,128)(2,1)}, bf16[32,69]{1,0:T(8,128)(2,1)}, /*index=5*/bf16[32,69]{1,0:T(8,128)(2,1)}) custom-call(f32[8,16,69]{2,1,0:T(8,128)} %direction_ref.5, bf16[32,69]{1,0:T(8,128)(2,1)} %copy-done.21, bf16[32,69]{1,0:T(8,128)(2,1)} %copy-done.36, ...), custom_call_target="tpu_custom_call" | custom-call | tf_op jit(solution)/shard_map/observe/pallas_call | solution.py:495
  63.7 0.9 collective-permute-start.7
  64.6 2.5 %collective-permute-start.8 = (bf16[32,69]{1,0:T(8,128)(2,1)}, bf16[32,69]{1,0:T(8,128)(2,1)S(1)}, u32[]{:S(2)}, u32[]{:S(2)}) collective-permute-start(bf16[32,69]{1,0:T(8,128)(2,1)} %get-tuple-element.41), channel_id=1, source_target_pairs={{0,127},{1,124},{2,125},{3,126},{4,3},{5,0},{6,1},{7,2},{8,7},{9,4... | collective-permute-start | bytes 13256 | tf_op jit(solution)/shard_map/ppermute | solution.py:413
  67.0 1.7 %collective-permute-done.8.far_piece = bf16[32,69]{1,0:T(8,128)(2,1)S(1)} collective-permute-done((bf16[32,69]{1,0:T(8,128)(2,1)}, bf16[32,69]{1,0:T(8,128)(2,1)S(1)}, u32[]{:S(2)}, u32[]{:S(2)}) %collective-permute-start.8) | collective-permute-done | bytes 4448 | tf_op jit(solution)/shard_map/ppermute | solution.py:413
  68.8 2.8 %copy-done.1 = bf16[1024,3072]{1,0:T(8,128)(2,1)S(1)} copy-done((bf16[1024,3072]{1,0:T(8,128)(2,1)S(1)}, bf16[1024,3072]{1,0:T(8,128)(2,1)}, u32[]{:S(2)}) %copy-start.1) | copy-done | bytes 6291480
  71.6 1.0 copy-done.5
  72.6 0.9 copy-done.7
  73.6 0.9 copy-done.9
  74.5 0.9 copy-done.11
  75.5 0.9 copy-done.13
  76.4 0.9 copy-done.18
  77.3 0.7 copy-done.20
  78.0 0.7 copy-done.24
  78.7 0.7 copy-done.26
  80.1 11.1 %adjoint.1 = (bf16[32,69]{1,0:T(8,128)(2,1)S(1)}, bf16[32,69]{1,0:T(8,128)(2,1)}, bf16[32,69]{1,0:T(8,128)(2,1)}, bf16[32,69]{1,0:T(8,128)(2,1)}) custom-call(f32[16]{0:T(128)S(1)} %copy-done.28, bf16[32,69]{1,0:T(8,128)(2,1)S(1)} %copy-done.20, bf16[32,69]{1,0:T(8,128)(2,1)S(1)} %collective-permute-done.6.lat_piece, ...), custom_call_target="tpu_custom_call" | custom-call | flops 1500000000 | bytes 10000000 | tf_op jit(solution)/shard_map/adjoint/pallas_call | solution.py:505
  92.3 1.2 collective-permute-start.10
  93.4 19.1 %all_to_all.22 = f32[128,1,8]{2,1,0:T(1,128)} all-to-all(f32[128,1,8]{2,1,0:T(1,128)S(1)} %bitcast.25), channel_id=1, replica_groups=mesh['lon'=32,'lat'=4] {'lon','lat'}, dimensions={0} | all-to-all | bytes 8192 | tf_op jit(solution)/shard_map/all_to_all | solution.py:503
  112.5 1.7 %unpack.1 = f32[1,512]{1,0:T(1,128)} custom-call(s32[1,512]{1,0:T(1,128)} %bitcast.27, f32[1,512]{1,0:T(1,128)} %get-tuple-element.54.slots_ref, f32[128,8]{1,0:T(8,128)} %bitcast.23), custom_call_target="tpu_custom_call" | custom-call | tf_op jit(solution)/shard_map/unpack/pallas_call | solution.py:542
  114.8 1.5 %finish.1 = f32[8,16,69]{2,1,0:T(8,128)} custom-call(f32[8,16,69]{2,1,0:T(8,128)} %get-tuple-element.37.adjoint_ref, bf16[32,69]{1,0:T(8,128)(2,1)} %copy-done.22, bf16[32,69]{1,0:T(8,128)(2,1)} %copy-done.38, bf16[32,69]{1,0:T(8,128)(2,1)} %copy-done.39, bf16[32,69]{1,0:T(8,128)(2,1)} %copy-done.40), custom_call_target="tpu_custom_call" | custom-call | tf_op jit(solution)/shard_map/finish/pallas_call | solution.py:535
  (68 shorter events, 5.5 us)
Async XLA Ops:
  0.6 68.1 %copy-start.16 = (bf16[69,1024]{1,0:T(8,128)(2,1)S(1)}, bf16[69,1024]{1,0:T(8,128)(2,1)}, u32[]{:S(2)}) copy-start(bf16[69,1024]{1,0:T(8,128)(2,1)} %embed_ref.3) | copy-start | bytes 423940
  2.2 17.7 %collective-permute-start = (bf16[64,69]{1,0:T(8,128)(2,1)}, bf16[64,69]{1,0:T(8,128)(2,1)S(1)}, u32[]{:S(2)}, u32[]{:S(2)}) collective-permute-start(bf16[64,69]{1,0:T(8,128)(2,1)} %get-tuple-element.29), channel_id=1, source_target_pairs={{0,3},{1,0},{2,1},{3,2},{4,7},{5,4},{6,5},{7,6},{8,11},{9,8},{10,9... | collective-permute-start | bytes 26504 | tf_op jit(solution)/shard_map/ppermute | solution.py:406
  3.6 16.9 %collective-permute-start.1 = (bf16[64,69]{1,0:T(8,128)(2,1)}, bf16[64,69]{1,0:T(8,128)(2,1)S(1)}, u32[]{:S(2)}, u32[]{:S(2)}) collective-permute-start(bf16[64,69]{1,0:T(8,128)(2,1)} %get-tuple-element.30), channel_id=1, source_target_pairs={{0,124},{4,0},{8,4},{12,8},{16,12},{20,16},{24,20},{28,24},{32,28}... | collective-permute-start | bytes 26504 | tf_op jit(solution)/shard_map/ppermute | solution.py:407
  12.3 8.7 %collective-permute-start.2 = (bf16[64,69]{1,0:T(8,128)(2,1)}, bf16[64,69]{1,0:T(8,128)(2,1)S(1)}, u32[]{:S(2)}, u32[]{:S(2)}) collective-permute-start(bf16[64,69]{1,0:T(8,128)(2,1)} %get-tuple-element.31), channel_id=1, source_target_pairs={{0,127},{1,124},{2,125},{3,126},{4,3},{5,0},{6,1},{7,2},{8,7},{9,4... | collective-permute-start | bytes 26504 | tf_op jit(solution)/shard_map/ppermute | solution.py:413
  15.2 46.0 %all-to-all-start = ((f32[128,1,64]{2,1,0:T(1,128)}), f32[128,1,64]{2,1,0:T(1,128)}, u32[]{:S(2)}, u32[]{:S(2)}) async-start(f32[128,1,64]{2,1,0:T(1,128)} %bitcast.24), calls=%async_computation | async-start | bytes 131072 | tf_op jit(solution)/shard_map/all_to_all | solution.py:460
  19.9 0.6 copy-start.29
  20.5 0.6 copy-start.31
  21.7 2.8 %copy-start = (bf16[1024,3072]{1,0:T(8,128)(2,1)S(1)}, bf16[1024,3072]{1,0:T(8,128)(2,1)}, u32[]{:S(2)}) copy-start(bf16[1024,3072]{1,0:T(8,128)(2,1)} %qkv_hbm.3) | copy-start | bytes 18874372
  24.5 1.6 %copy-start.2 = (bf16[1024,1024]{1,0:T(8,128)(2,1)S(1)}, bf16[1024,1024]{1,0:T(8,128)(2,1)}, u32[]{:S(2)}) copy-start(bf16[1024,1024]{1,0:T(8,128)(2,1)} %outw_hbm.3) | copy-start | bytes 6291460
  26.1 0.8 copy-start.14
  26.9 0.9 copy-start.15
  27.8 0.9 copy-start.17
  28.7 0.8 copy-start.19
  29.6 0.7 copy-start.23
  30.2 0.7 copy-start.25
  30.9 0.7 copy-start.27
  31.6 0.7 copy-start.30
  32.3 0.7 copy-start.32
  33.0 0.7 copy-start.34
  33.7 35.0 %copy-start.3 = (bf16[1024,1024]{1,0:T(8,128)(2,1)S(1)}, bf16[1024,1024]{1,0:T(8,128)(2,1)}, u32[]{:S(2)}) copy-start(bf16[1024,1024]{1,0:T(8,128)(2,1)} %outw_hbm.3) | copy-start | bytes 6291460
  45.3 0.8 copy-start.4
  46.1 0.7 copy-start.6
  46.8 0.7 copy-start.8
  47.5 0.7 copy-start.10
  48.2 0.7 copy-start.12
  49.5 4.4 %collective-permute-start.3 = (bf16[32,69]{1,0:T(8,128)(2,1)S(1)}, bf16[32,69]{1,0:T(8,128)(2,1)S(1)}, u32[]{:S(2)}, u32[]{:S(2)}) collective-permute-start(bf16[32,69]{1,0:T(8,128)(2,1)S(1)} %get-tuple-element.33), channel_id=1, source_target_pairs={{0,1},{1,2},{2,3},{3,0},{4,5},{5,6},{6,7},{7,4},{8,9},{9,10},{10,1... | collective-permute-start | bytes 13256 | tf_op jit(solution)/shard_map/ppermute | solution.py:406
  50.8 8.8 %collective-permute-start.4 = (bf16[32,69]{1,0:T(8,128)(2,1)S(1)}, bf16[32,69]{1,0:T(8,128)(2,1)S(1)}, u32[]{:S(2)}, u32[]{:S(2)}) collective-permute-start(bf16[32,69]{1,0:T(8,128)(2,1)S(1)} %get-tuple-element.34), channel_id=1, source_target_pairs={{0,4},{4,8},{8,12},{12,16},{16,20},{20,24},{24,28},{28,32},{32,36}... | collective-permute-start | bytes 13256 | tf_op jit(solution)/shard_map/ppermute | solution.py:407
  52.3 8.9 %collective-permute-start.5 = (bf16[32,69]{1,0:T(8,128)(2,1)S(1)}, bf16[32,69]{1,0:T(8,128)(2,1)}, u32[]{:S(2)}, u32[]{:S(2)}) collective-permute-start(bf16[32,69]{1,0:T(8,128)(2,1)S(1)} %get-tuple-element.35), channel_id=1, source_target_pairs={{0,5},{1,6},{2,7},{3,4},{4,9},{5,10},{6,11},{7,8},{8,13},{9,14},{1... | collective-permute-start | bytes 13256 | tf_op jit(solution)/shard_map/ppermute | solution.py:413
  53.9 5.7 %copy-start.36 = (bf16[32,69]{1,0:T(8,128)(2,1)}, bf16[32,69]{1,0:T(8,128)(2,1)S(1)}, u32[]{:S(2)}) copy-start(bf16[32,69]{1,0:T(8,128)(2,1)S(1)} %collective-permute-done.3.lat_piece) | copy-start | bytes 13252
  63.7 3.4 %collective-permute-start.6 = (bf16[32,69]{1,0:T(8,128)(2,1)}, bf16[32,69]{1,0:T(8,128)(2,1)S(1)}, u32[]{:S(2)}, u32[]{:S(2)}) collective-permute-start(bf16[32,69]{1,0:T(8,128)(2,1)} %get-tuple-element.39), channel_id=1, source_target_pairs={{0,3},{1,0},{2,1},{3,2},{4,7},{5,4},{6,5},{7,6},{8,11},{9,8},{10,9... | collective-permute-start | bytes 13256 | tf_op jit(solution)/shard_map/ppermute | solution.py:406
  63.7 3.4 %collective-permute-start.7 = (bf16[32,69]{1,0:T(8,128)(2,1)}, bf16[32,69]{1,0:T(8,128)(2,1)S(1)}, u32[]{:S(2)}, u32[]{:S(2)}) collective-permute-start(bf16[32,69]{1,0:T(8,128)(2,1)} %get-tuple-element.40), channel_id=1, source_target_pairs={{0,124},{4,0},{8,4},{12,8},{16,12},{20,16},{24,20},{28,24},{32,28}... | collective-permute-start | bytes 13256 | tf_op jit(solution)/shard_map/ppermute | solution.py:407
  64.6 4.2 %collective-permute-start.8 = (bf16[32,69]{1,0:T(8,128)(2,1)}, bf16[32,69]{1,0:T(8,128)(2,1)S(1)}, u32[]{:S(2)}, u32[]{:S(2)}) collective-permute-start(bf16[32,69]{1,0:T(8,128)(2,1)} %get-tuple-element.41), channel_id=1, source_target_pairs={{0,127},{1,124},{2,125},{3,126},{4,3},{5,0},{6,1},{7,2},{8,7},{9,4... | collective-permute-start | bytes 13256 | tf_op jit(solution)/shard_map/ppermute | solution.py:413
  68.8 2.8 %copy-start.1 = (bf16[1024,3072]{1,0:T(8,128)(2,1)S(1)}, bf16[1024,3072]{1,0:T(8,128)(2,1)}, u32[]{:S(2)}) copy-start(bf16[1024,3072]{1,0:T(8,128)(2,1)} %qkv_hbm.3) | copy-start | bytes 18874372
  71.6 1.0 copy-start.5
  72.6 0.9 copy-start.7
  73.6 0.9 copy-start.9
  74.5 0.9 copy-start.11
  75.5 0.9 copy-start.13
  76.4 0.9 copy-start.18
  77.3 0.7 copy-start.20
  78.0 0.7 copy-start.24
  78.7 0.7 copy-start.26
  79.4 0.7 copy-start.28
  80.1 13.4 %copy-start.35 = (f32[128,8]{1,0:T(8,128)S(1)}, f32[128,8]{1,0:T(8,128)}, u32[]{:S(2)}) copy-start(f32[128,8]{1,0:T(8,128)} %get-tuple-element.55) | copy-start | bytes 12292
  91.7 22.5 %collective-permute-start.9 = (bf16[32,69]{1,0:T(8,128)(2,1)}, bf16[32,69]{1,0:T(8,128)(2,1)S(1)}, u32[]{:S(2)}, u32[]{:S(2)}) collective-permute-start(bf16[32,69]{1,0:T(8,128)(2,1)} %get-tuple-element.51), channel_id=1, source_target_pairs={{0,1},{1,2},{2,3},{3,0},{4,5},{5,6},{6,7},{7,4},{8,9},{9,10},{10,1... | collective-permute-start | bytes 13256 | tf_op jit(solution)/shard_map/ppermute | solution.py:406
  92.3 21.9 %collective-permute-start.10 = (bf16[32,69]{1,0:T(8,128)(2,1)}, bf16[32,69]{1,0:T(8,128)(2,1)S(1)}, u32[]{:S(2)}, u32[]{:S(2)}) collective-permute-start(bf16[32,69]{1,0:T(8,128)(2,1)} %get-tuple-element.52), channel_id=1, source_target_pairs={{0,4},{4,8},{8,12},{12,16},{16,20},{20,24},{24,28},{28,32},{32,36}... | collective-permute-start | bytes 13256 | tf_op jit(solution)/shard_map/ppermute | solution.py:407
  93.4 20.8 %collective-permute-start.11 = (bf16[32,69]{1,0:T(8,128)(2,1)}, bf16[32,69]{1,0:T(8,128)(2,1)S(1)}, u32[]{:S(2)}, u32[]{:S(2)}) collective-permute-start(bf16[32,69]{1,0:T(8,128)(2,1)} %get-tuple-element.53), channel_id=1, source_target_pairs={{0,5},{1,6},{2,7},{3,4},{4,9},{5,10},{6,11},{7,8},{8,13},{9,14},{1... | collective-permute-start | bytes 13256 | tf_op jit(solution)/shard_map/ppermute | solution.py:413
  114.2 0.6 copy-start.40
  (6 other events, 3.6 us)
where the time goes:
time: 117 us; the launch traced here: 116 us
  Pallas kernels  31.7 us (27%)
  local copies, waits for them, and re-layouts  31.1 us (27%)
  starting transfers between devices  25.2 us (22%)
  blocking collectives  19.1 us (16%)
  waiting for transfers between devices  8.46 us (7%)
    unnamed x82, local copies, waits for them, and re-layouts  31.1 us
    all_to_all x1, blocking collectives, per_device(): lax.all_to_all(at_obs, ('lon', 'lat'), split_axis=0, concat_axis=0, tiled...  19.1 us
    ppermute x4, starting transfers between devices, exchanged(): lax.ppermute(lon_piece, 'lon', [(i, (i + steps) % lon_count) for i in ran...  12.3 us
    pallas_call x1, Pallas kernels, per_device(): pl.pallas_call(forward_kernel, out_shape=[quarter] * 4 + [wide, wide, wid...  11.5 us
    pallas_call x1, Pallas kernels, per_device(): pl.pallas_call(adjoint_kernel, out_shape=[quarter] * 4, in_specs=[SMEM] +...  11.1 us
    ppermute x4, waiting for transfers between devices, exchanged(): lax.ppermute(lon_piece, 'lon', [(i, (i + steps) % lon_count) for i in ran...  5.74 us
    ppermute x4, starting transfers between devices, exchanged(): far_piece = lax.ppermute(far_piece, ('lon', 'lat'), pairs)  4.97 us
    all_to_all x1, starting transfers between devices, per_device(): lax.all_to_all(outgoing, ('lon', 'lat'), split_axis=0, concat_axis=0, til...  4.63 us
  transfers between devices with their start and end apart: 13, of which 3 were waited for; matrix products, arithmetic and copies ran while one was open for 0% of the time, Pallas kernels for 13%

commit v1 on v0

--- a/solution.py
+++ b/solution.py
@@ -437,7 +437,6 @@
     gain = attn_gain.reshape(1, width)
     decode_gain = decode_gain.reshape(1, width)
     decode_rows = decode_weight.T
-    params = pltpu.CompilerParams(vmem_limit_bytes=40 * 1024 * 1024)
     quarter = shape((QUARTER, var_count), bf16)
 
     strips = pl.pallas_call(
@@ -474,7 +473,6 @@
             pltpu.VMEM((2 * CELLS, width), bf16),
             pltpu.SemaphoreType.DMA((3 * (width // 512) + 1,)),
         ],
-        compiler_params=params,
         cost_estimate=pl.CostEstimate(flops=2_500_000_000, bytes_accessed=10_000_000, transcendentals=300_000),
         name="forward",
     )(
@@ -513,7 +511,6 @@
             pltpu.VMEM((CELLS, 3 * width), bf16),
             pltpu.SemaphoreType.DMA((2,)),
         ],
-        compiler_params=params,
         cost_estimate=pl.CostEstimate(flops=1_500_000_000, bytes_accessed=10_000_000, transcendentals=300_000),
         name="adjoint",
     )(
@@ -530,6 +527,7 @@
         qkv_weight,
         out_weight,
     )
+    lat_piece, lon_piece, far_piece, returned = lax.optimization_barrier((lat_piece, lon_piece, far_piece, returned))
     lat_piece, lon_piece, far_piece = exchanged(lat_piece, lon_piece, far_piece, 1)
 
     hvp = pl.pallas_call(

time: 117 us -> 83.1 us (0.71)
  local copies, waits for them, and re-layouts: 31.1 us -> 2.41 us
  blocking collectives: 19.1 us -> 0 us
  starting transfers between devices: 25.2 us -> 31.7 us
  waiting for transfers between devices: 8.46 us -> 13.2 us
  Pallas kernels: 31.7 us -> 34.5 us
    unnamed x82 -> x28, local copies, waits for them, and re-layouts: 31.1 us -> 2.41 us
    all_to_all x1 -> x0, blocking collectives: 19.1 us -> none  [per_device(): lax.all_to_all(at_obs, ('lon', 'lat'), split_axis=0, concat_axis=0, tiled...]
    ppermute x4, waiting for transfers between devices: 5.74 us -> 10.2 us  [exchanged(): lax.ppermute(lon_piece, 'lon', [(i, (i + steps) % lon_count) for i in ran...]
    all_to_all x0 -> x1, starting transfers between devices: none -> 4.42 us  [per_device(): lax.all_to_all(at_obs, ('lon', 'lat'), split_axis=0, concat_axis=0, tiled...]
    pallas_call x1, Pallas kernels: 11.1 us -> 13.1 us  [per_device(): pl.pallas_call(adjoint_kernel, out_shape=[quarter] * 4, in_specs=[SMEM] +...]
    ppermute x4, starting transfers between devices: 4.97 us -> 6.6 us  [exchanged(): far_piece = lax.ppermute(far_piece, ('lon', 'lat'), pairs)]
    ppermute x4, starting transfers between devices: 3.32 us -> 4.83 us  [exchanged(): lax.ppermute(lat_piece, 'lat', [(i, (i + steps) % lat_count) for i in ran...]
  transfers between devices with their start and end apart: 13 -> 14, of which waited for: 3 -> 4; matrix products, arithmetic and copies ran while one was open for 0% -> 0% of each run, Pallas kernels for 13% -> 35%
where the time goes in v1:
time: 83.1 us; the launch traced here: 82.6 us
  Pallas kernels  34.5 us (42%)
  starting transfers between devices  31.7 us (38%)
  waiting for transfers between devices  13.2 us (16%)
  local copies, waits for them, and re-layouts  2.41 us (3%)
    pallas_call x1, Pallas kernels, per_device(): pl.pallas_call(adjoint_kernel, out_shape=[quarter] * 4, in_specs=[SMEM] +...  13.1 us
    pallas_call x1, Pallas kernels, per_device(): pl.pallas_call(forward_kernel, out_shape=[quarter] * 4 + [wide, wide, wid...  12.4 us
    ppermute x4, starting transfers between devices, exchanged(): lax.ppermute(lon_piece, 'lon', [(i, (i + steps) % lon_count) for i in ran...  12.3 us
    ppermute x4, waiting for transfers between devices, exchanged(): lax.ppermute(lon_piece, 'lon', [(i, (i + steps) % lon_count) for i in ran...  10.2 us
    ppermute x4, starting transfers between devices, exchanged(): far_piece = lax.ppermute(far_piece, ('lon', 'lat'), pairs)  6.6 us
    ppermute x4, starting transfers between devices, exchanged(): lax.ppermute(lat_piece, 'lat', [(i, (i + steps) % lat_count) for i in ran...  4.83 us
    all_to_all x1, starting transfers between devices, per_device(): lax.all_to_all(at_obs, ('lon', 'lat'), split_axis=0, concat_axis=0, tiled...  4.42 us
    all_to_all x1, starting transfers between devices, per_device(): lax.all_to_all(outgoing, ('lon', 'lat'), split_axis=0, concat_axis=0, til...  3.56 us
  transfers between devices with their start and end apart: 14, of which 4 were waited for; matrix products, arithmetic and copies ran while one was open for 0% of the time, Pallas kernels for 35%

profile of v1, /device:TPU:1, one launch (start us, length us, event | category | flops | bytes accessed | tf_op | source)
XLA Modules:
  0.0 82.6 jit_solution(2213847733515314706)
XLA Ops:
  0.6 1.5 %strips.1 = (bf16[64,69]{1,0:T(8,128)(2,1)}, bf16[64,69]{1,0:T(8,128)(2,1)}, bf16[64,69]{1,0:T(8,128)(2,1)}) custom-call(f32[8,16,69]{2,1,0:T(8,128)} %background_ref.3, f32[8,16,69]{2,1,0:T(8,128)} %direction_ref.5), custom_call_target="tpu_custom_call" | custom-call | tf_op jit(solution)/shard_map/strips/pallas_call | solution.py:442
  2.1 1.4 %collective-permute-start = (bf16[64,69]{1,0:T(8,128)(2,1)}, bf16[64,69]{1,0:T(8,128)(2,1)S(1)}, u32[]{:S(2)}, u32[]{:S(2)}) collective-permute-start(bf16[64,69]{1,0:T(8,128)(2,1)} %get-tuple-element.33), channel_id=1, source_target_pairs={{0,3},{1,0},{2,1},{3,2},{4,7},{5,4},{6,5},{7,6},{8,11},{9,8},{10,9... | collective-permute-start | bytes 26504 | tf_op jit(solution)/shard_map/ppermute | solution.py:406
  3.5 8.8 %collective-permute-start.1 = (bf16[64,69]{1,0:T(8,128)(2,1)}, bf16[64,69]{1,0:T(8,128)(2,1)S(1)}, u32[]{:S(2)}, u32[]{:S(2)}) collective-permute-start(bf16[64,69]{1,0:T(8,128)(2,1)} %get-tuple-element.34), channel_id=1, source_target_pairs={{0,124},{4,0},{8,4},{12,8},{16,12},{20,16},{24,20},{28,24},{32,28}... | collective-permute-start | bytes 26504 | tf_op jit(solution)/shard_map/ppermute | solution.py:407
  12.3 0.9 %collective-permute-start.2 = (bf16[64,69]{1,0:T(8,128)(2,1)}, bf16[64,69]{1,0:T(8,128)(2,1)S(1)}, u32[]{:S(2)}, u32[]{:S(2)}) collective-permute-start(bf16[64,69]{1,0:T(8,128)(2,1)} %get-tuple-element.35), channel_id=1, source_target_pairs={{0,127},{1,124},{2,125},{3,126},{4,3},{5,0},{6,1},{7,2},{8,7},{9,4... | collective-permute-start | bytes 26504 | tf_op jit(solution)/shard_map/ppermute | solution.py:413
  13.2 1.9 %pack.1 = (f32[128,64]{1,0:T(8,128)}, f32[1,512]{1,0:T(1,128)}) custom-call(s32[1,512]{1,0:T(1,128)} %bitcast.23, s32[1,512]{1,0:T(1,128)} %bitcast.30, f32[4,512]{1,0:T(4,128)} %bitcast.25, f32[1,512]{1,0:T(1,128)} %bitcast.31), custom_call_target="tpu_custom_call" | custom-call | tf_op jit(solution)/shard_map/pack/pallas_call | solution.py:452
  15.1 3.6 %all-to-all-start = ((f32[128,1,64]{2,1,0:T(1,128)}), f32[128,1,64]{2,1,0:T(1,128)S(1)}, u32[]{:S(2)}, u32[]{:S(2)}) async-start(f32[128,1,64]{2,1,0:T(1,128)} %bitcast.21), calls=%async_computation | async-start | bytes 131072 | tf_op jit(solution)/shard_map/all_to_all | solution.py:459
  18.7 0.0 collective-permute-done.lat_piece
  18.7 0.0 copy-start.11
  18.7 0.0 collective-permute-done.1.lon_piece
  18.8 0.0 collective-permute-done.2.far_piece
  18.8 0.6 copy-done.11
  19.3 0.0 copy-done.12
  19.3 0.0 copy-done.13
  19.4 12.4 %forward.1 = (bf16[32,69]{1,0:T(8,128)(2,1)}, bf16[32,69]{1,0:T(8,128)(2,1)}, bf16[32,69]{1,0:T(8,128)(2,1)}, bf16[32,69]{1,0:T(8,128)(2,1)}, bf16[128,1024]{1,0...) custom-call(s32[1]{0:T(128)} %bitcast.lat_ref, ...), custom_call_target="tpu_custom_call" | custom-call | flops 2500000000 | bytes 10000000 | tf_op jit(solution)/shard_map/forward/pallas_call | solution.py:463
  31.8 1.7 %collective-permute-start.3 = (bf16[32,69]{1,0:T(8,128)(2,1)}, bf16[32,69]{1,0:T(8,128)(2,1)S(1)}, u32[]{:S(2)}, u32[]{:S(2)}) collective-permute-start(bf16[32,69]{1,0:T(8,128)(2,1)} %get-tuple-element.37), channel_id=1, source_target_pairs={{0,1},{1,2},{2,3},{3,0},{4,5},{5,6},{6,7},{7,4},{8,9},{9,10},{10,1... | collective-permute-start | bytes 13256 | tf_op jit(solution)/shard_map/ppermute | solution.py:406
  33.5 1.3 %collective-permute-start.4 = (bf16[32,69]{1,0:T(8,128)(2,1)}, bf16[32,69]{1,0:T(8,128)(2,1)S(1)}, u32[]{:S(2)}, u32[]{:S(2)}) collective-permute-start(bf16[32,69]{1,0:T(8,128)(2,1)} %get-tuple-element.38), channel_id=1, source_target_pairs={{0,4},{4,8},{8,12},{12,16},{16,20},{20,24},{24,28},{28,32},{32,36}... | collective-permute-start | bytes 13256 | tf_op jit(solution)/shard_map/ppermute | solution.py:407
  34.8 1.6 %collective-permute-start.5 = (bf16[32,69]{1,0:T(8,128)(2,1)}, bf16[32,69]{1,0:T(8,128)(2,1)S(1)}, u32[]{:S(2)}, u32[]{:S(2)}) collective-permute-start(bf16[32,69]{1,0:T(8,128)(2,1)} %get-tuple-element.39), channel_id=1, source_target_pairs={{0,5},{1,6},{2,7},{3,4},{4,9},{5,10},{6,11},{7,8},{8,13},{9,14},{1... | collective-permute-start | bytes 13256 | tf_op jit(solution)/shard_map/ppermute | solution.py:413
  36.4 0.0 collective-permute-done.3.lat_piece
  36.4 5.9 %collective-permute-done.4.lon_piece = bf16[32,69]{1,0:T(8,128)(2,1)S(1)} collective-permute-done((bf16[32,69]{1,0:T(8,128)(2,1)}, bf16[32,69]{1,0:T(8,128)(2,1)S(1)}, u32[]{:S(2)}, u32[]{:S(2)}) %collective-permute-start.4) | collective-permute-done | bytes 4448 | tf_op jit(solution)/shard_map/ppermute | solution.py:407
  42.4 1.5 %collective-permute-done.5.far_piece = bf16[32,69]{1,0:T(8,128)(2,1)S(1)} collective-permute-done((bf16[32,69]{1,0:T(8,128)(2,1)}, bf16[32,69]{1,0:T(8,128)(2,1)S(1)}, u32[]{:S(2)}, u32[]{:S(2)}) %collective-permute-start.5) | collective-permute-done | bytes 4448 | tf_op jit(solution)/shard_map/ppermute | solution.py:413
  43.8 0.0 all-to-all-done
  43.8 0.0 copy-done.6
  43.8 0.6 copy-done.8
  44.4 0.0 copy-done
  44.5 2.5 %observe.1 = (f32[128,8]{1,0:T(8,128)}, f32[8,16,69]{2,1,0:T(8,128)}, bf16[32,69]{1,0:T(8,128)(2,1)}, bf16[32,69]{1,0:T(8,128)(2,1)}, bf16[32,69]{1,0:T(8,128)(2,1)}, /*index=5*/bf16[32,69]{1,0:T(8,128)(2,1)}) custom-call(f32[8,16,69]{2,1,0:T(8,128)} %direction_ref.5, bf16[32,69]{1,0:T(8,128)(2,1)} %get-tuple-element.36.own_piece, bf16[32,69]{1,0:T(8,128)(2,1)} %copy-done.5, ...), custom_call_target="tpu_custom_call" | custom-call | tf_op jit(solution)/shard_map/observe/pallas_call | solution.py:493
  47.0 0.0 collective-permute-start.6
  47.0 0.9 %collective-permute-start.7 = (bf16[32,69]{1,0:T(8,128)(2,1)}, bf16[32,69]{1,0:T(8,128)(2,1)S(1)}, u32[]{:S(2)}, u32[]{:S(2)}) collective-permute-start(bf16[32,69]{1,0:T(8,128)(2,1)} %get-tuple-element.44), channel_id=1, source_target_pairs={{0,124},{4,0},{8,4},{12,8},{16,12},{20,16},{24,20},{28,24},{32,28}... | collective-permute-start | bytes 13256 | tf_op jit(solution)/shard_map/ppermute | solution.py:407
  47.8 2.5 %collective-permute-start.8 = (bf16[32,69]{1,0:T(8,128)(2,1)}, bf16[32,69]{1,0:T(8,128)(2,1)S(1)}, u32[]{:S(2)}, u32[]{:S(2)}) collective-permute-start(bf16[32,69]{1,0:T(8,128)(2,1)} %get-tuple-element.45), channel_id=1, source_target_pairs={{0,127},{1,124},{2,125},{3,126},{4,3},{5,0},{6,1},{7,2},{8,7},{9,4... | collective-permute-start | bytes 13256 | tf_op jit(solution)/shard_map/ppermute | solution.py:413
  50.3 4.4 %all-to-all-start.1 = ((f32[128,1,8]{2,1,0:T(1,128)}), f32[128,1,8]{2,1,0:T(1,128)S(1)}, u32[]{:S(2)}, u32[]{:S(2)}) async-start(f32[128,1,8]{2,1,0:T(1,128)} %bitcast.22), calls=%async_computation.1 | async-start | bytes 131072 | tf_op jit(solution)/shard_map/all_to_all | solution.py:501
  54.7 0.0 collective-permute-done.6.lat_piece
  54.8 0.0 copy-start.2
  54.8 0.0 collective-permute-done.7.lon_piece
  54.8 0.0 collective-permute-done.8.far_piece
  54.8 0.5 copy-done.2
  55.4 0.0 copy-done.3
  55.4 0.0 copy-done.4
  55.4 13.1 %adjoint.1 = (bf16[32,69]{1,0:T(8,128)(2,1)}, bf16[32,69]{1,0:T(8,128)(2,1)}, bf16[32,69]{1,0:T(8,128)(2,1)}, bf16[32,69]{1,0:T(8,128)(2,1)}) custom-call(f32[16]{0:T(128)} %logit_ref.3, bf16[32,69]{1,0:T(8,128)(2,1)} %get-tuple-element.42.own_piece, bf16[32,69]{1,0:T(8,128)(2,1)} %copy-done.2, bf16[32,69]{1,0:T(8,128)(2,1)} %copy-done.3, ...), custom_call_target="tpu_custom_call" | custom-call | flops 1500000000 | bytes 10000000 | tf_op jit(solution)/shard_map/adjoint/pallas_call | solution.py:503
  68.5 0.0 all-to-all-done.1
  68.5 0.0 copy-start.1
  68.5 1.7 %collective-permute-start.9 = (bf16[32,69]{1,0:T(8,128)(2,1)}, bf16[32,69]{1,0:T(8,128)(2,1)S(1)}, u32[]{:S(2)}, u32[]{:S(2)}) collective-permute-start(bf16[32,69]{1,0:T(8,128)(2,1)} %get-tuple-element.59), channel_id=1, source_target_pairs={{0,1},{1,2},{2,3},{3,0},{4,5},{5,6},{6,7},{7,4},{8,9},{9,10},{10,1... | collective-permute-start | bytes 13256 | tf_op jit(solution)/shard_map/ppermute | solution.py:406
  70.2 1.3 %collective-permute-start.10 = (bf16[32,69]{1,0:T(8,128)(2,1)}, bf16[32,69]{1,0:T(8,128)(2,1)S(1)}, u32[]{:S(2)}, u32[]{:S(2)}) collective-permute-start(bf16[32,69]{1,0:T(8,128)(2,1)} %get-tuple-element.60), channel_id=1, source_target_pairs={{0,4},{4,8},{8,12},{12,16},{16,20},{20,24},{24,28},{28,32},{32,36}... | collective-permute-start | bytes 13256 | tf_op jit(solution)/shard_map/ppermute | solution.py:407
  71.5 1.6 %collective-permute-start.11 = (bf16[32,69]{1,0:T(8,128)(2,1)}, bf16[32,69]{1,0:T(8,128)(2,1)S(1)}, u32[]{:S(2)}, u32[]{:S(2)}) collective-permute-start(bf16[32,69]{1,0:T(8,128)(2,1)} %get-tuple-element.61), channel_id=1, source_target_pairs={{0,5},{1,6},{2,7},{3,4},{4,9},{5,10},{6,11},{7,8},{8,13},{9,14},{1... | collective-permute-start | bytes 13256 | tf_op jit(solution)/shard_map/ppermute | solution.py:413
  73.1 1.7 %unpack.1 = f32[1,512]{1,0:T(1,128)} custom-call(s32[1,512]{1,0:T(1,128)} %bitcast.24, f32[1,512]{1,0:T(1,128)} %get-tuple-element.62.slots_ref, f32[128,8]{1,0:T(8,128)} %bitcast.18), custom_call_target="tpu_custom_call" | custom-call | tf_op jit(solution)/shard_map/unpack/pallas_call | solution.py:540
  74.8 0.0 collective-permute-done.9.lat_piece
  74.8 4.3 %collective-permute-done.10.lon_piece = bf16[32,69]{1,0:T(8,128)(2,1)S(1)} collective-permute-done((bf16[32,69]{1,0:T(8,128)(2,1)}, bf16[32,69]{1,0:T(8,128)(2,1)S(1)}, u32[]{:S(2)}, u32[]{:S(2)}) %collective-permute-start.10) | collective-permute-done | bytes 4448 | tf_op jit(solution)/shard_map/ppermute | solution.py:407
  79.0 1.5 %collective-permute-done.11.far_piece = bf16[32,69]{1,0:T(8,128)(2,1)S(1)} collective-permute-done((bf16[32,69]{1,0:T(8,128)(2,1)}, bf16[32,69]{1,0:T(8,128)(2,1)S(1)}, u32[]{:S(2)}, u32[]{:S(2)}) %collective-permute-start.11) | collective-permute-done | bytes 4448 | tf_op jit(solution)/shard_map/ppermute | solution.py:413
  80.5 0.6 copy-done.10
  81.1 1.5 %finish.1 = f32[8,16,69]{2,1,0:T(8,128)} custom-call(f32[8,16,69]{2,1,0:T(8,128)} %get-tuple-element.41.adjoint_ref, bf16[32,69]{1,0:T(8,128)(2,1)} %get-tuple-element.54.own_piece, bf16[32,69]{1,0:T(8,128)(2,1)} %copy-done.7, bf16[32,69]{1,0:T(8,128)(2,1)} %copy-done.9, bf16[32,69]{1,0:T(8,128)(2,1)} %copy-done.10), custom_call_target="tpu_custom_call" | custom-call | tf_op jit(solution)/shard_map/finish/pallas_call | solution.py:533
  (15 shorter events, 0.0 us)
Async XLA Ops:
  2.1 16.6 %collective-permute-start = (bf16[64,69]{1,0:T(8,128)(2,1)}, bf16[64,69]{1,0:T(8,128)(2,1)S(1)}, u32[]{:S(2)}, u32[]{:S(2)}) collective-permute-start(bf16[64,69]{1,0:T(8,128)(2,1)} %get-tuple-element.33), channel_id=1, source_target_pairs={{0,3},{1,0},{2,1},{3,2},{4,7},{5,4},{6,5},{7,6},{8,11},{9,8},{10,9... | collective-permute-start | bytes 26504 | tf_op jit(solution)/shard_map/ppermute | solution.py:406
  3.5 15.2 %collective-permute-start.1 = (bf16[64,69]{1,0:T(8,128)(2,1)}, bf16[64,69]{1,0:T(8,128)(2,1)S(1)}, u32[]{:S(2)}, u32[]{:S(2)}) collective-permute-start(bf16[64,69]{1,0:T(8,128)(2,1)} %get-tuple-element.34), channel_id=1, source_target_pairs={{0,124},{4,0},{8,4},{12,8},{16,12},{20,16},{24,20},{28,24},{32,28}... | collective-permute-start | bytes 26504 | tf_op jit(solution)/shard_map/ppermute | solution.py:407
  12.3 6.5 %collective-permute-start.2 = (bf16[64,69]{1,0:T(8,128)(2,1)}, bf16[64,69]{1,0:T(8,128)(2,1)S(1)}, u32[]{:S(2)}, u32[]{:S(2)}) collective-permute-start(bf16[64,69]{1,0:T(8,128)(2,1)} %get-tuple-element.35), channel_id=1, source_target_pairs={{0,127},{1,124},{2,125},{3,126},{4,3},{5,0},{6,1},{7,2},{8,7},{9,4... | collective-permute-start | bytes 26504 | tf_op jit(solution)/shard_map/ppermute | solution.py:413
  15.1 28.7 %all-to-all-start = ((f32[128,1,64]{2,1,0:T(1,128)}), f32[128,1,64]{2,1,0:T(1,128)S(1)}, u32[]{:S(2)}, u32[]{:S(2)}) async-start(f32[128,1,64]{2,1,0:T(1,128)} %bitcast.21), calls=%async_computation | async-start | bytes 131072 | tf_op jit(solution)/shard_map/all_to_all | solution.py:459
  18.7 0.6 copy-start.11
  18.7 0.6 copy-start.12
  18.8 0.6 copy-start.13
  31.8 4.6 %collective-permute-start.3 = (bf16[32,69]{1,0:T(8,128)(2,1)}, bf16[32,69]{1,0:T(8,128)(2,1)S(1)}, u32[]{:S(2)}, u32[]{:S(2)}) collective-permute-start(bf16[32,69]{1,0:T(8,128)(2,1)} %get-tuple-element.37), channel_id=1, source_target_pairs={{0,1},{1,2},{2,3},{3,0},{4,5},{5,6},{6,7},{7,4},{8,9},{9,10},{10,1... | collective-permute-start | bytes 13256 | tf_op jit(solution)/shard_map/ppermute | solution.py:406
  33.5 8.9 %collective-permute-start.4 = (bf16[32,69]{1,0:T(8,128)(2,1)}, bf16[32,69]{1,0:T(8,128)(2,1)S(1)}, u32[]{:S(2)}, u32[]{:S(2)}) collective-permute-start(bf16[32,69]{1,0:T(8,128)(2,1)} %get-tuple-element.38), channel_id=1, source_target_pairs={{0,4},{4,8},{8,12},{12,16},{16,20},{20,24},{24,28},{28,32},{32,36}... | collective-permute-start | bytes 13256 | tf_op jit(solution)/shard_map/ppermute | solution.py:407
  34.8 9.0 %collective-permute-start.5 = (bf16[32,69]{1,0:T(8,128)(2,1)}, bf16[32,69]{1,0:T(8,128)(2,1)S(1)}, u32[]{:S(2)}, u32[]{:S(2)}) collective-permute-start(bf16[32,69]{1,0:T(8,128)(2,1)} %get-tuple-element.39), channel_id=1, source_target_pairs={{0,5},{1,6},{2,7},{3,4},{4,9},{5,10},{6,11},{7,8},{8,13},{9,14},{1... | collective-permute-start | bytes 13256 | tf_op jit(solution)/shard_map/ppermute | solution.py:413
  36.4 7.4 %copy-start.5 = (bf16[32,69]{1,0:T(8,128)(2,1)}, bf16[32,69]{1,0:T(8,128)(2,1)S(1)}, u32[]{:S(2)}) copy-start(bf16[32,69]{1,0:T(8,128)(2,1)S(1)} %collective-permute-done.3.lat_piece) | copy-start | bytes 13252
  42.4 1.5 %copy-start.6 = (bf16[32,69]{1,0:T(8,128)(2,1)}, bf16[32,69]{1,0:T(8,128)(2,1)S(1)}, u32[]{:S(2)}) copy-start(bf16[32,69]{1,0:T(8,128)(2,1)S(1)} %collective-permute-done.4.lon_piece) | copy-start | bytes 13252
  43.8 0.6 copy-start.8
  43.8 0.6 copy-start
  47.0 7.8 %collective-permute-start.6 = (bf16[32,69]{1,0:T(8,128)(2,1)}, bf16[32,69]{1,0:T(8,128)(2,1)S(1)}, u32[]{:S(2)}, u32[]{:S(2)}) collective-permute-start(bf16[32,69]{1,0:T(8,128)(2,1)} %get-tuple-element.43), channel_id=1, source_target_pairs={{0,3},{1,0},{2,1},{3,2},{4,7},{5,4},{6,5},{7,6},{8,11},{9,8},{10,9... | collective-permute-start | bytes 13256 | tf_op jit(solution)/shard_map/ppermute | solution.py:406
  47.0 7.8 %collective-permute-start.7 = (bf16[32,69]{1,0:T(8,128)(2,1)}, bf16[32,69]{1,0:T(8,128)(2,1)S(1)}, u32[]{:S(2)}, u32[]{:S(2)}) collective-permute-start(bf16[32,69]{1,0:T(8,128)(2,1)} %get-tuple-element.44), channel_id=1, source_target_pairs={{0,124},{4,0},{8,4},{12,8},{16,12},{20,16},{24,20},{28,24},{32,28}... | collective-permute-start | bytes 13256 | tf_op jit(solution)/shard_map/ppermute | solution.py:407
  47.8 7.0 %collective-permute-start.8 = (bf16[32,69]{1,0:T(8,128)(2,1)}, bf16[32,69]{1,0:T(8,128)(2,1)S(1)}, u32[]{:S(2)}, u32[]{:S(2)}) collective-permute-start(bf16[32,69]{1,0:T(8,128)(2,1)} %get-tuple-element.45), channel_id=1, source_target_pairs={{0,127},{1,124},{2,125},{3,126},{4,3},{5,0},{6,1},{7,2},{8,7},{9,4... | collective-permute-start | bytes 13256 | tf_op jit(solution)/shard_map/ppermute | solution.py:413
  50.3 18.1 %all-to-all-start.1 = ((f32[128,1,8]{2,1,0:T(1,128)}), f32[128,1,8]{2,1,0:T(1,128)S(1)}, u32[]{:S(2)}, u32[]{:S(2)}) async-start(f32[128,1,8]{2,1,0:T(1,128)} %bitcast.22), calls=%async_computation.1 | async-start | bytes 131072 | tf_op jit(solution)/shard_map/all_to_all | solution.py:501
  54.8 0.6 copy-start.2
  54.8 0.6 copy-start.3
  54.8 0.6 copy-start.4
  68.5 4.6 %copy-start.1 = (f32[128,1,8]{2,1,0:T(1,128)}, f32[128,1,8]{2,1,0:T(1,128)S(1)}, u32[]{:S(2)}) copy-start(f32[128,1,8]{2,1,0:T(1,128)S(1)} %all-to-all-done.1) | copy-start | bytes 12292
  68.5 6.3 %collective-permute-start.9 = (bf16[32,69]{1,0:T(8,128)(2,1)}, bf16[32,69]{1,0:T(8,128)(2,1)S(1)}, u32[]{:S(2)}, u32[]{:S(2)}) collective-permute-start(bf16[32,69]{1,0:T(8,128)(2,1)} %get-tuple-element.59), channel_id=1, source_target_pairs={{0,1},{1,2},{2,3},{3,0},{4,5},{5,6},{6,7},{7,4},{8,9},{9,10},{10,1... | collective-permute-start | bytes 13256 | tf_op jit(solution)/shard_map/ppermute | solution.py:406
  70.2 8.9 %collective-permute-start.10 = (bf16[32,69]{1,0:T(8,128)(2,1)}, bf16[32,69]{1,0:T(8,128)(2,1)S(1)}, u32[]{:S(2)}, u32[]{:S(2)}) collective-permute-start(bf16[32,69]{1,0:T(8,128)(2,1)} %get-tuple-element.60), channel_id=1, source_target_pairs={{0,4},{4,8},{8,12},{12,16},{16,20},{20,24},{24,28},{28,32},{32,36}... | collective-permute-start | bytes 13256 | tf_op jit(solution)/shard_map/ppermute | solution.py:407
  71.5 9.0 %collective-permute-start.11 = (bf16[32,69]{1,0:T(8,128)(2,1)}, bf16[32,69]{1,0:T(8,128)(2,1)S(1)}, u32[]{:S(2)}, u32[]{:S(2)}) collective-permute-start(bf16[32,69]{1,0:T(8,128)(2,1)} %get-tuple-element.61), channel_id=1, source_target_pairs={{0,5},{1,6},{2,7},{3,4},{4,9},{5,10},{6,11},{7,8},{8,13},{9,14},{1... | collective-permute-start | bytes 13256 | tf_op jit(solution)/shard_map/ppermute | solution.py:413
  74.8 5.8 %copy-start.7 = (bf16[32,69]{1,0:T(8,128)(2,1)}, bf16[32,69]{1,0:T(8,128)(2,1)S(1)}, u32[]{:S(2)}) copy-start(bf16[32,69]{1,0:T(8,128)(2,1)S(1)} %collective-permute-done.9.lat_piece) | copy-start | bytes 13252
  79.0 1.5 %copy-start.9 = (bf16[32,69]{1,0:T(8,128)(2,1)}, bf16[32,69]{1,0:T(8,128)(2,1)S(1)}, u32[]{:S(2)}) copy-start(bf16[32,69]{1,0:T(8,128)(2,1)S(1)} %collective-permute-done.10.lon_piece) | copy-start | bytes 13252
  80.5 0.6 copy-start.10

commit v2 on v1

v2 whole, which is shorter than its diff:
```python
import jax
import jax.numpy as jnp
from jax import lax
from jax.experimental import pallas as pl
from jax.experimental.pallas import tpu as pltpu
from jax.sharding import PartitionSpec as P

HEADS = 16
WLAT = 8
WLON = 16
CELLS = WLAT * WLON
HALF_LAT = WLAT // 2
HALF_LON = WLON // 2
QUARTER = HALF_LAT * HALF_LON
SLOTS = 8
PIECES = 3
QUAD = 256

eps_norm = 1e-05
eps_head = 1e-06

f32 = jnp.float32
bf16 = jnp.bfloat16

NN = ((1,), (0,))
NT = ((1,), (1,))
TN = ((0,), (0,))

VMEM = pl.BlockSpec(memory_space=pltpu.VMEM)
SMEM = pl.BlockSpec(memory_space=pltpu.SMEM)
ANY = pl.BlockSpec(memory_space=pl.ANY)


def product(left, right, dims):
    return lax.dot_general(left, right, (dims, ((), ())), preferred_element_type=f32)


def parts_of(value, count):
    parts = []
    for _ in range(count):
        part = value.astype(bf16)
        parts.append(part)
        value = value - part.astype(f32)
    return parts


def quadrants(top_left, bottom_left, top_right, bottom_right):
    rows = []
    for left, right in ((top_left, top_right), (bottom_left, bottom_right)):
        for i in range(HALF_LAT):
            rows.append(left[i * HALF_LON : (i + 1) * HALF_LON])
            rows.append(right[i * HALF_LON : (i + 1) * HALF_LON])
    return jnp.concatenate(rows, axis=0)


def quadrant_of(cells, row, col):
    return jnp.concatenate(
        [cells[(row + i) * WLON + col : (row + i) * WLON + col + HALF_LON] for i in range(HALF_LAT)], axis=0
    )


def normed_rows(values):
    centred = values - jnp.mean(values, axis=-1, keepdims=True)
    scale = lax.rsqrt(jnp.mean(centred * centred, axis=-1, keepdims=True) + eps_norm)
    return centred * scale, scale


def norm_tangent(unit, scale, tangent):
    moved = tangent - jnp.mean(tangent, axis=-1, keepdims=True)
    return scale * (moved - unit * jnp.mean(unit * tangent, axis=-1, keepdims=True))


def normed_with_tangent(values, tangent):
    centred = values - jnp.mean(values, axis=-1, keepdims=True)
    moved = tangent - jnp.mean(tangent, axis=-1, keepdims=True)
    spread = jnp.mean(centred * centred, axis=-1, keepdims=True)
    along = jnp.mean(centred * moved, axis=-1, keepdims=True)
    scale = lax.rsqrt(spread + eps_norm)
    unit = centred * scale
    return unit, scale * (moved - unit * (scale * along))


def same_head_block():
    rows = lax.broadcasted_iota(jnp.int32, (QUAD, QUAD), 0) >> 6
    return (rows == lax.broadcasted_iota(jnp.int32, (QUAD, QUAD), 1) >> 6).astype(bf16)


def by_head(pair, first):
    zero = jnp.zeros((), pair.dtype)
    return jnp.concatenate([jnp.where(first, pair, zero), jnp.where(first, zero, pair)], axis=0)


def halves(value):
    return value[:, :CELLS], value[:, CELLS:]


def slots_of(owners, rows, devices):
    owner_hot = (lax.broadcasted_iota(jnp.int32, (devices, rows), 0) == owners).astype(f32)
    upper = (
        lax.broadcasted_iota(jnp.int32, (rows, rows), 0) <= lax.broadcasted_iota(jnp.int32, (rows, rows), 1)
    ).astype(bf16)
    counted = product(owner_hot.astype(bf16), upper, NN)
    slots = jnp.sum(counted * owner_hot, axis=0, keepdims=True) - 1.0
    return owner_hot, slots


def prepare_kernel(
    background_ref,
    direction_ref,
    owner_ref,
    site_ref,
    weights_ref,
    precision_ref,
    lat_out,
    lon_out,
    far_out,
    out_ref,
    slots_ref,
):
    for piece_out, row, col in ((lat_out, 0, HALF_LON), (lon_out, HALF_LAT, 0), (far_out, 0, 0)):
        pieces = []
        for source in (background_ref, direction_ref):
            for i in range(HALF_LAT):
                pieces.append(source[row + i, col : col + HALF_LON, :])
        piece_out[...] = jnp.concatenate(pieces, axis=0).astype(bf16)
    rows = owner_ref.shape[1]
    devices = out_ref.shape[0]
    owner_hot, slots = slots_of(owner_ref[...], rows, devices)
    slots_ref[...] = slots
    payload = jnp.concatenate(
        [weights_ref[...], precision_ref[...], site_ref[...].astype(f32), jnp.zeros((2, rows), f32)], axis=0
    )
    owner_hot = owner_hot.astype(bf16)
    spread = jnp.concatenate([jnp.where(slots == float(k), payload, 0.0) for k in range(SLOTS)], axis=0)
    out = jnp.zeros((devices, SLOTS * 8), f32)
    for part in parts_of(spread, PIECES):
        out = out + product(owner_hot, part, NT)
    out_ref[...] = out


def unpack_kernel(owner_ref, slots_ref, returned_ref, out_ref):
    rows = owner_ref.shape[1]
    devices = returned_ref.shape[0]
    owner_hot = (lax.broadcasted_iota(jnp.int32, (devices, rows), 0) == owner_ref[...]).astype(bf16)
    picked = jnp.zeros((SLOTS, rows), f32)
    for part in parts_of(returned_ref[...], PIECES):
        picked = picked + product(part, owner_hot, TN)
    slot_hot = lax.broadcasted_iota(jnp.int32, (SLOTS, rows), 0).astype(f32) == slots_ref[...]
    out_ref[...] = jnp.sum(jnp.where(slot_hot, picked, 0.0), axis=0, keepdims=True)


def forward_kernel(
    band_hbm,
    logit_hbm,
    background_hbm,
    direction_hbm,
    lat_hbm,
    lon_hbm,
    far_hbm,
    embed_hbm,
    gain_hbm,
    decode_gain_hbm,
    decode_hbm,
    qkv_hbm,
    outw_hbm,
    lat_out,
    lon_out,
    far_out,
    own_out,
    hidden_hbm,
    block_hbm,
    unit_q_hbm,
    unit_k_hbm,
    scale_q_hbm,
    scale_k_hbm,
    value_hbm,
    probs_hbm,
    band_ref,
    logit_ref,
    background_ref,
    direction_ref,
    lat_piece,
    lon_piece,
    far_piece,
    embed_ref,
    gain_ref,
    decode_gain_ref,
    decode_ref,
    qkv_ref,
    outw_ref,
    hidden_ref,
    block_ref,
    unit_q_ref,
    unit_k_ref,
    scale_q_ref,
    scale_k_ref,
    value_ref,
    probs_ref,
    mixed_ref,
    sems_in,
    sems_out,
):
    width = embed_ref.shape[1]
    quads = width // QUAD
    count = 0

    def fetch(source, target):
        nonlocal count
        copy = pltpu.make_async_copy(source, target, sems_in.at[count])
        copy.start()
        count += 1
        return copy

    first_needed = [
        fetch(*pair)
        for pair in (
            (lat_hbm, lat_piece),
            (lon_hbm, lon_piece),
            (far_hbm, far_piece),
            (background_hbm, background_ref),
            (direction_hbm, direction_ref),
            (embed_hbm, embed_ref),
            (gain_hbm, gain_ref),
            (band_hbm, band_ref),
            (logit_hbm, logit_ref),
        )
    ]
    fetched = []
    for quad in range(quads):
        for third in range(3):
            columns = pl.ds(third * width + quad * QUAD, QUAD)
            fetched.append(fetch(qkv_hbm.at[:, columns], qkv_ref.at[:, columns]))
    last_needed = [
        fetch(*pair) for pair in ((outw_hbm, outw_ref), (decode_gain_hbm, decode_gain_ref), (decode_hbm, decode_ref))
    ]
    kept = []

    def keep(source, target):
        copy = pltpu.make_async_copy(source, target, sems_out.at[len(kept)])
        copy.start()
        kept.append(copy)

    lane = lax.broadcasted_iota(jnp.int32, (1, 128), 1)
    first = lane < 64
    same_head = same_head_block()
    for copy in first_needed:
        copy.wait()
    low_q = lax.broadcasted_iota(jnp.int32, (CELLS, CELLS), 0) < CELLS // 2
    low_k = lax.broadcasted_iota(jnp.int32, (CELLS, CELLS), 1) < CELLS // 2
    allowed = jnp.where(low_q == low_k, 1.0, 1.0 - band_ref[...])
    logits = logit_ref[...]
    states = []
    for number, source in enumerate((background_ref, direction_ref)):
        own = jnp.concatenate([source[HALF_LAT + i, HALF_LON:, :] for i in range(HALF_LAT)], axis=0)
        part = slice(number * QUARTER, (number + 1) * QUARTER)
        received = [piece[part, :].astype(f32) for piece in (lat_piece, lon_piece, far_piece)]
        states.append(quadrants(own, *received))
    states = jnp.concatenate(states, axis=0).astype(bf16)
    hidden = product(states, embed_ref[...], NN).astype(bf16)
    hidden_ref[...] = hidden
    keep(hidden_ref.at[:CELLS], hidden_hbm)
    hidden = hidden.astype(f32)
    gain = gain_ref[...]
    normed = jnp.concatenate(
        [part * gain for part in normed_with_tangent(hidden[:CELLS], hidden[CELLS:])], axis=0
    ).astype(bf16)

    def project(quad):
        here = pl.ds(quad * QUAD, QUAD)
        packed = []
        for third in range(3):
            packed.append(product(normed, qkv_ref[:, pl.ds(third * width + quad * QUAD, QUAD)], NN))
        raw = jnp.concatenate([packed[0][:CELLS], packed[1][:CELLS]], axis=0)
        raw_tan = jnp.concatenate([packed[0][CELLS:], packed[1][CELLS:]], axis=0)
        scale = lax.rsqrt(product((raw * raw).astype(bf16), same_head, NN) + eps_head)
        unit = raw * scale
        along = product((unit * raw_tan).astype(bf16), same_head, NN)
        unit_tan = (scale * (raw_tan - unit * along)).astype(bf16)
        unit = unit.astype(bf16)
        value = packed[2].astype(bf16)
        scale_q_ref[:, here] = scale[:CELLS]
        scale_k_ref[:, here] = scale[CELLS:]
        unit_q_ref[:, here] = unit[:CELLS]
        unit_k_ref[:, here] = unit[CELLS:]
        value_ref[:, here] = value[:CELLS]
        for source, target in (
            (scale_q_ref, scale_q_hbm),
            (scale_k_ref, scale_k_hbm),
            (unit_q_ref, unit_q_hbm),
            (unit_k_ref, unit_k_hbm),
            (value_ref, value_hbm),
        ):
            keep(source.at[:, here], target.at[:, here])
        return unit, unit_tan, value

    def attend(quad, unit, unit_tan, value):
        for side in range(2):
            pair = quad * 2 + side
            lanes = slice(side * 128, (side + 1) * 128)
            query, key = unit[:CELLS, lanes], by_head(unit[CELLS:, lanes], first)
            query_tan, key_tan = unit_tan[:CELLS, lanes], by_head(unit_tan[CELLS:, lanes], first)
            values = jnp.concatenate(
                [by_head(value[:CELLS, lanes], first), by_head(value[CELLS:, lanes], first)], axis=1
            )
            scores = product(query, key, NT)
            scores_tan = product(
                jnp.concatenate([query, query_tan], axis=1), jnp.concatenate([key_tan, key], axis=1), NT
            )
            probs, probs_tan = [], []
            for half, (score, score_tan) in enumerate(zip(halves(scores), halves(scores_tan))):
                head = pair * 2 + half
                logit = logits[:, head : head + 1]
                weights = jnp.exp(score * logit) * allowed
                prob = weights * (1.0 / jnp.sum(weights, axis=-1, keepdims=True))
                score_tan = score_tan * logit
                prob_tan = prob * (score_tan - jnp.sum(prob * score_tan, axis=-1, keepdims=True))
                probs.append(prob.astype(bf16))
                probs_tan.append(prob_tan.astype(bf16))
            probs = jnp.concatenate(probs, axis=1)
            probs_ref[pair] = probs
            mixed, mixed_tan = halves(product(probs, values, NN))
            mixed_tan = mixed_tan + product(jnp.concatenate(probs_tan, axis=1), values[:, :128], NN)
            columns = pl.ds(pair * 128, 128)
            mixed_ref[:CELLS, columns] = mixed.astype(bf16)
            mixed_ref[CELLS:, columns] = mixed_tan.astype(bf16)
        pairs = pl.ds(quad * 2, 2)
        keep(probs_ref.at[pairs], probs_hbm.at[pairs])

    for copy in fetched[0:3]:
        copy.wait()
    vals0 = project(0)
    for copy in fetched[3:6]:
        copy.wait()
    vals1 = project(1)
    attend(0, *vals0)
    for copy in fetched[6:9]:
        copy.wait()
    vals2 = project(2)
    attend(1, *vals1)
    for copy in fetched[9:12]:
        copy.wait()
    vals3 = project(3)
    attend(2, *vals2)
    attend(3, *vals3)

    for copy in last_needed:
        copy.wait()
    block = (hidden_ref[...].astype(f32) + product(mixed_ref[...], outw_ref[...], NN)).astype(bf16)
    block_ref[...] = block
    keep(block_ref.at[:CELLS], block_hbm)
    block = block.astype(f32)
    moved = normed_with_tangent(block[:CELLS], block[CELLS:])[1]
    change = product((moved * decode_gain_ref[...]).astype(bf16), decode_ref[...], NT)
    lat_out[...] = quadrant_of(change, HALF_LAT, 0).astype(bf16)
    lon_out[...] = quadrant_of(change, 0, HALF_LON).astype(bf16)
    far_out[...] = quadrant_of(change, HALF_LAT, HALF_LON).astype(bf16)
    own_out[...] = quadrant_of(change, 0, 0).astype(bf16)
    for copy in kept:
        copy.wait()


def observe_kernel(
    direction_ref,
    own_piece,
    lat_piece,
    lon_piece,
    far_piece,
    arrived_ref,
    at_obs_out,
    adjoint_out,
    own_out,
    lat_out,
    lon_out,
    far_out,
):
    var_count = direction_ref.shape[2]
    devices = arrived_ref.shape[0]
    pieces = [piece[...].astype(f32) for piece in (far_piece, lon_piece, lat_piece, own_piece)]
    moved = quadrants(*pieces)
    tangent = jnp.concatenate([direction_ref[i] for i in range(WLAT)], axis=0) + moved
    arrived = jnp.transpose(arrived_ref[...])
    cell_ids = lax.broadcasted_iota(jnp.int32, (CELLS, devices), 0).astype(f32)
    var_ids = lax.broadcasted_iota(jnp.int32, (var_count, devices), 0).astype(f32)
    selectors, var_hots, precisions = [], [], []
    for k in range(SLOTS):
        row = arrived[k * 8 : (k + 1) * 8]
        site = row[5:6]
        cell = jnp.floor((site + 0.5) * (1.0 / var_count))
        variable = site - cell * var_count
        selector = jnp.zeros((CELLS, devices), f32)
        for corner, offset in enumerate((0, 1, WLON, WLON + 1)):
            selector = selector + jnp.where(cell_ids == cell + float(offset), row[corner : corner + 1], 0.0)
        selectors.append(selector)
        var_hots.append((var_ids == variable).astype(f32))
        precisions.append(row[4:5])
    selector = jnp.concatenate(selectors, axis=1)
    var_hot = jnp.concatenate(var_hots, axis=1)
    precision = jnp.concatenate(precisions, axis=1)
    selector_parts = parts_of(selector, 2)
    tangent_parts = parts_of(tangent, 3)
    picked = product(tangent_parts[0], selector_parts[0], TN)
    for left, right in ((1, 0), (0, 1), (2, 0)):
        picked = picked + product(tangent_parts[left], selector_parts[right], TN)
    at_obs = jnp.sum(picked * var_hot, axis=0, keepdims=True)
    at_obs_out[...] = jnp.transpose(
        jnp.concatenate([at_obs[:, k * devices : (k + 1) * devices] for k in range(SLOTS)], axis=0)
    )
    spread_parts = parts_of(var_hot * (at_obs * precision), 2)
    adjoint = product(selector_parts[0], spread_parts[0], NT)
    for left, right in ((1, 0), (0, 1)):
        adjoint = adjoint + product(selector_parts[left], spread_parts[right], NT)
    for i in range(WLAT):
        adjoint_out[i] = adjoint[i * WLON : (i + 1) * WLON]
    own_out[...] = quadrant_of(adjoint, HALF_LAT, HALF_LON).astype(bf16)
    lat_out[...] = quadrant_of(adjoint, 0, HALF_LON).astype(bf16)
    lon_out[...] = quadrant_of(adjoint, HALF_LAT, 0).astype(bf16)
    far_out[...] = quadrant_of(adjoint, 0, 0).astype(bf16)


def adjoint_kernel(
    logit_ref,
    own_piece,
    lat_piece,
    lon_piece,
    far_piece,
    decode_gain_ref,
    decode_ref,
    block_ref,
    embed_hbm,
    gain_hbm,
    hidden_hbm,
    unit_q_hbm,
    unit_k_hbm,
    scale_q_hbm,
    scale_k_hbm,
    value_hbm,
    probs_hbm,
    qkv_hbm,
    outw_hbm,
    own_out,
    lat_out,
    lon_out,
    far_out,
    embed_ref,
    gain_ref,
    hidden_ref,
    unit_q_ref,
    unit_k_ref,
    scale_q_ref,
    scale_k_ref,
    value_ref,
    probs_ref,
    qkv_ref,
    outw_ref,
    packed_ref,
    sems,
):
    width = embed_ref.shape[1]
    quads = width // QUAD
    fetched = []
    for source, target in (
        (outw_hbm, outw_ref),
        (value_hbm, value_ref),
        (probs_hbm, probs_ref),
        (unit_q_hbm, unit_q_ref),
        (unit_k_hbm, unit_k_ref),
        (scale_q_hbm, scale_q_ref),
        (scale_k_hbm, scale_k_ref),
        (qkv_hbm, qkv_ref),
        (gain_hbm, gain_ref),
        (hidden_hbm, hidden_ref),
        (embed_hbm, embed_ref),
    ):
        copy = pltpu.make_async_copy(source, target, sems.at[len(fetched)])
        copy.start()
        fetched.append(copy)

    change = quadrants(*[piece[...].astype(f32) for piece in (own_piece, lat_piece, lon_piece, far_piece)])
    unit, scale = normed_rows(block_ref[...].astype(f32))
    normed_ct = product(change.astype(bf16), decode_ref[...], NN).astype(bf16).astype(f32) * decode_gain_ref[...]
    block_ct = norm_tangent(unit, scale, normed_ct).astype(bf16)
    fetched[0].wait()
    mixed_ct = product(block_ct, outw_ref[...], NT).astype(bf16)

    lane = lax.broadcasted_iota(jnp.int32, (1, 128), 1)
    first = lane < 64
    same_head = same_head_block()
    logits = logit_ref[...]
    for copy in fetched[1:7]:
        copy.wait()
    for quad in range(quads):
        cotangents = []
        for side in range(2):
            pair = quad * 2 + side
            here = pl.ds(pair * 128, 128)
            query, key, value = unit_q_ref[:, here], unit_k_ref[:, here], value_ref[:, here]
            mixed_here = mixed_ct[:, pair * 128 : (pair + 1) * 128]
            probs = halves(probs_ref[pair])
            scores_ct = []
            for prob, prob_ct in zip(probs, halves(product(mixed_here, by_head(value, first), NT))):
                prob = prob.astype(f32)
                scores_ct.append((prob * (prob_ct - jnp.sum(prob * prob_ct, axis=-1, keepdims=True))).astype(bf16))
            head = pair * 2
            logit = jnp.where(first, logits[:, head : head + 1], logits[:, head + 1 : head + 2])
            query_ct = product(jnp.concatenate(scores_ct, axis=1), by_head(key, first), NN) * logit
            key_ct = product(jnp.concatenate(scores_ct, axis=0), by_head(query, first), TN) * logit
            value_ct = product(jnp.concatenate(probs, axis=0), by_head(mixed_here, first), TN)
            packed_ref[:, pl.ds(2 * width + pair * 128, 128)] = value_ct.astype(bf16)
            cotangents.append(jnp.concatenate([query_ct, key_ct], axis=0))
        unit_ct = jnp.concatenate(cotangents, axis=1)
        here = pl.ds(quad * QUAD, QUAD)
        units = jnp.concatenate([unit_q_ref[:, here], unit_k_ref[:, here]], axis=0).astype(f32)
        along = product((units * unit_ct).astype(bf16), same_head, NN)
        rest = unit_ct - units * along
        packed_ref[:, here] = (scale_q_ref[:, here] * rest[:CELLS]).astype(bf16)
        packed_ref[:, pl.ds(width + quad * QUAD, QUAD)] = (scale_k_ref[:, here] * rest[CELLS:]).astype(bf16)

    for copy in fetched[7:]:
        copy.wait()
    unit, scale = normed_rows(hidden_ref[...].astype(f32))
    normed_ct = product(packed_ref[...], qkv_ref[...], NT).astype(bf16).astype(f32) * gain_ref[...]
    hidden_ct = (norm_tangent(unit, scale, normed_ct) + block_ct.astype(f32)).astype(bf16)
    state = product(hidden_ct, embed_ref[...], NT)
    lat_out[...] = quadrant_of(state, HALF_LAT, 0).astype(bf16)
    lon_out[...] = quadrant_of(state, 0, HALF_LON).astype(bf16)
    far_out[...] = quadrant_of(state, HALF_LAT, HALF_LON).astype(bf16)
    own_out[...] = quadrant_of(state, 0, 0).astype(bf16)


def finish_kernel(adjoint_ref, own_piece, lat_piece, lon_piece, far_piece, out_ref):
    pieces = [piece[...].astype(f32) for piece in (far_piece, lon_piece, lat_piece, own_piece)]
    moved = quadrants(*pieces)
    for i in range(WLAT):
        out_ref[i] = adjoint_ref[i] + moved[i * WLON : (i + 1) * WLON]


def shape(dims, dtype):
    return jax.ShapeDtypeStruct(dims, dtype)


def exchanged(lat_piece, lon_piece, far_piece, steps):
    lat_count, lon_count = lax.axis_size("lat"), lax.axis_size("lon")
    lat_piece = lax.ppermute(lat_piece, "lat", [(i, (i + steps) % lat_count) for i in range(lat_count)])
    lon_piece = lax.ppermute(lon_piece, "lon", [(i, (i + steps) % lon_count) for i in range(lon_count)])
    pairs = [
        (i * lat_count + j, ((i + steps) % lon_count) * lat_count + (j + steps) % lat_count)
        for i in range(lon_count)
        for j in range(lat_count)
    ]
    far_piece = lax.ppermute(far_piece, ("lon", "lat"), pairs)
    return lat_piece, lon_piece, far_piece


def run_forward(
    last_band, logit_scale, background, direction, strips, embed_weight, gain, decode_gain, decode_rows, qkv_weight, out_weight
):
    width = embed_weight.shape[1]
    quarter = shape((QUARTER, background.shape[2]), bf16)
    wide = shape((CELLS, width), bf16)
    wide_long = shape((CELLS, width), f32)
    kept = [wide, wide, wide, wide, wide_long, wide_long, wide, shape((HEADS // 2, CELLS, 2 * CELLS), bf16)]
    inputs = (last_band, logit_scale, background, direction, *strips, embed_weight, gain, decode_gain, decode_rows, qkv_weight, out_weight)
    both = pltpu.VMEM((2 * CELLS, width), bf16)
    return pl.pallas_call(
        forward_kernel,
        out_shape=[quarter] * 4 + kept,
        in_specs=[ANY] * 13,
        out_specs=[VMEM] * 4 + [ANY] * 8,
        scratch_shapes=[pltpu.VMEM(item.shape, item.dtype) for item in inputs]
        + [both, both]
        + [pltpu.VMEM(item.shape, item.dtype) for item in kept[2:]]
        + [both, pltpu.SemaphoreType.DMA((12 + 3 * (width // QUAD),)), pltpu.SemaphoreType.DMA((2 + 6 * (width // QUAD),))],
        cost_estimate=pl.CostEstimate(flops=2_500_000_000, bytes_accessed=10_000_000, transcendentals=300_000),
        name="forward",
    )(*inputs)


def run_observe(direction, pieces, arrived):
    quarter = shape(pieces[0].shape, bf16)
    devices = arrived.shape[0]
    return pl.pallas_call(
        observe_kernel,
        out_shape=[shape((devices, SLOTS), f32), shape(direction.shape, f32)] + [quarter] * 4,
        in_specs=[VMEM] * 6,
        out_specs=[VMEM] * 6,
        name="observe",
    )(direction, *pieces, arrived)


def run_adjoint(logit_scale, pieces, embed_weight, gain, decode_gain, decode_rows, kept, qkv_weight, out_weight):
    hidden, block, *attention = kept
    width = embed_weight.shape[1]
    late = (embed_weight, gain, hidden, *attention, qkv_weight, out_weight)
    return pl.pallas_call(
        adjoint_kernel,
        out_shape=[shape(pieces[0].shape, bf16)] * 4,
        in_specs=[VMEM] * 8 + [ANY] * len(late),
        out_specs=[VMEM] * 4,
        scratch_shapes=[pltpu.VMEM(item.shape, item.dtype) for item in late]
        + [pltpu.VMEM((CELLS, 3 * width), bf16), pltpu.SemaphoreType.DMA((len(late),))],
        cost_estimate=pl.CostEstimate(flops=1_500_000_000, bytes_accessed=10_000_000, transcendentals=300_000),
        name="adjoint",
    )(logit_scale, *pieces, decode_gain, decode_rows, block, *late)


def per_device(
    background,
    direction,
    obs_owner,
    obs_site,
    obs_weights,
    obs_precision,
    embed_weight,
    attn_gain,
    qkv_weight,
    logit_scale,
    out_weight,
    decode_gain,
    decode_weight,
):
    var_count = background.shape[2]
    width = embed_weight.shape[1]
    devices = lax.axis_size("lat") * lax.axis_size("lon")
    obs_rows = obs_site.shape[0]
    last_band = (lax.axis_index("lat") == lax.axis_size("lat") - 1).astype(f32).reshape(1, 1)
    logit_scale = logit_scale.reshape(1, HEADS)
    gain = attn_gain.reshape(1, width)
    decode_gain = decode_gain.reshape(1, width)
    decode_rows = decode_weight.T

    owners = obs_owner.reshape(1, obs_rows)
    *strips, outgoing, slots = pl.pallas_call(
        prepare_kernel,
        out_shape=[shape((2 * QUARTER, var_count), bf16)] * 3
        + [shape((devices, SLOTS * 8), f32), shape((1, obs_rows), f32)],
        in_specs=[VMEM] * 6,
        out_specs=[VMEM] * 5,
        name="prepare",
    )(
        background,
        direction,
        owners,
        obs_site.reshape(1, obs_rows),
        obs_weights.T,
        obs_precision.reshape(1, obs_rows),
    )
    strips = exchanged(*strips, -1)
    arrived = lax.all_to_all(outgoing, ("lon", "lat"), split_axis=0, concat_axis=0, tiled=True)

    lat_piece, lon_piece, far_piece, own_piece, *kept = run_forward(
        last_band, logit_scale, background, direction, strips, embed_weight, gain, decode_gain, decode_rows, qkv_weight, out_weight
    )
    lat_piece, lon_piece, far_piece = exchanged(lat_piece, lon_piece, far_piece, 1)

    at_obs, adjoint_field, own_piece, lat_piece, lon_piece, far_piece = run_observe(
        direction, (own_piece, lat_piece, lon_piece, far_piece), arrived
    )
    lat_piece, lon_piece, far_piece = exchanged(lat_piece, lon_piece, far_piece, -1)
    returned = lax.all_to_all(at_obs, ("lon", "lat"), split_axis=0, concat_axis=0, tiled=True)

    own_piece, lat_piece, lon_piece, far_piece = run_adjoint(
        logit_scale, (own_piece, lat_piece, lon_piece, far_piece), embed_weight, gain, decode_gain, decode_rows, kept, qkv_weight, out_weight
    )
    lat_piece, lon_piece, far_piece, returned = lax.optimization_barrier((lat_piece, lon_piece, far_piece, returned))
    lat_piece, lon_piece, far_piece = exchanged(lat_piece, lon_piece, far_piece, 1)

    hvp = pl.pallas_call(
        finish_kernel,
        out_shape=shape(background.shape, f32),
        in_specs=[VMEM] * 5,
        out_specs=VMEM,
        name="finish",
    )(adjoint_field, own_piece, lat_piece, lon_piece, far_piece)
    obs_increment = pl.pallas_call(
        unpack_kernel,
        out_shape=shape((1, obs_rows), f32),
        in_specs=[VMEM] * 3,
        out_specs=VMEM,
        name="unpack",
    )(owners, slots, returned)
    return (hvp, obs_increment.reshape(obs_rows))


def solution(mesh):
    in_specs = (
        P("lat", "lon", None),
        P("lat", "lon", None),
        P(("lon", "lat"), None),
        P(("lon", "lat")),
        P(("lon", "lat"), None),
        P(("lon", "lat")),
        P(),
        P(),
        P(),
        P(),
        P(),
        P(),
        P(),
    )
    out_specs = (P("lat", "lon", None), P(("lon", "lat")))
    return jax.shard_map(
        per_device, mesh=mesh, in_specs=in_specs, out_specs=out_specs, check_vma=False
    )
```

time: 83.1 us -> 75.1 us (0.904)
  Pallas kernels: 34.5 us -> 26.7 us
    pallas_call x5 -> x4, Pallas kernels: 31.4 us -> 23.5 us  [the longest x1 9.56 us: run_forward(): pl.pallas_call(forward_kernel, out_shape=[quarter] * 4 + kept, in_specs=[...]
  transfers between devices with their start and end apart: 14 -> 14, of which waited for: 4 -> 4; matrix products, arithmetic and copies ran while one was open for 0% -> 0% of each run, Pallas kernels for 35% -> 28%
where the time goes in v2:
time: 75.1 us; the launch traced here: 74.8 us
  starting transfers between devices  31.7 us (42%)
  Pallas kernels  26.7 us (36%)
  waiting for transfers between devices  13.2 us (18%)
  local copies, waits for them, and re-layouts  2.42 us (3%)
  between operations  0.82 us (1%)
    ppermute x4, starting transfers between devices, exchanged(): lax.ppermute(lon_piece, 'lon', [(i, (i + steps) % lon_count) for i in ran...  12.3 us
    ppermute x4, waiting for transfers between devices, exchanged(): lax.ppermute(lon_piece, 'lon', [(i, (i + steps) % lon_count) for i in ran...  10.3 us
    pallas_call x1, Pallas kernels, run_forward(): pl.pallas_call(forward_kernel, out_shape=[quarter] * 4 + kept, in_specs=[...  9.56 us
    pallas_call x1, Pallas kernels, run_adjoint(): pl.pallas_call(adjoint_kernel, out_shape=[shape(pieces[0].shape, bf16)] *...  9.37 us
    ppermute x4, starting transfers between devices, exchanged(): far_piece = lax.ppermute(far_piece, ('lon', 'lat'), pairs)  6.62 us
    ppermute x4, starting transfers between devices, exchanged(): lax.ppermute(lat_piece, 'lat', [(i, (i + steps) % lat_count) for i in ran...  4.83 us
    all_to_all x1, starting transfers between devices, per_device(): lax.all_to_all(at_obs, ('lon', 'lat'), split_axis=0, concat_axis=0, tiled...  4.42 us
    all_to_all x1, starting transfers between devices, per_device(): lax.all_to_all(outgoing, ('lon', 'lat'), split_axis=0, concat_axis=0, til...  3.56 us
  transfers between devices with their start and end apart: 14, of which 4 were waited for; matrix products, arithmetic and copies ran while one was open for 0% of the time, Pallas kernels for 28%

profile of v2, /device:TPU:1, one launch (start us, length us, event | category | flops | bytes accessed | tf_op | source)
XLA Modules:
  0.0 74.8 jit_solution(2265032296585526824)
XLA Ops:
  0.6 2.1 %prepare.1 = (bf16[64,69]{1,0:T(8,128)(2,1)}, bf16[64,69]{1,0:T(8,128)(2,1)}, bf16[64,69]{1,0:T(8,128)(2,1)}, f32[128,64]{1,0:T(8,128)}, f32[1,512]{1,0:T(1,128)}) custom-call(f32[8,16,69]{2,1,0:T(8,128)} %background_hbm.1, f32[8,16,69]{2,1,0:T(8,128)} %direction_ref.3, s32[1,512]{1,0:T(1,128)} %bitcast.24, s32[1,512]{1,0:T(1,128)} %bitcast.31, ...), custom_call_target="tpu_custom_call" | custom-call | tf_op jit(solution)/shard_map/prepare/pallas_call | solution.py:632
  2.7 1.4 %collective-permute-start = (bf16[64,69]{1,0:T(8,128)(2,1)}, bf16[64,69]{1,0:T(8,128)(2,1)S(1)}, u32[]{:S(2)}, u32[]{:S(2)}) collective-permute-start(bf16[64,69]{1,0:T(8,128)(2,1)} %get-tuple-element.33), channel_id=1, source_target_pairs={{0,3},{1,0},{2,1},{3,2},{4,7},{5,4},{6,5},{7,6},{8,11},{9,8},{10,9... | collective-permute-start | bytes 26504 | tf_op jit(solution)/shard_map/ppermute | solution.py:543
  4.1 8.8 %collective-permute-start.1 = (bf16[64,69]{1,0:T(8,128)(2,1)}, bf16[64,69]{1,0:T(8,128)(2,1)S(1)}, u32[]{:S(2)}, u32[]{:S(2)}) collective-permute-start(bf16[64,69]{1,0:T(8,128)(2,1)} %get-tuple-element.34), channel_id=1, source_target_pairs={{0,124},{4,0},{8,4},{12,8},{16,12},{20,16},{24,20},{28,24},{32,28}... | collective-permute-start | bytes 26504 | tf_op jit(solution)/shard_map/ppermute | solution.py:544
  12.9 0.9 %collective-permute-start.2 = (bf16[64,69]{1,0:T(8,128)(2,1)}, bf16[64,69]{1,0:T(8,128)(2,1)S(1)}, u32[]{:S(2)}, u32[]{:S(2)}) collective-permute-start(bf16[64,69]{1,0:T(8,128)(2,1)} %get-tuple-element.35), channel_id=1, source_target_pairs={{0,127},{1,124},{2,125},{3,126},{4,3},{5,0},{6,1},{7,2},{8,7},{9,4... | collective-permute-start | bytes 26504 | tf_op jit(solution)/shard_map/ppermute | solution.py:550
  13.8 3.6 %all-to-all-start = ((f32[128,1,64]{2,1,0:T(1,128)}), f32[128,1,64]{2,1,0:T(1,128)S(1)}, u32[]{:S(2)}, u32[]{:S(2)}) async-start(f32[128,1,64]{2,1,0:T(1,128)} %bitcast.22), calls=%async_computation | async-start | bytes 131072 | tf_op jit(solution)/shard_map/all_to_all | solution.py:648
  17.4 0.0 collective-permute-done.lat_hbm
  17.4 0.0 copy-start.11
  17.4 0.0 collective-permute-done.1.lon_hbm
  17.4 0.0 copy-start.12
  17.4 0.0 collective-permute-done.2.far_hbm
  17.4 0.0 copy-start.13
  17.5 0.5 copy-done.11
  18.0 0.0 copy-done.12
  18.0 0.0 copy-done.13
  18.0 9.6 %forward.1 = (bf16[32,69]{1,0:T(8,128)(2,1)}, bf16[32,69]{1,0:T(8,128)(2,1)}, bf16[32,69]{1,0:T(8,128)(2,1)}, bf16[32,69]{1,0:T(8,128)(2,1)}, bf16[128,1024]{1,0...) custom-call(f32[1,1]{1,0:T(1,128)} %bitcast.band_hbm, ...), custom_call_target="tpu_custom_call" | custom-call | flops 2500000000 | bytes 10000000 | tf_op jit(solution)/shard_map/forward/pallas_call | solution.py:564
  27.6 1.7 %collective-permute-start.3 = (bf16[32,69]{1,0:T(8,128)(2,1)}, bf16[32,69]{1,0:T(8,128)(2,1)S(1)}, u32[]{:S(2)}, u32[]{:S(2)}) collective-permute-start(bf16[32,69]{1,0:T(8,128)(2,1)} %get-tuple-element.37), channel_id=1, source_target_pairs={{0,1},{1,2},{2,3},{3,0},{4,5},{5,6},{6,7},{7,4},{8,9},{9,10},{10,1... | collective-permute-start | bytes 13256 | tf_op jit(solution)/shard_map/ppermute | solution.py:543
  29.3 1.3 %collective-permute-start.4 = (bf16[32,69]{1,0:T(8,128)(2,1)}, bf16[32,69]{1,0:T(8,128)(2,1)S(1)}, u32[]{:S(2)}, u32[]{:S(2)}) collective-permute-start(bf16[32,69]{1,0:T(8,128)(2,1)} %get-tuple-element.38), channel_id=1, source_target_pairs={{0,4},{4,8},{8,12},{12,16},{16,20},{20,24},{24,28},{28,32},{32,36}... | collective-permute-start | bytes 13256 | tf_op jit(solution)/shard_map/ppermute | solution.py:544
  30.6 1.6 %collective-permute-start.5 = (bf16[32,69]{1,0:T(8,128)(2,1)}, bf16[32,69]{1,0:T(8,128)(2,1)S(1)}, u32[]{:S(2)}, u32[]{:S(2)}) collective-permute-start(bf16[32,69]{1,0:T(8,128)(2,1)} %get-tuple-element.39), channel_id=1, source_target_pairs={{0,5},{1,6},{2,7},{3,4},{4,9},{5,10},{6,11},{7,8},{8,13},{9,14},{1... | collective-permute-start | bytes 13256 | tf_op jit(solution)/shard_map/ppermute | solution.py:550
  32.2 0.0 collective-permute-done.3.lat_piece
  32.2 5.9 %collective-permute-done.4.lon_piece = bf16[32,69]{1,0:T(8,128)(2,1)S(1)} collective-permute-done((bf16[32,69]{1,0:T(8,128)(2,1)}, bf16[32,69]{1,0:T(8,128)(2,1)S(1)}, u32[]{:S(2)}, u32[]{:S(2)}) %collective-permute-start.4) | collective-permute-done | bytes 4448 | tf_op jit(solution)/shard_map/ppermute | solution.py:544
  38.2 1.5 %collective-permute-done.5.far_piece = bf16[32,69]{1,0:T(8,128)(2,1)S(1)} collective-permute-done((bf16[32,69]{1,0:T(8,128)(2,1)}, bf16[32,69]{1,0:T(8,128)(2,1)S(1)}, u32[]{:S(2)}, u32[]{:S(2)}) %collective-permute-start.5) | collective-permute-done | bytes 4448 | tf_op jit(solution)/shard_map/ppermute | solution.py:550
  39.6 0.0 all-to-all-done
  39.7 0.6 copy-done.8
  40.2 0.0 copy-done
  40.3 2.5 %observe.1 = (f32[128,8]{1,0:T(8,128)}, f32[8,16,69]{2,1,0:T(8,128)}, bf16[32,69]{1,0:T(8,128)(2,1)}, bf16[32,69]{1,0:T(8,128)(2,1)}, bf16[32,69]{1,0:T(8,128)(2,1)}, /*index=5*/bf16[32,69]{1,0:T(8,128)(2,1)}) custom-call(f32[8,16,69]{2,1,0:T(8,128)} %direction_ref.3, bf16[32,69]{1,0:T(8,128)(2,1)} %get-tuple-element.36.own_piece, bf16[32,69]{1,0:T(8,128)(2,1)} %copy-done.5, ...), custom_call_target="tpu_custom_call" | custom-call | tf_op jit(solution)/shard_map/observe/pallas_call | solution.py:581
  42.8 0.0 collective-permute-start.6
  42.8 0.9 %collective-permute-start.7 = (bf16[32,69]{1,0:T(8,128)(2,1)}, bf16[32,69]{1,0:T(8,128)(2,1)S(1)}, u32[]{:S(2)}, u32[]{:S(2)}) collective-permute-start(bf16[32,69]{1,0:T(8,128)(2,1)} %get-tuple-element.44), channel_id=1, source_target_pairs={{0,124},{4,0},{8,4},{12,8},{16,12},{20,16},{24,20},{28,24},{32,28}... | collective-permute-start | bytes 13256 | tf_op jit(solution)/shard_map/ppermute | solution.py:544
  43.6 2.5 %collective-permute-start.8 = (bf16[32,69]{1,0:T(8,128)(2,1)}, bf16[32,69]{1,0:T(8,128)(2,1)S(1)}, u32[]{:S(2)}, u32[]{:S(2)}) collective-permute-start(bf16[32,69]{1,0:T(8,128)(2,1)} %get-tuple-element.45), channel_id=1, source_target_pairs={{0,127},{1,124},{2,125},{3,126},{4,3},{5,0},{6,1},{7,2},{8,7},{9,4... | collective-permute-start | bytes 13256 | tf_op jit(solution)/shard_map/ppermute | solution.py:550
  46.1 4.4 %all-to-all-start.1 = ((f32[128,1,8]{2,1,0:T(1,128)}), f32[128,1,8]{2,1,0:T(1,128)S(1)}, u32[]{:S(2)}, u32[]{:S(2)}) async-start(f32[128,1,8]{2,1,0:T(1,128)} %bitcast.23), calls=%async_computation.1 | async-start | bytes 131072 | tf_op jit(solution)/shard_map/all_to_all | solution.py:659
  50.6 0.0 collective-permute-done.6.lat_piece
  50.6 0.0 copy-start.2
  50.6 0.0 collective-permute-done.7.lon_piece
  50.6 0.0 collective-permute-done.8.far_piece
  50.6 0.5 copy-done.2
  51.2 0.0 copy-done.3
  51.2 0.0 copy-done.4
  51.2 9.4 %adjoint.1 = (bf16[32,69]{1,0:T(8,128)(2,1)}, bf16[32,69]{1,0:T(8,128)(2,1)}, bf16[32,69]{1,0:T(8,128)(2,1)}, bf16[32,69]{1,0:T(8,128)(2,1)}) custom-call(f32[1,16]{1,0:T(1,128)} %bitcast.35, bf16[32,69]{1,0:T(8,128)(2,1)} %get-tuple-element.42.own_piece, bf16[32,69]{1,0:T(8,128)(2,1)} %copy-done.2, bf16[32,69]{1,0:T(8,128)(2,1)} %copy-done.3, ...), custom_call_target="tpu_custom_call" | custom-call | flops 1500000000 | bytes 10000000 | tf_op jit(solution)/shard_map/adjoint/pallas_call | solution.py:594
  60.6 0.0 all-to-all-done.1
  60.6 0.0 copy-start.1
  60.6 1.7 %collective-permute-start.9 = (bf16[32,69]{1,0:T(8,128)(2,1)}, bf16[32,69]{1,0:T(8,128)(2,1)S(1)}, u32[]{:S(2)}, u32[]{:S(2)}) collective-permute-start(bf16[32,69]{1,0:T(8,128)(2,1)} %get-tuple-element.59), channel_id=1, source_target_pairs={{0,1},{1,2},{2,3},{3,0},{4,5},{5,6},{6,7},{7,4},{8,9},{9,10},{10,1... | collective-permute-start | bytes 13256 | tf_op jit(solution)/shard_map/ppermute | solution.py:543
  62.3 1.3 %collective-permute-start.10 = (bf16[32,69]{1,0:T(8,128)(2,1)}, bf16[32,69]{1,0:T(8,128)(2,1)S(1)}, u32[]{:S(2)}, u32[]{:S(2)}) collective-permute-start(bf16[32,69]{1,0:T(8,128)(2,1)} %get-tuple-element.60), channel_id=1, source_target_pairs={{0,4},{4,8},{8,12},{12,16},{16,20},{20,24},{24,28},{28,32},{32,36}... | collective-permute-start | bytes 13256 | tf_op jit(solution)/shard_map/ppermute | solution.py:544
  63.6 1.6 %collective-permute-start.11 = (bf16[32,69]{1,0:T(8,128)(2,1)}, bf16[32,69]{1,0:T(8,128)(2,1)S(1)}, u32[]{:S(2)}, u32[]{:S(2)}) collective-permute-start(bf16[32,69]{1,0:T(8,128)(2,1)} %get-tuple-element.61), channel_id=1, source_target_pairs={{0,5},{1,6},{2,7},{3,4},{4,9},{5,10},{6,11},{7,8},{8,13},{9,14},{1... | collective-permute-start | bytes 13256 | tf_op jit(solution)/shard_map/ppermute | solution.py:550
  65.2 1.7 %unpack.1 = f32[1,512]{1,0:T(1,128)} custom-call(s32[1,512]{1,0:T(1,128)} %bitcast.25, f32[1,512]{1,0:T(1,128)} %get-tuple-element.62.slots_ref, f32[128,8]{1,0:T(8,128)} %bitcast.19), custom_call_target="tpu_custom_call" | custom-call | tf_op jit(solution)/shard_map/unpack/pallas_call | solution.py:674
  66.9 0.0 collective-permute-done.9.lat_piece
  66.9 4.3 %collective-permute-done.10.lon_piece = bf16[32,69]{1,0:T(8,128)(2,1)S(1)} collective-permute-done((bf16[32,69]{1,0:T(8,128)(2,1)}, bf16[32,69]{1,0:T(8,128)(2,1)S(1)}, u32[]{:S(2)}, u32[]{:S(2)}) %collective-permute-start.10) | collective-permute-done | bytes 4448 | tf_op jit(solution)/shard_map/ppermute | solution.py:544
  71.2 1.4 %collective-permute-done.11.far_piece = bf16[32,69]{1,0:T(8,128)(2,1)S(1)} collective-permute-done((bf16[32,69]{1,0:T(8,128)(2,1)}, bf16[32,69]{1,0:T(8,128)(2,1)S(1)}, u32[]{:S(2)}, u32[]{:S(2)}) %collective-permute-start.11) | collective-permute-done | bytes 4448 | tf_op jit(solution)/shard_map/ppermute | solution.py:550
  72.6 0.6 copy-done.10
  73.2 1.5 %finish.1 = f32[8,16,69]{2,1,0:T(8,128)} custom-call(f32[8,16,69]{2,1,0:T(8,128)} %get-tuple-element.41.adjoint_ref, bf16[32,69]{1,0:T(8,128)(2,1)} %get-tuple-element.54.own_piece, bf16[32,69]{1,0:T(8,128)(2,1)} %copy-done.7, bf16[32,69]{1,0:T(8,128)(2,1)} %copy-done.9, bf16[32,69]{1,0:T(8,128)(2,1)} %copy-done.10), custom_call_target="tpu_custom_call" | custom-call | tf_op jit(solution)/shard_map/finish/pallas_call | solution.py:667
  (14 shorter events, 0.0 us)
Async XLA Ops:
  2.7 14.7 %collective-permute-start = (bf16[64,69]{1,0:T(8,128)(2,1)}, bf16[64,69]{1,0:T(8,128)(2,1)S(1)}, u32[]{:S(2)}, u32[]{:S(2)}) collective-permute-start(bf16[64,69]{1,0:T(8,128)(2,1)} %get-tuple-element.33), channel_id=1, source_target_pairs={{0,3},{1,0},{2,1},{3,2},{4,7},{5,4},{6,5},{7,6},{8,11},{9,8},{10,9... | collective-permute-start | bytes 26504 | tf_op jit(solution)/shard_map/ppermute | solution.py:543
  4.1 13.3 %collective-permute-start.1 = (bf16[64,69]{1,0:T(8,128)(2,1)}, bf16[64,69]{1,0:T(8,128)(2,1)S(1)}, u32[]{:S(2)}, u32[]{:S(2)}) collective-permute-start(bf16[64,69]{1,0:T(8,128)(2,1)} %get-tuple-element.34), channel_id=1, source_target_pairs={{0,124},{4,0},{8,4},{12,8},{16,12},{20,16},{24,20},{28,24},{32,28}... | collective-permute-start | bytes 26504 | tf_op jit(solution)/shard_map/ppermute | solution.py:544
  12.9 4.5 %collective-permute-start.2 = (bf16[64,69]{1,0:T(8,128)(2,1)}, bf16[64,69]{1,0:T(8,128)(2,1)S(1)}, u32[]{:S(2)}, u32[]{:S(2)}) collective-permute-start(bf16[64,69]{1,0:T(8,128)(2,1)} %get-tuple-element.35), channel_id=1, source_target_pairs={{0,127},{1,124},{2,125},{3,126},{4,3},{5,0},{6,1},{7,2},{8,7},{9,4... | collective-permute-start | bytes 26504 | tf_op jit(solution)/shard_map/ppermute | solution.py:550
  13.8 25.8 %all-to-all-start = ((f32[128,1,64]{2,1,0:T(1,128)}), f32[128,1,64]{2,1,0:T(1,128)S(1)}, u32[]{:S(2)}, u32[]{:S(2)}) async-start(f32[128,1,64]{2,1,0:T(1,128)} %bitcast.22), calls=%async_computation | async-start | bytes 131072 | tf_op jit(solution)/shard_map/all_to_all | solution.py:648
  17.4 0.6 copy-start.11
  17.4 0.6 copy-start.12
  17.4 0.6 copy-start.13
  27.6 4.6 %collective-permute-start.3 = (bf16[32,69]{1,0:T(8,128)(2,1)}, bf16[32,69]{1,0:T(8,128)(2,1)S(1)}, u32[]{:S(2)}, u32[]{:S(2)}) collective-permute-start(bf16[32,69]{1,0:T(8,128)(2,1)} %get-tuple-element.37), channel_id=1, source_target_pairs={{0,1},{1,2},{2,3},{3,0},{4,5},{5,6},{6,7},{7,4},{8,9},{9,10},{10,1... | collective-permute-start | bytes 13256 | tf_op jit(solution)/shard_map/ppermute | solution.py:543
  29.3 8.9 %collective-permute-start.4 = (bf16[32,69]{1,0:T(8,128)(2,1)}, bf16[32,69]{1,0:T(8,128)(2,1)S(1)}, u32[]{:S(2)}, u32[]{:S(2)}) collective-permute-start(bf16[32,69]{1,0:T(8,128)(2,1)} %get-tuple-element.38), channel_id=1, source_target_pairs={{0,4},{4,8},{8,12},{12,16},{16,20},{20,24},{24,28},{28,32},{32,36}... | collective-permute-start | bytes 13256 | tf_op jit(solution)/shard_map/ppermute | solution.py:544
  30.6 9.0 %collective-permute-start.5 = (bf16[32,69]{1,0:T(8,128)(2,1)}, bf16[32,69]{1,0:T(8,128)(2,1)S(1)}, u32[]{:S(2)}, u32[]{:S(2)}) collective-permute-start(bf16[32,69]{1,0:T(8,128)(2,1)} %get-tuple-element.39), channel_id=1, source_target_pairs={{0,5},{1,6},{2,7},{3,4},{4,9},{5,10},{6,11},{7,8},{8,13},{9,14},{1... | collective-permute-start | bytes 13256 | tf_op jit(solution)/shard_map/ppermute | solution.py:550
  32.2 7.4 %copy-start.5 = (bf16[32,69]{1,0:T(8,128)(2,1)}, bf16[32,69]{1,0:T(8,128)(2,1)S(1)}, u32[]{:S(2)}) copy-start(bf16[32,69]{1,0:T(8,128)(2,1)S(1)} %collective-permute-done.3.lat_piece) | copy-start | bytes 13252
  38.2 1.5 %copy-start.6 = (bf16[32,69]{1,0:T(8,128)(2,1)}, bf16[32,69]{1,0:T(8,128)(2,1)S(1)}, u32[]{:S(2)}) copy-start(bf16[32,69]{1,0:T(8,128)(2,1)S(1)} %collective-permute-done.4.lon_piece) | copy-start | bytes 13252
  39.6 0.6 copy-start.8
  39.6 0.6 copy-start
  42.8 7.8 %collective-permute-start.6 = (bf16[32,69]{1,0:T(8,128)(2,1)}, bf16[32,69]{1,0:T(8,128)(2,1)S(1)}, u32[]{:S(2)}, u32[]{:S(2)}) collective-permute-start(bf16[32,69]{1,0:T(8,128)(2,1)} %get-tuple-element.43), channel_id=1, source_target_pairs={{0,3},{1,0},{2,1},{3,2},{4,7},{5,4},{6,5},{7,6},{8,11},{9,8},{10,9... | collective-permute-start | bytes 13256 | tf_op jit(solution)/shard_map/ppermute | solution.py:543
  42.8 7.8 %collective-permute-start.7 = (bf16[32,69]{1,0:T(8,128)(2,1)}, bf16[32,69]{1,0:T(8,128)(2,1)S(1)}, u32[]{:S(2)}, u32[]{:S(2)}) collective-permute-start(bf16[32,69]{1,0:T(8,128)(2,1)} %get-tuple-element.44), channel_id=1, source_target_pairs={{0,124},{4,0},{8,4},{12,8},{16,12},{20,16},{24,20},{28,24},{32,28}... | collective-permute-start | bytes 13256 | tf_op jit(solution)/shard_map/ppermute | solution.py:544
  43.6 7.0 %collective-permute-start.8 = (bf16[32,69]{1,0:T(8,128)(2,1)}, bf16[32,69]{1,0:T(8,128)(2,1)S(1)}, u32[]{:S(2)}, u32[]{:S(2)}) collective-permute-start(bf16[32,69]{1,0:T(8,128)(2,1)} %get-tuple-element.45), channel_id=1, source_target_pairs={{0,127},{1,124},{2,125},{3,126},{4,3},{5,0},{6,1},{7,2},{8,7},{9,4... | collective-permute-start | bytes 13256 | tf_op jit(solution)/shard_map/ppermute | solution.py:550
  46.1 14.5 %all-to-all-start.1 = ((f32[128,1,8]{2,1,0:T(1,128)}), f32[128,1,8]{2,1,0:T(1,128)S(1)}, u32[]{:S(2)}, u32[]{:S(2)}) async-start(f32[128,1,8]{2,1,0:T(1,128)} %bitcast.23), calls=%async_computation.1 | async-start | bytes 131072 | tf_op jit(solution)/shard_map/all_to_all | solution.py:659
  50.6 0.6 copy-start.2
  50.6 0.6 copy-start.3
  50.6 0.6 copy-start.4
  60.6 4.6 %copy-start.1 = (f32[128,1,8]{2,1,0:T(1,128)}, f32[128,1,8]{2,1,0:T(1,128)S(1)}, u32[]{:S(2)}) copy-start(f32[128,1,8]{2,1,0:T(1,128)S(1)} %all-to-all-done.1) | copy-start | bytes 12292
  60.6 6.3 %collective-permute-start.9 = (bf16[32,69]{1,0:T(8,128)(2,1)}, bf16[32,69]{1,0:T(8,128)(2,1)S(1)}, u32[]{:S(2)}, u32[]{:S(2)}) collective-permute-start(bf16[32,69]{1,0:T(8,128)(2,1)} %get-tuple-element.59), channel_id=1, source_target_pairs={{0,1},{1,2},{2,3},{3,0},{4,5},{5,6},{6,7},{7,4},{8,9},{9,10},{10,1... | collective-permute-start | bytes 13256 | tf_op jit(solution)/shard_map/ppermute | solution.py:543
  62.3 8.9 %collective-permute-start.10 = (bf16[32,69]{1,0:T(8,128)(2,1)}, bf16[32,69]{1,0:T(8,128)(2,1)S(1)}, u32[]{:S(2)}, u32[]{:S(2)}) collective-permute-start(bf16[32,69]{1,0:T(8,128)(2,1)} %get-tuple-element.60), channel_id=1, source_target_pairs={{0,4},{4,8},{8,12},{12,16},{16,20},{20,24},{24,28},{28,32},{32,36}... | collective-permute-start | bytes 13256 | tf_op jit(solution)/shard_map/ppermute | solution.py:544
  63.6 9.0 %collective-permute-start.11 = (bf16[32,69]{1,0:T(8,128)(2,1)}, bf16[32,69]{1,0:T(8,128)(2,1)S(1)}, u32[]{:S(2)}, u32[]{:S(2)}) collective-permute-start(bf16[32,69]{1,0:T(8,128)(2,1)} %get-tuple-element.61), channel_id=1, source_target_pairs={{0,5},{1,6},{2,7},{3,4},{4,9},{5,10},{6,11},{7,8},{8,13},{9,14},{1... | collective-permute-start | bytes 13256 | tf_op jit(solution)/shard_map/ppermute | solution.py:550
  66.9 5.8 %copy-start.7 = (bf16[32,69]{1,0:T(8,128)(2,1)}, bf16[32,69]{1,0:T(8,128)(2,1)S(1)}, u32[]{:S(2)}) copy-start(bf16[32,69]{1,0:T(8,128)(2,1)S(1)} %collective-permute-done.9.lat_piece) | copy-start | bytes 13252
  71.2 1.4 %copy-start.9 = (bf16[32,69]{1,0:T(8,128)(2,1)}, bf16[32,69]{1,0:T(8,128)(2,1)S(1)}, u32[]{:S(2)}) copy-start(bf16[32,69]{1,0:T(8,128)(2,1)S(1)} %collective-permute-done.10.lon_piece) | copy-start | bytes 13252
  72.6 0.6 copy-start.10

commit v3 on v2

--- a/solution.py
+++ b/solution.py
@@ -154,9 +154,9 @@
     logit_hbm,
     background_hbm,
     direction_hbm,
-    lat_hbm,
     lon_hbm,
     far_hbm,
+    lat_hbm,
     embed_hbm,
     gain_hbm,
     decode_gain_hbm,
@@ -169,19 +169,16 @@
     own_out,
     hidden_hbm,
     block_hbm,
-    unit_q_hbm,
-    unit_k_hbm,
-    scale_q_hbm,
-    scale_k_hbm,
-    value_hbm,
+    units_hbm,
+    scales_hbm,
     probs_hbm,
     band_ref,
     logit_ref,
     background_ref,
     direction_ref,
-    lat_piece,
     lon_piece,
     far_piece,
+    lat_piece,
     embed_ref,
     gain_ref,
     decode_gain_ref,
@@ -190,11 +187,8 @@
     outw_ref,
     hidden_ref,
     block_ref,
-    unit_q_ref,
-    unit_k_ref,
-    scale_q_ref,
-    scale_k_ref,
-    value_ref,
+    units_ref,
+    scales_ref,
     probs_ref,
     mixed_ref,
     sems_in,
@@ -226,9 +220,9 @@
         )
     ]
     fetched = []
-    for quad in range(quads):
+    for half in range(2):
         for third in range(3):
-            columns = pl.ds(third * width + quad * QUAD, QUAD)
+            columns = pl.ds(third * width + half * (width // 2), width // 2)
             fetched.append(fetch(qkv_hbm.at[:, columns], qkv_ref.at[:, columns]))
     last_needed = [
         fetch(*pair) for pair in ((outw_hbm, outw_ref), (decode_gain_hbm, decode_gain_ref), (decode_hbm, decode_ref))
@@ -278,19 +272,9 @@
         unit_tan = (scale * (raw_tan - unit * along)).astype(bf16)
         unit = unit.astype(bf16)
         value = packed[2].astype(bf16)
-        scale_q_ref[:, here] = scale[:CELLS]
-        scale_k_ref[:, here] = scale[CELLS:]
-        unit_q_ref[:, here] = unit[:CELLS]
-        unit_k_ref[:, here] = unit[CELLS:]
-        value_ref[:, here] = value[:CELLS]
-        for source, target in (
-            (scale_q_ref, scale_q_hbm),
-            (scale_k_ref, scale_k_hbm),
-            (unit_q_ref, unit_q_hbm),
-            (unit_k_ref, unit_k_hbm),
-            (value_ref, value_hbm),
-        ):
-            keep(source.at[:, here], target.at[:, here])
+        scales_ref[:, here] = scale
+        units_ref[: 2 * CELLS, here] = unit
+        units_ref[2 * CELLS :, here] = value[:CELLS]
         return unit, unit_tan, value
 
     def attend(quad, unit, unit_tan, value):
@@ -323,26 +307,23 @@
             columns = pl.ds(pair * 128, 128)
             mixed_ref[:CELLS, columns] = mixed.astype(bf16)
             mixed_ref[CELLS:, columns] = mixed_tan.astype(bf16)
-        pairs = pl.ds(quad * 2, 2)
-        keep(probs_ref.at[pairs], probs_hbm.at[pairs])
 
     for copy in fetched[0:3]:
         copy.wait()
     vals0 = project(0)
+    vals1 = project(1)
     for copy in fetched[3:6]:
         copy.wait()
-    vals1 = project(1)
+    vals2 = project(2)
+    vals3 = project(3)
     attend(0, *vals0)
-    for copy in fetched[6:9]:
-        copy.wait()
-    vals2 = project(2)
     attend(1, *vals1)
-    for copy in fetched[9:12]:
-        copy.wait()
-    vals3 = project(3)
     attend(2, *vals2)
     attend(3, *vals3)
 
+    keep(units_ref, units_hbm)
+    keep(scales_ref, scales_hbm)
+    keep(probs_ref, probs_hbm)
     for copy in last_needed:
         copy.wait()
     block = (hidden_ref[...].astype(f32) + product(mixed_ref[...], outw_ref[...], NN)).astype(bf16)
@@ -362,9 +343,9 @@
 def observe_kernel(
     direction_ref,
     own_piece,
-    lat_piece,
     lon_piece,
     far_piece,
+    lat_piece,
     arrived_ref,
     at_obs_out,
     adjoint_out,
@@ -420,20 +401,17 @@
 def adjoint_kernel(
     logit_ref,
     own_piece,
-    lat_piece,
     lon_piece,
     far_piece,
+    lat_piece,
     decode_gain_ref,
     decode_ref,
     block_ref,
     embed_hbm,
     gain_hbm,
     hidden_hbm,
-    unit_q_hbm,
-    unit_k_hbm,
-    scale_q_hbm,
-    scale_k_hbm,
-    value_hbm,
+    units_hbm,
+    scales_hbm,
     probs_hbm,
     qkv_hbm,
     outw_hbm,
@@ -444,11 +422,8 @@
     embed_ref,
     gain_ref,
     hidden_ref,
-    unit_q_ref,
-    unit_k_ref,
-    scale_q_ref,
-    scale_k_ref,
-    value_ref,
+    units_ref,
+    scales_ref,
     probs_ref,
     qkv_ref,
     outw_ref,
@@ -460,12 +435,9 @@
     fetched = []
     for source, target in (
         (outw_hbm, outw_ref),
-        (value_hbm, value_ref),
+        (units_hbm, units_ref),
         (probs_hbm, probs_ref),
-        (unit_q_hbm, unit_q_ref),
-        (unit_k_hbm, unit_k_ref),
-        (scale_q_hbm, scale_q_ref),
-        (scale_k_hbm, scale_k_ref),
+        (scales_hbm, scales_ref),
         (qkv_hbm, qkv_ref),
         (gain_hbm, gain_ref),
         (hidden_hbm, hidden_ref),
@@ -486,14 +458,14 @@
     first = lane < 64
     same_head = same_head_block()
     logits = logit_ref[...]
-    for copy in fetched[1:7]:
+    for copy in fetched[1:4]:
         copy.wait()
     for quad in range(quads):
         cotangents = []
         for side in range(2):
             pair = quad * 2 + side
             here = pl.ds(pair * 128, 128)
-            query, key, value = unit_q_ref[:, here], unit_k_ref[:, here], value_ref[:, here]
+            query, key, value = (units_ref[i * CELLS : (i + 1) * CELLS, here] for i in range(3))
             mixed_here = mixed_ct[:, pair * 128 : (pair + 1) * 128]
             probs = halves(probs_ref[pair])
             scores_ct = []
@@ -509,13 +481,13 @@
             cotangents.append(jnp.concatenate([query_ct, key_ct], axis=0))
         unit_ct = jnp.concatenate(cotangents, axis=1)
         here = pl.ds(quad * QUAD, QUAD)
-        units = jnp.concatenate([unit_q_ref[:, here], unit_k_ref[:, here]], axis=0).astype(f32)
+        units = units_ref[: 2 * CELLS, here].astype(f32)
         along = product((units * unit_ct).astype(bf16), same_head, NN)
-        rest = unit_ct - units * along
-        packed_ref[:, here] = (scale_q_ref[:, here] * rest[:CELLS]).astype(bf16)
-        packed_ref[:, pl.ds(width + quad * QUAD, QUAD)] = (scale_k_ref[:, here] * rest[CELLS:]).astype(bf16)
-
-    for copy in fetched[7:]:
+        raw_ct = (scales_ref[:, here] * (unit_ct - units * along)).astype(bf16)
+        packed_ref[:, here] = raw_ct[:CELLS]
+        packed_ref[:, pl.ds(width + quad * QUAD, QUAD)] = raw_ct[CELLS:]
+
+    for copy in fetched[4:]:
         copy.wait()
     unit, scale = normed_rows(hidden_ref[...].astype(f32))
     normed_ct = product(packed_ref[...], qkv_ref[...], NT).astype(bf16).astype(f32) * gain_ref[...]
@@ -525,13 +497,6 @@
     lon_out[...] = quadrant_of(state, 0, HALF_LON).astype(bf16)
     far_out[...] = quadrant_of(state, HALF_LAT, HALF_LON).astype(bf16)
     own_out[...] = quadrant_of(state, 0, 0).astype(bf16)
-
-
-def finish_kernel(adjoint_ref, own_piece, lat_piece, lon_piece, far_piece, out_ref):
-    pieces = [piece[...].astype(f32) for piece in (far_piece, lon_piece, lat_piece, own_piece)]
-    moved = quadrants(*pieces)
-    for i in range(WLAT):
-        out_ref[i] = adjoint_ref[i] + moved[i * WLON : (i + 1) * WLON]
 
 
 def shape(dims, dtype):
@@ -557,19 +522,24 @@
     width = embed_weight.shape[1]
     quarter = shape((QUARTER, background.shape[2]), bf16)
     wide = shape((CELLS, width), bf16)
-    wide_long = shape((CELLS, width), f32)
-    kept = [wide, wide, wide, wide, wide_long, wide_long, wide, shape((HEADS // 2, CELLS, 2 * CELLS), bf16)]
-    inputs = (last_band, logit_scale, background, direction, *strips, embed_weight, gain, decode_gain, decode_rows, qkv_weight, out_weight)
+    kept = [
+        wide,
+        wide,
+        shape((3 * CELLS, width), bf16),
+        shape((2 * CELLS, width), f32),
+        shape((HEADS // 2, CELLS, 2 * CELLS), bf16),
+    ]
+    inputs = (last_band, logit_scale, background, direction, strips[1], strips[2], strips[0], embed_weight, gain, decode_gain, decode_rows, qkv_weight, out_weight)
     both = pltpu.VMEM((2 * CELLS, width), bf16)
     return pl.pallas_call(
         forward_kernel,
         out_shape=[quarter] * 4 + kept,
         in_specs=[ANY] * 13,
-        out_specs=[VMEM] * 4 + [ANY] * 8,
+        out_specs=[VMEM] * 4 + [ANY] * 5,
         scratch_shapes=[pltpu.VMEM(item.shape, item.dtype) for item in inputs]
         + [both, both]
         + [pltpu.VMEM(item.shape, item.dtype) for item in kept[2:]]
-        + [both, pltpu.SemaphoreType.DMA((12 + 3 * (width // QUAD),)), pltpu.SemaphoreType.DMA((2 + 6 * (width // QUAD),))],
+        + [both, pltpu.SemaphoreType.DMA((18,)), pltpu.SemaphoreType.DMA((5,))],
         cost_estimate=pl.CostEstimate(flops=2_500_000_000, bytes_accessed=10_000_000, transcendentals=300_000),
         name="forward",
     )(*inputs)
@@ -653,24 +623,27 @@
     lat_piece, lon_piece, far_piece = exchanged(lat_piece, lon_piece, far_piece, 1)
 
     at_obs, adjoint_field, own_piece, lat_piece, lon_piece, far_piece = run_observe(
-        direction, (own_piece, lat_piece, lon_piece, far_piece), arrived
+        direction, (own_piece, lon_piece, far_piece, lat_piece), arrived
     )
     lat_piece, lon_piece, far_piece = exchanged(lat_piece, lon_piece, far_piece, -1)
     returned = lax.all_to_all(at_obs, ("lon", "lat"), split_axis=0, concat_axis=0, tiled=True)
 
     own_piece, lat_piece, lon_piece, far_piece = run_adjoint(
-        logit_scale, (own_piece, lat_piece, lon_piece, far_piece), embed_weight, gain, decode_gain, decode_rows, kept, qkv_weight, out_weight
+        logit_scale, (own_piece, lon_piece, far_piece, lat_piece), embed_weight, gain, decode_gain, decode_rows, kept, qkv_weight, out_weight
     )
     lat_piece, lon_piece, far_piece, returned = lax.optimization_barrier((lat_piece, lon_piece, far_piece, returned))
     lat_piece, lon_piece, far_piece = exchanged(lat_piece, lon_piece, far_piece, 1)
 
-    hvp = pl.pallas_call(
-        finish_kernel,
-        out_shape=shape(background.shape, f32),
-        in_specs=[VMEM] * 5,
-        out_specs=VMEM,
-        name="finish",
-    )(adjoint_field, own_piece, lat_piece, lon_piece, far_piece)
+    hvp = adjoint_field
+    for piece, row, col in (
+        (lon_piece, HALF_LAT, 0),
+        (far_piece, 0, 0),
+        (lat_piece, 0, HALF_LON),
+        (own_piece, HALF_LAT, HALF_LON),
+    ):
+        piece = piece.reshape(HALF_LAT, HALF_LON, var_count).astype(f32)
+        around = ((row, HALF_LAT - row, 0), (col, HALF_LON - col, 0), (0, 0, 0))
+        hvp = hvp + lax.pad(piece, jnp.zeros((), f32), around)
     obs_increment = pl.pallas_call(
         unpack_kernel,
         out_shape=shape((1, obs_rows), f32),

time: 75.1 us -> 72.6 us (0.967)
  waiting for transfers between devices: 13.2 us -> 10.5 us
  Pallas kernels: 26.7 us -> 24.8 us
  other arithmetic: 0 us -> 1.34 us
  starting transfers between devices: 31.7 us -> 33 us
    ppermute x4, starting transfers between devices: 4.83 us -> 0.09 us  [exchanged(): lax.ppermute(lat_piece, 'lat', [(i, (i + steps) % lat_count) for i in ran...]
    ppermute x4, starting transfers between devices: 6.62 us -> 9.29 us  [exchanged(): far_piece = lax.ppermute(far_piece, ('lon', 'lat'), pairs)]
    ppermute x4, waiting for transfers between devices: 10.3 us -> 7.97 us  [exchanged(): lax.ppermute(lon_piece, 'lon', [(i, (i + steps) % lon_count) for i in ran...]
    ppermute x4, starting transfers between devices: 12.3 us -> 14.1 us  [exchanged(): lax.ppermute(lon_piece, 'lon', [(i, (i + steps) % lon_count) for i in ran...]
    pallas_call x1 -> x0, Pallas kernels: 1.51 us -> none  [per_device(): pl.pallas_call(finish_kernel, out_shape=shape(background.shape, f32), in_...]
    add x0 -> x1, other arithmetic: none -> 1.34 us  [per_device(): hvp = hvp + lax.pad(piece, jnp.zeros((), f32), around)]
    all_to_all x1, starting transfers between devices: 3.56 us -> 4.64 us  [per_device(): lax.all_to_all(outgoing, ('lon', 'lat'), split_axis=0, concat_axis=0, til...]
    unnamed x28 -> x24, local copies, waits for them, and re-layouts: 2.42 us -> 1.82 us
where the time goes in v3:
time: 72.6 us; the launch traced here: 72.2 us
  starting transfers between devices  33 us (45%)
  Pallas kernels  24.8 us (34%)
  waiting for transfers between devices  10.5 us (14%)
  local copies, waits for them, and re-layouts  1.82 us (3%)
  other arithmetic  1.34 us (2%)
  between operations  0.82 us (1%)
    ppermute x4, starting transfers between devices, exchanged(): lax.ppermute(lon_piece, 'lon', [(i, (i + steps) % lon_count) for i in ran...  14.1 us
    pallas_call x1, Pallas kernels, run_adjoint(): pl.pallas_call(adjoint_kernel, out_shape=[shape(pieces[0].shape, bf16)] *...  9.37 us
    ppermute x4, starting transfers between devices, exchanged(): far_piece = lax.ppermute(far_piece, ('lon', 'lat'), pairs)  9.29 us
    pallas_call x1, Pallas kernels, run_forward(): pl.pallas_call(forward_kernel, out_shape=[quarter] * 4 + kept, in_specs=[...  9.18 us
    ppermute x4, waiting for transfers between devices, exchanged(): lax.ppermute(lon_piece, 'lon', [(i, (i + steps) % lon_count) for i in ran...  7.97 us
    all_to_all x1, starting transfers between devices, per_device(): lax.all_to_all(at_obs, ('lon', 'lat'), split_axis=0, concat_axis=0, tiled...  4.83 us
    all_to_all x1, starting transfers between devices, per_device(): lax.all_to_all(outgoing, ('lon', 'lat'), split_axis=0, concat_axis=0, til...  4.64 us
    ppermute x4, waiting for transfers between devices, exchanged(): far_piece = lax.ppermute(far_piece, ('lon', 'lat'), pairs)  2.53 us
  transfers between devices with their start and end apart: 14, of which 4 were waited for; matrix products, arithmetic and copies ran while one was open for 0% of the time, Pallas kernels for 28%

profile of v3, /device:TPU:1, one launch (start us, length us, event | category | flops | bytes accessed | tf_op | source)
XLA Modules:
  0.0 72.2 jit_solution(17240414512697229186)
XLA Ops:
  0.6 2.1 %prepare.1 = (bf16[64,69]{1,0:T(8,128)(2,1)}, bf16[64,69]{1,0:T(8,128)(2,1)}, bf16[64,69]{1,0:T(8,128)(2,1)}, f32[128,64]{1,0:T(8,128)}, f32[1,512]{1,0:T(1,128)}) custom-call(f32[8,16,69]{2,1,0:T(8,128)} %background_hbm.1, f32[8,16,69]{2,1,0:T(8,128)} %direction_ref.3, s32[1,512]{1,0:T(1,128)} %bitcast.28, s32[1,512]{1,0:T(1,128)} %bitcast.39, ...), custom_call_target="tpu_custom_call" | custom-call | tf_op jit(solution)/shard_map/prepare/pallas_call | solution.py:602
  2.7 9.5 %collective-permute-start = (bf16[64,69]{1,0:T(8,128)(2,1)}, bf16[64,69]{1,0:T(8,128)(2,1)S(1)}, u32[]{:S(2)}, u32[]{:S(2)}) collective-permute-start(bf16[64,69]{1,0:T(8,128)(2,1)} %get-tuple-element.30), channel_id=1, source_target_pairs={{0,124},{4,0},{8,4},{12,8},{16,12},{20,16},{24,20},{28,24},{32,28}... | collective-permute-start | bytes 26504 | tf_op jit(solution)/shard_map/ppermute | solution.py:509
  12.2 1.0 %collective-permute-start.1 = (bf16[64,69]{1,0:T(8,128)(2,1)}, bf16[64,69]{1,0:T(8,128)(2,1)S(1)}, u32[]{:S(2)}, u32[]{:S(2)}) collective-permute-start(bf16[64,69]{1,0:T(8,128)(2,1)} %get-tuple-element.31), channel_id=1, source_target_pairs={{0,127},{1,124},{2,125},{3,126},{4,3},{5,0},{6,1},{7,2},{8,7},{9,4... | collective-permute-start | bytes 26504 | tf_op jit(solution)/shard_map/ppermute | solution.py:515
  13.2 0.0 collective-permute-start.2
  13.2 4.6 %all-to-all-start = ((f32[128,1,64]{2,1,0:T(1,128)}), f32[128,1,64]{2,1,0:T(1,128)S(1)}, u32[]{:S(2)}, u32[]{:S(2)}) async-start(f32[128,1,64]{2,1,0:T(1,128)} %bitcast.26), calls=%async_computation | async-start | bytes 131072 | tf_op jit(solution)/shard_map/all_to_all | solution.py:618
  17.8 0.0 collective-permute-done.lon_hbm
  17.9 0.0 collective-permute-done.1.far_hbm
  17.9 0.0 collective-permute-done.2.lat_hbm
  17.9 0.5 copy-done.9
  18.5 0.0 copy-done.10
  18.5 0.0 copy-done.11
  18.5 9.2 %forward.1 = (bf16[32,69]{1,0:T(8,128)(2,1)}, bf16[32,69]{1,0:T(8,128)(2,1)}, bf16[32,69]{1,0:T(8,128)(2,1)}, bf16[32,69]{1,0:T(8,128)(2,1)}, bf16[128,1024]{1,0...) custom-call(f32[1,1]{1,0:T(1,128)} %bitcast.band_hbm, ...), custom_call_target="tpu_custom_call" | custom-call | flops 2500000000 | bytes 10000000 | tf_op jit(solution)/shard_map/forward/pallas_call | solution.py:534
  27.7 1.6 %collective-permute-start.3 = (bf16[32,69]{1,0:T(8,128)(2,1)}, bf16[32,69]{1,0:T(8,128)(2,1)S(1)}, u32[]{:S(2)}, u32[]{:S(2)}) collective-permute-start(bf16[32,69]{1,0:T(8,128)(2,1)} %get-tuple-element.34), channel_id=1, source_target_pairs={{0,4},{4,8},{8,12},{12,16},{16,20},{20,24},{24,28},{28,32},{32,36}... | collective-permute-start | bytes 13256 | tf_op jit(solution)/shard_map/ppermute | solution.py:509
  29.3 2.9 %collective-permute-start.4 = (bf16[32,69]{1,0:T(8,128)(2,1)}, bf16[32,69]{1,0:T(8,128)(2,1)S(1)}, u32[]{:S(2)}, u32[]{:S(2)}) collective-permute-start(bf16[32,69]{1,0:T(8,128)(2,1)} %get-tuple-element.35), channel_id=1, source_target_pairs={{0,5},{1,6},{2,7},{3,4},{4,9},{5,10},{6,11},{7,8},{8,13},{9,14},{1... | collective-permute-start | bytes 13256 | tf_op jit(solution)/shard_map/ppermute | solution.py:515
  32.2 0.0 collective-permute-start.5
  32.2 4.8 %collective-permute-done.3.lon_piece = bf16[32,69]{1,0:T(8,128)(2,1)S(1)} collective-permute-done((bf16[32,69]{1,0:T(8,128)(2,1)}, bf16[32,69]{1,0:T(8,128)(2,1)S(1)}, u32[]{:S(2)}, u32[]{:S(2)}) %collective-permute-start.3) | collective-permute-done | bytes 4448 | tf_op jit(solution)/shard_map/ppermute | solution.py:509
  37.0 1.3 %collective-permute-done.4.far_piece = bf16[32,69]{1,0:T(8,128)(2,1)S(1)} collective-permute-done((bf16[32,69]{1,0:T(8,128)(2,1)}, bf16[32,69]{1,0:T(8,128)(2,1)S(1)}, u32[]{:S(2)}, u32[]{:S(2)}) %collective-permute-start.4) | collective-permute-done | bytes 4448 | tf_op jit(solution)/shard_map/ppermute | solution.py:515
  38.3 0.0 collective-permute-done.5.lat_piece
  38.3 0.0 all-to-all-done
  38.3 0.0 copy-start
  38.3 0.0 copy-done.6
  38.3 0.6 copy-done.7
  38.9 0.0 copy-done.8
  38.9 0.0 copy-done
  38.9 2.5 %observe.1 = (f32[128,8]{1,0:T(8,128)}, f32[8,16,69]{2,1,0:T(8,128)}, bf16[32,69]{1,0:T(8,128)(2,1)}, bf16[32,69]{1,0:T(8,128)(2,1)}, bf16[32,69]{1,0:T(8,128)(2,1)}, /*index=5*/bf16[32,69]{1,0:T(8,128)(2,1)}) custom-call(f32[8,16,69]{2,1,0:T(8,128)} %direction_ref.3, bf16[32,69]{1,0:T(8,128)(2,1)} %get-tuple-element.33.own_piece, bf16[32,69]{1,0:T(8,128)(2,1)} %copy-done.6, ...), custom_call_target="tpu_custom_call" | custom-call | tf_op jit(solution)/shard_map/observe/pallas_call | solution.py:551
  41.4 1.5 %collective-permute-start.6 = (bf16[32,69]{1,0:T(8,128)(2,1)}, bf16[32,69]{1,0:T(8,128)(2,1)S(1)}, u32[]{:S(2)}, u32[]{:S(2)}) collective-permute-start(bf16[32,69]{1,0:T(8,128)(2,1)} %get-tuple-element.40), channel_id=1, source_target_pairs={{0,124},{4,0},{8,4},{12,8},{16,12},{20,16},{24,20},{28,24},{32,28}... | collective-permute-start | bytes 13256 | tf_op jit(solution)/shard_map/ppermute | solution.py:509
  42.9 2.5 %collective-permute-start.7 = (bf16[32,69]{1,0:T(8,128)(2,1)}, bf16[32,69]{1,0:T(8,128)(2,1)S(1)}, u32[]{:S(2)}, u32[]{:S(2)}) collective-permute-start(bf16[32,69]{1,0:T(8,128)(2,1)} %get-tuple-element.41), channel_id=1, source_target_pairs={{0,127},{1,124},{2,125},{3,126},{4,3},{5,0},{6,1},{7,2},{8,7},{9,4... | collective-permute-start | bytes 13256 | tf_op jit(solution)/shard_map/ppermute | solution.py:515
  45.4 0.0 collective-permute-start.8
  45.4 4.8 %all-to-all-start.1 = ((f32[128,1,8]{2,1,0:T(1,128)}), f32[128,1,8]{2,1,0:T(1,128)S(1)}, u32[]{:S(2)}, u32[]{:S(2)}) async-start(f32[128,1,8]{2,1,0:T(1,128)} %bitcast.27), calls=%async_computation.1 | async-start | bytes 131072 | tf_op jit(solution)/shard_map/all_to_all | solution.py:629
  50.2 0.0 collective-permute-done.6.lon_piece
  50.2 0.0 copy-start.3
  50.3 0.0 collective-permute-done.7.far_piece
  50.3 0.0 copy-start.4
  50.3 0.0 collective-permute-done.8.lat_piece
  50.3 0.5 copy-done.3
  50.9 0.0 copy-done.4
  50.9 0.0 copy-done.5
  50.9 9.4 %adjoint.1 = (bf16[32,69]{1,0:T(8,128)(2,1)}, bf16[32,69]{1,0:T(8,128)(2,1)}, bf16[32,69]{1,0:T(8,128)(2,1)}, bf16[32,69]{1,0:T(8,128)(2,1)}) custom-call(f32[1,16]{1,0:T(1,128)} %bitcast.43, bf16[32,69]{1,0:T(8,128)(2,1)} %get-tuple-element.39.own_piece, bf16[32,69]{1,0:T(8,128)(2,1)} %copy-done.3, bf16[32,69]{1,0:T(8,128)(2,1)} %copy-done.4, ...), custom_call_target="tpu_custom_call" | custom-call | flops 1500000000 | bytes 10000000 | tf_op jit(solution)/shard_map/adjoint/pallas_call | solution.py:564
  60.3 0.0 all-to-all-done.1
  60.3 0.0 copy-start.1
  60.3 1.6 %collective-permute-start.9 = (bf16[32,69]{1,0:T(8,128)(2,1)}, bf16[32,69]{1,0:T(8,128)(2,1)S(1)}, u32[]{:S(2)}, u32[]{:S(2)}) collective-permute-start(bf16[32,69]{1,0:T(8,128)(2,1)} %get-tuple-element.52), channel_id=1, source_target_pairs={{0,4},{4,8},{8,12},{12,16},{16,20},{20,24},{24,28},{28,32},{32,36}... | collective-permute-start | bytes 13256 | tf_op jit(solution)/shard_map/ppermute | solution.py:509
  61.9 2.9 %collective-permute-start.10 = (bf16[32,69]{1,0:T(8,128)(2,1)}, bf16[32,69]{1,0:T(8,128)(2,1)S(1)}, u32[]{:S(2)}, u32[]{:S(2)}) collective-permute-start(bf16[32,69]{1,0:T(8,128)(2,1)} %get-tuple-element.53), channel_id=1, source_target_pairs={{0,5},{1,6},{2,7},{3,4},{4,9},{5,10},{6,11},{7,8},{8,13},{9,14},{1... | collective-permute-start | bytes 13256 | tf_op jit(solution)/shard_map/ppermute | solution.py:515
  64.8 0.0 collective-permute-start.11
  64.8 1.7 %unpack.1 = f32[1,512]{1,0:T(1,128)} custom-call(s32[1,512]{1,0:T(1,128)} %bitcast.29, f32[1,512]{1,0:T(1,128)} %get-tuple-element.56.slots_ref, f32[128,8]{1,0:T(8,128)} %bitcast.23), custom_call_target="tpu_custom_call" | custom-call | tf_op jit(solution)/shard_map/unpack/pallas_call | solution.py:647
  66.5 3.2 %collective-permute-done.9 = bf16[32,69]{1,0:T(8,128)(2,1)S(1)} collective-permute-done((bf16[32,69]{1,0:T(8,128)(2,1)}, bf16[32,69]{1,0:T(8,128)(2,1)S(1)}, u32[]{:S(2)}, u32[]{:S(2)}) %collective-permute-start.9) | collective-permute-done | bytes 4448 | tf_op jit(solution)/shard_map/ppermute | solution.py:509
  69.6 1.3 %collective-permute-done.10 = bf16[32,69]{1,0:T(8,128)(2,1)S(1)} collective-permute-done((bf16[32,69]{1,0:T(8,128)(2,1)}, bf16[32,69]{1,0:T(8,128)(2,1)S(1)}, u32[]{:S(2)}, u32[]{:S(2)}) %collective-permute-start.10) | collective-permute-done | bytes 4448 | tf_op jit(solution)/shard_map/ppermute | solution.py:515
  70.9 0.0 collective-permute-done.11
  70.9 1.3 %convert_add_fusion = f32[8,16,69]{2,1,0:T(8,128)} fusion(f32[8,16,69]{2,1,0:T(8,128)S(1)} %copy-done.2, bf16[4,8,69]{2,1,0:T(8,128)(2,1)} %bitcast.31, bf16[4,8,69]{2,1,0:T(8,128)(2,1)S(1)} %bitcast.34, bf16[4,8,69]{2,1,0:T(8,128)(2,1)S(1)} %bitcast.33, bf16[4,8,69]{2,1,0:T(8,128)(2,1)S(1)} %bitcast.32), kind=kLoop, calls=%fused_computation | loop fusion | flops 70656 | bytes 88320 | tf_op jit(solution)/shard_map/add | solution.py:646
  (10 shorter events, 0.0 us)
Async XLA Ops:
  2.7 15.1 %collective-permute-start = (bf16[64,69]{1,0:T(8,128)(2,1)}, bf16[64,69]{1,0:T(8,128)(2,1)S(1)}, u32[]{:S(2)}, u32[]{:S(2)}) collective-permute-start(bf16[64,69]{1,0:T(8,128)(2,1)} %get-tuple-element.30), channel_id=1, source_target_pairs={{0,124},{4,0},{8,4},{12,8},{16,12},{20,16},{24,20},{28,24},{32,28}... | collective-permute-start | bytes 26504 | tf_op jit(solution)/shard_map/ppermute | solution.py:509
  12.2 5.6 %collective-permute-start.1 = (bf16[64,69]{1,0:T(8,128)(2,1)}, bf16[64,69]{1,0:T(8,128)(2,1)S(1)}, u32[]{:S(2)}, u32[]{:S(2)}) collective-permute-start(bf16[64,69]{1,0:T(8,128)(2,1)} %get-tuple-element.31), channel_id=1, source_target_pairs={{0,127},{1,124},{2,125},{3,126},{4,3},{5,0},{6,1},{7,2},{8,7},{9,4... | collective-permute-start | bytes 26504 | tf_op jit(solution)/shard_map/ppermute | solution.py:515
  13.2 4.7 %collective-permute-start.2 = (bf16[64,69]{1,0:T(8,128)(2,1)}, bf16[64,69]{1,0:T(8,128)(2,1)S(1)}, u32[]{:S(2)}, u32[]{:S(2)}) collective-permute-start(bf16[64,69]{1,0:T(8,128)(2,1)} %get-tuple-element.32), channel_id=1, source_target_pairs={{0,3},{1,0},{2,1},{3,2},{4,7},{5,4},{6,5},{7,6},{8,11},{9,8},{10,9... | collective-permute-start | bytes 26504 | tf_op jit(solution)/shard_map/ppermute | solution.py:508
  13.2 25.1 %all-to-all-start = ((f32[128,1,64]{2,1,0:T(1,128)}), f32[128,1,64]{2,1,0:T(1,128)S(1)}, u32[]{:S(2)}, u32[]{:S(2)}) async-start(f32[128,1,64]{2,1,0:T(1,128)} %bitcast.26), calls=%async_computation | async-start | bytes 131072 | tf_op jit(solution)/shard_map/all_to_all | solution.py:618
  17.9 0.6 copy-start.9
  17.9 0.6 copy-start.10
  17.9 0.6 copy-start.11
  27.7 9.3 %collective-permute-start.3 = (bf16[32,69]{1,0:T(8,128)(2,1)}, bf16[32,69]{1,0:T(8,128)(2,1)S(1)}, u32[]{:S(2)}, u32[]{:S(2)}) collective-permute-start(bf16[32,69]{1,0:T(8,128)(2,1)} %get-tuple-element.34), channel_id=1, source_target_pairs={{0,4},{4,8},{8,12},{12,16},{16,20},{20,24},{24,28},{28,32},{32,36}... | collective-permute-start | bytes 13256 | tf_op jit(solution)/shard_map/ppermute | solution.py:509
  29.3 9.0 %collective-permute-start.4 = (bf16[32,69]{1,0:T(8,128)(2,1)}, bf16[32,69]{1,0:T(8,128)(2,1)S(1)}, u32[]{:S(2)}, u32[]{:S(2)}) collective-permute-start(bf16[32,69]{1,0:T(8,128)(2,1)} %get-tuple-element.35), channel_id=1, source_target_pairs={{0,5},{1,6},{2,7},{3,4},{4,9},{5,10},{6,11},{7,8},{8,13},{9,14},{1... | collective-permute-start | bytes 13256 | tf_op jit(solution)/shard_map/ppermute | solution.py:515
  32.2 6.1 %collective-permute-start.5 = (bf16[32,69]{1,0:T(8,128)(2,1)}, bf16[32,69]{1,0:T(8,128)(2,1)S(1)}, u32[]{:S(2)}, u32[]{:S(2)}) collective-permute-start(bf16[32,69]{1,0:T(8,128)(2,1)} %get-tuple-element.36), channel_id=1, source_target_pairs={{0,1},{1,2},{2,3},{3,0},{4,5},{5,6},{6,7},{7,4},{8,9},{9,10},{10,1... | collective-permute-start | bytes 13256 | tf_op jit(solution)/shard_map/ppermute | solution.py:508
  37.0 1.3 %copy-start.6 = (bf16[32,69]{1,0:T(8,128)(2,1)}, bf16[32,69]{1,0:T(8,128)(2,1)S(1)}, u32[]{:S(2)}) copy-start(bf16[32,69]{1,0:T(8,128)(2,1)S(1)} %collective-permute-done.3.lon_piece) | copy-start | bytes 13252
  38.3 0.6 copy-start.7
  38.3 0.6 copy-start.8
  38.3 0.6 copy-start
  41.4 29.5 %copy-start.2 = (f32[8,16,69]{2,1,0:T(8,128)S(1)}, f32[8,16,69]{2,1,0:T(8,128)}, u32[]{:S(2)}) copy-start(f32[8,16,69]{2,1,0:T(8,128)} %get-tuple-element.38) | copy-start | bytes 105988
  41.4 8.9 %collective-permute-start.6 = (bf16[32,69]{1,0:T(8,128)(2,1)}, bf16[32,69]{1,0:T(8,128)(2,1)S(1)}, u32[]{:S(2)}, u32[]{:S(2)}) collective-permute-start(bf16[32,69]{1,0:T(8,128)(2,1)} %get-tuple-element.40), channel_id=1, source_target_pairs={{0,124},{4,0},{8,4},{12,8},{16,12},{20,16},{24,20},{28,24},{32,28}... | collective-permute-start | bytes 13256 | tf_op jit(solution)/shard_map/ppermute | solution.py:509
  42.9 7.4 %collective-permute-start.7 = (bf16[32,69]{1,0:T(8,128)(2,1)}, bf16[32,69]{1,0:T(8,128)(2,1)S(1)}, u32[]{:S(2)}, u32[]{:S(2)}) collective-permute-start(bf16[32,69]{1,0:T(8,128)(2,1)} %get-tuple-element.41), channel_id=1, source_target_pairs={{0,127},{1,124},{2,125},{3,126},{4,3},{5,0},{6,1},{7,2},{8,7},{9,4... | collective-permute-start | bytes 13256 | tf_op jit(solution)/shard_map/ppermute | solution.py:515
  45.4 4.9 %collective-permute-start.8 = (bf16[32,69]{1,0:T(8,128)(2,1)}, bf16[32,69]{1,0:T(8,128)(2,1)S(1)}, u32[]{:S(2)}, u32[]{:S(2)}) collective-permute-start(bf16[32,69]{1,0:T(8,128)(2,1)} %get-tuple-element.42), channel_id=1, source_target_pairs={{0,3},{1,0},{2,1},{3,2},{4,7},{5,4},{6,5},{7,6},{8,11},{9,8},{10,9... | collective-permute-start | bytes 13256 | tf_op jit(solution)/shard_map/ppermute | solution.py:508
  45.4 14.9 %all-to-all-start.1 = ((f32[128,1,8]{2,1,0:T(1,128)}), f32[128,1,8]{2,1,0:T(1,128)S(1)}, u32[]{:S(2)}, u32[]{:S(2)}) async-start(f32[128,1,8]{2,1,0:T(1,128)} %bitcast.27), calls=%async_computation.1 | async-start | bytes 131072 | tf_op jit(solution)/shard_map/all_to_all | solution.py:629
  50.2 0.6 copy-start.3
  50.3 0.6 copy-start.4
  50.3 0.6 copy-start.5
  60.3 4.5 %copy-start.1 = (f32[128,1,8]{2,1,0:T(1,128)}, f32[128,1,8]{2,1,0:T(1,128)S(1)}, u32[]{:S(2)}) copy-start(f32[128,1,8]{2,1,0:T(1,128)S(1)} %all-to-all-done.1) | copy-start | bytes 12292
  60.3 9.3 %collective-permute-start.9 = (bf16[32,69]{1,0:T(8,128)(2,1)}, bf16[32,69]{1,0:T(8,128)(2,1)S(1)}, u32[]{:S(2)}, u32[]{:S(2)}) collective-permute-start(bf16[32,69]{1,0:T(8,128)(2,1)} %get-tuple-element.52), channel_id=1, source_target_pairs={{0,4},{4,8},{8,12},{12,16},{16,20},{20,24},{24,28},{28,32},{32,36}... | collective-permute-start | bytes 13256 | tf_op jit(solution)/shard_map/ppermute | solution.py:509
  61.9 9.0 %collective-permute-start.10 = (bf16[32,69]{1,0:T(8,128)(2,1)}, bf16[32,69]{1,0:T(8,128)(2,1)S(1)}, u32[]{:S(2)}, u32[]{:S(2)}) collective-permute-start(bf16[32,69]{1,0:T(8,128)(2,1)} %get-tuple-element.53), channel_id=1, source_target_pairs={{0,5},{1,6},{2,7},{3,4},{4,9},{5,10},{6,11},{7,8},{8,13},{9,14},{1... | collective-permute-start | bytes 13256 | tf_op jit(solution)/shard_map/ppermute | solution.py:515
  64.8 6.1 %collective-permute-start.11 = (bf16[32,69]{1,0:T(8,128)(2,1)}, bf16[32,69]{1,0:T(8,128)(2,1)S(1)}, u32[]{:S(2)}, u32[]{:S(2)}) collective-permute-start(bf16[32,69]{1,0:T(8,128)(2,1)} %get-tuple-element.54), channel_id=1, source_target_pairs={{0,1},{1,2},{2,3},{3,0},{4,5},{5,6},{6,7},{7,4},{8,9},{9,10},{10,1... | collective-permute-start | bytes 13256 | tf_op jit(solution)/shard_map/ppermute | solution.py:508

commit v4 on v3

--- a/solution.py
+++ b/solution.py
@@ -13,7 +13,7 @@
 HALF_LON = WLON // 2
 QUARTER = HALF_LAT * HALF_LON
 SLOTS = 8
-PIECES = 3
+PIECES = 2
 QUAD = 256
 
 eps_norm = 1e-05
@@ -399,67 +399,91 @@
 
 
 def adjoint_kernel(
-    logit_ref,
+    own_hbm,
+    lon_hbm,
+    far_hbm,
+    lat_hbm,
+    block_hbm,
+    decode_hbm,
+    decode_gain_hbm,
+    logit_hbm,
+    outw_hbm,
+    units_hbm,
+    probs_hbm,
+    scales_hbm,
+    hidden_hbm,
+    gain_hbm,
+    embed_hbm,
+    qkv_hbm,
+    own_out,
+    lat_out,
+    lon_out,
+    far_out,
     own_piece,
     lon_piece,
     far_piece,
     lat_piece,
+    block_ref,
+    decode_ref,
     decode_gain_ref,
-    decode_ref,
-    block_ref,
-    embed_hbm,
-    gain_hbm,
-    hidden_hbm,
-    units_hbm,
-    scales_hbm,
-    probs_hbm,
-    qkv_hbm,
-    outw_hbm,
-    own_out,
-    lat_out,
-    lon_out,
-    far_out,
+    logit_ref,
+    outw_ref,
+    units_ref,
+    probs_ref,
+    scales_ref,
+    hidden_ref,
+    gain_ref,
     embed_ref,
-    gain_ref,
-    hidden_ref,
-    units_ref,
-    scales_ref,
-    probs_ref,
     qkv_ref,
-    outw_ref,
     packed_ref,
     sems,
 ):
     width = embed_ref.shape[1]
     quads = width // QUAD
     fetched = []
+
+    def fetch(source, target):
+        copy = pltpu.make_async_copy(source, target, sems.at[len(fetched)])
+        copy.start()
+        fetched.append(copy)
+
     for source, target in (
+        (own_hbm, own_piece),
+        (lon_hbm, lon_piece),
+        (far_hbm, far_piece),
+        (lat_hbm, lat_piece),
+        (block_hbm, block_ref),
+        (decode_hbm, decode_ref),
+        (decode_gain_hbm, decode_gain_ref),
+        (logit_hbm, logit_ref),
         (outw_hbm, outw_ref),
         (units_hbm, units_ref),
         (probs_hbm, probs_ref),
         (scales_hbm, scales_ref),
+        (hidden_hbm, hidden_ref),
+        (gain_hbm, gain_ref),
+        (embed_hbm, embed_ref),
         (qkv_hbm, qkv_ref),
-        (gain_hbm, gain_ref),
-        (hidden_hbm, hidden_ref),
-        (embed_hbm, embed_ref),
     ):
-        copy = pltpu.make_async_copy(source, target, sems.at[len(fetched)])
-        copy.start()
-        fetched.append(copy)
-
+        fetch(source, target)
+
+    def wait(start, stop):
+        for copy in fetched[start:stop]:
+            copy.wait()
+
+    wait(0, 8)
     change = quadrants(*[piece[...].astype(f32) for piece in (own_piece, lat_piece, lon_piece, far_piece)])
     unit, scale = normed_rows(block_ref[...].astype(f32))
     normed_ct = product(change.astype(bf16), decode_ref[...], NN).astype(bf16).astype(f32) * decode_gain_ref[...]
     block_ct = norm_tangent(unit, scale, normed_ct).astype(bf16)
-    fetched[0].wait()
+    wait(8, 9)
     mixed_ct = product(block_ct, outw_ref[...], NT).astype(bf16)
 
     lane = lax.broadcasted_iota(jnp.int32, (1, 128), 1)
     first = lane < 64
     same_head = same_head_block()
     logits = logit_ref[...]
-    for copy in fetched[1:4]:
-        copy.wait()
+    wait(9, 15)
     for quad in range(quads):
         cotangents = []
         for side in range(2):
@@ -487,9 +511,8 @@
         packed_ref[:, here] = raw_ct[:CELLS]
         packed_ref[:, pl.ds(width + quad * QUAD, QUAD)] = raw_ct[CELLS:]
 
-    for copy in fetched[4:]:
-        copy.wait()
     unit, scale = normed_rows(hidden_ref[...].astype(f32))
+    wait(15, 16)
     normed_ct = product(packed_ref[...], qkv_ref[...], NT).astype(bf16).astype(f32) * gain_ref[...]
     hidden_ct = (norm_tangent(unit, scale, normed_ct) + block_ct.astype(f32)).astype(bf16)
     state = product(hidden_ct, embed_ref[...], NT)
@@ -558,19 +581,20 @@
 
 
 def run_adjoint(logit_scale, pieces, embed_weight, gain, decode_gain, decode_rows, kept, qkv_weight, out_weight):
-    hidden, block, *attention = kept
+    hidden, block, units, scales, probs = kept
     width = embed_weight.shape[1]
-    late = (embed_weight, gain, hidden, *attention, qkv_weight, out_weight)
+    inputs = (*pieces, block, decode_rows, decode_gain, logit_scale, out_weight, units, probs, scales)
+    inputs = (*inputs, hidden, gain, embed_weight, qkv_weight)
     return pl.pallas_call(
         adjoint_kernel,
         out_shape=[shape(pieces[0].shape, bf16)] * 4,
-        in_specs=[VMEM] * 8 + [ANY] * len(late),
+        in_specs=[ANY] * len(inputs),
         out_specs=[VMEM] * 4,
-        scratch_shapes=[pltpu.VMEM(item.shape, item.dtype) for item in late]
-        + [pltpu.VMEM((CELLS, 3 * width), bf16), pltpu.SemaphoreType.DMA((len(late),))],
+        scratch_shapes=[pltpu.VMEM(item.shape, item.dtype) for item in inputs]
+        + [pltpu.VMEM((CELLS, 3 * width), bf16), pltpu.SemaphoreType.DMA((len(inputs),))],
         cost_estimate=pl.CostEstimate(flops=1_500_000_000, bytes_accessed=10_000_000, transcendentals=300_000),
         name="adjoint",
-    )(logit_scale, *pieces, decode_gain, decode_rows, block, *late)
+    )(*inputs)
 
 
 def per_device(

time: 72.6 us -> 71.8 us (0.989)
  Pallas kernels: 24.8 us -> 24 us
    pallas_call x1, Pallas kernels: 9.37 us -> 8.62 us  [run_adjoint(): pl.pallas_call(adjoint_kernel, out_shape=[shape(pieces[0].shape, bf16)] *...]
  transfers between devices with their start and end apart: 14 -> 14, of which waited for: 4 -> 5; matrix products, arithmetic and copies ran while one was open for 0% -> 0% of each run, Pallas kernels for 28% -> 27%
where the time goes in v4:
time: 71.8 us; the launch traced here: 71.4 us
  starting transfers between devices  32.7 us (46%)
  Pallas kernels  24 us (33%)
  waiting for transfers between devices  10.8 us (15%)
  local copies, waits for them, and re-layouts  1.81 us (3%)
  other arithmetic  1.34 us (2%)
  between operations  0.8 us (1%)
    ppermute x4, starting transfers between devices, exchanged(): lax.ppermute(lon_piece, 'lon', [(i, (i + steps) % lon_count) for i in ran...  13.9 us
    ppermute x4, starting transfers between devices, exchanged(): far_piece = lax.ppermute(far_piece, ('lon', 'lat'), pairs)  9.29 us
    pallas_call x1, Pallas kernels, run_forward(): pl.pallas_call(forward_kernel, out_shape=[quarter] * 4 + kept, in_specs=[...  9.18 us
    pallas_call x1, Pallas kernels, run_adjoint(): pl.pallas_call(adjoint_kernel, out_shape=[shape(pieces[0].shape, bf16)] *...  8.62 us
    ppermute x4, waiting for transfers between devices, exchanged(): lax.ppermute(lon_piece, 'lon', [(i, (i + steps) % lon_count) for i in ran...  7.99 us
    all_to_all x1, starting transfers between devices, per_device(): lax.all_to_all(at_obs, ('lon', 'lat'), split_axis=0, concat_axis=0, tiled...  4.83 us
    all_to_all x1, starting transfers between devices, per_device(): lax.all_to_all(outgoing, ('lon', 'lat'), split_axis=0, concat_axis=0, til...  4.64 us
    ppermute x4, waiting for transfers between devices, exchanged(): far_piece = lax.ppermute(far_piece, ('lon', 'lat'), pairs)  2.53 us
  transfers between devices with their start and end apart: 14, of which 5 were waited for; matrix products, arithmetic and copies ran while one was open for 0% of the time, Pallas kernels for 27%

profile of v4, /device:TPU:1, one launch (start us, length us, event | category | flops | bytes accessed | tf_op | source)
XLA Modules:
  0.0 71.4 jit_solution(3882813102396762236)
XLA Ops:
  0.6 2.0 %prepare.1 = (bf16[64,69]{1,0:T(8,128)(2,1)}, bf16[64,69]{1,0:T(8,128)(2,1)}, bf16[64,69]{1,0:T(8,128)(2,1)}, f32[128,64]{1,0:T(8,128)}, f32[1,512]{1,0:T(1,128)}) custom-call(f32[8,16,69]{2,1,0:T(8,128)} %background_hbm.1, f32[8,16,69]{2,1,0:T(8,128)} %direction_ref.3, s32[1,512]{1,0:T(1,128)} %bitcast.28, s32[1,512]{1,0:T(1,128)} %bitcast.39, ...), custom_call_target="tpu_custom_call" | custom-call | tf_op jit(solution)/shard_map/prepare/pallas_call | solution.py:626
  2.7 9.5 %collective-permute-start = (bf16[64,69]{1,0:T(8,128)(2,1)}, bf16[64,69]{1,0:T(8,128)(2,1)S(1)}, u32[]{:S(2)}, u32[]{:S(2)}) collective-permute-start(bf16[64,69]{1,0:T(8,128)(2,1)} %get-tuple-element.30), channel_id=1, source_target_pairs={{0,124},{4,0},{8,4},{12,8},{16,12},{20,16},{24,20},{28,24},{32,28}... | collective-permute-start | bytes 26504 | tf_op jit(solution)/shard_map/ppermute | solution.py:532
  12.2 1.0 %collective-permute-start.1 = (bf16[64,69]{1,0:T(8,128)(2,1)}, bf16[64,69]{1,0:T(8,128)(2,1)S(1)}, u32[]{:S(2)}, u32[]{:S(2)}) collective-permute-start(bf16[64,69]{1,0:T(8,128)(2,1)} %get-tuple-element.31), channel_id=1, source_target_pairs={{0,127},{1,124},{2,125},{3,126},{4,3},{5,0},{6,1},{7,2},{8,7},{9,4... | collective-permute-start | bytes 26504 | tf_op jit(solution)/shard_map/ppermute | solution.py:538
  13.1 0.0 collective-permute-start.2
  13.1 4.6 %all-to-all-start = ((f32[128,1,64]{2,1,0:T(1,128)}), f32[128,1,64]{2,1,0:T(1,128)S(1)}, u32[]{:S(2)}, u32[]{:S(2)}) async-start(f32[128,1,64]{2,1,0:T(1,128)} %bitcast.26), calls=%async_computation | async-start | bytes 131072 | tf_op jit(solution)/shard_map/all_to_all | solution.py:642
  17.8 0.0 collective-permute-done.lon_hbm
  17.8 0.0 copy-start.9
  17.8 0.0 collective-permute-done.1.far_hbm
  17.8 0.0 collective-permute-done.2.lat_hbm
  17.8 0.0 copy-start.11
  17.9 0.5 copy-done.9
  18.4 0.0 copy-done.10
  18.4 0.0 copy-done.11
  18.4 9.2 %forward.1 = (bf16[32,69]{1,0:T(8,128)(2,1)}, bf16[32,69]{1,0:T(8,128)(2,1)}, bf16[32,69]{1,0:T(8,128)(2,1)}, bf16[32,69]{1,0:T(8,128)(2,1)}, bf16[128,1024]{1,0...) custom-call(f32[1,1]{1,0:T(1,128)} %bitcast.band_hbm, ...), custom_call_target="tpu_custom_call" | custom-call | flops 2500000000 | bytes 10000000 | tf_op jit(solution)/shard_map/forward/pallas_call | solution.py:557
  27.6 1.6 %collective-permute-start.3 = (bf16[32,69]{1,0:T(8,128)(2,1)}, bf16[32,69]{1,0:T(8,128)(2,1)S(1)}, u32[]{:S(2)}, u32[]{:S(2)}) collective-permute-start(bf16[32,69]{1,0:T(8,128)(2,1)} %get-tuple-element.34), channel_id=1, source_target_pairs={{0,4},{4,8},{8,12},{12,16},{16,20},{20,24},{24,28},{28,32},{32,36}... | collective-permute-start | bytes 13256 | tf_op jit(solution)/shard_map/ppermute | solution.py:532
  29.2 2.9 %collective-permute-start.4 = (bf16[32,69]{1,0:T(8,128)(2,1)}, bf16[32,69]{1,0:T(8,128)(2,1)S(1)}, u32[]{:S(2)}, u32[]{:S(2)}) collective-permute-start(bf16[32,69]{1,0:T(8,128)(2,1)} %get-tuple-element.35), channel_id=1, source_target_pairs={{0,5},{1,6},{2,7},{3,4},{4,9},{5,10},{6,11},{7,8},{8,13},{9,14},{1... | collective-permute-start | bytes 13256 | tf_op jit(solution)/shard_map/ppermute | solution.py:538
  32.1 0.0 collective-permute-start.5
  32.1 4.8 %collective-permute-done.3.lon_piece = bf16[32,69]{1,0:T(8,128)(2,1)S(1)} collective-permute-done((bf16[32,69]{1,0:T(8,128)(2,1)}, bf16[32,69]{1,0:T(8,128)(2,1)S(1)}, u32[]{:S(2)}, u32[]{:S(2)}) %collective-permute-start.3) | collective-permute-done | bytes 4448 | tf_op jit(solution)/shard_map/ppermute | solution.py:532
  37.0 1.3 %collective-permute-done.4.far_piece = bf16[32,69]{1,0:T(8,128)(2,1)S(1)} collective-permute-done((bf16[32,69]{1,0:T(8,128)(2,1)}, bf16[32,69]{1,0:T(8,128)(2,1)S(1)}, u32[]{:S(2)}, u32[]{:S(2)}) %collective-permute-start.4) | collective-permute-done | bytes 4448 | tf_op jit(solution)/shard_map/ppermute | solution.py:538
  38.2 0.0 collective-permute-done.5.lat_piece
  38.2 0.0 all-to-all-done
  38.2 0.0 copy-start
  38.3 0.6 copy-done.7
  38.8 0.0 copy-done.8
  38.8 0.0 copy-done
  38.9 2.5 %observe.1 = (f32[128,8]{1,0:T(8,128)}, f32[8,16,69]{2,1,0:T(8,128)}, bf16[32,69]{1,0:T(8,128)(2,1)}, bf16[32,69]{1,0:T(8,128)(2,1)}, bf16[32,69]{1,0:T(8,128)(2,1)}, /*index=5*/bf16[32,69]{1,0:T(8,128)(2,1)}) custom-call(f32[8,16,69]{2,1,0:T(8,128)} %direction_ref.3, bf16[32,69]{1,0:T(8,128)(2,1)} %get-tuple-element.33.own_piece, bf16[32,69]{1,0:T(8,128)(2,1)} %copy-done.6, ...), custom_call_target="tpu_custom_call" | custom-call | tf_op jit(solution)/shard_map/observe/pallas_call | solution.py:574
  41.3 1.5 %collective-permute-start.6 = (bf16[32,69]{1,0:T(8,128)(2,1)}, bf16[32,69]{1,0:T(8,128)(2,1)S(1)}, u32[]{:S(2)}, u32[]{:S(2)}) collective-permute-start(bf16[32,69]{1,0:T(8,128)(2,1)} %get-tuple-element.40), channel_id=1, source_target_pairs={{0,124},{4,0},{8,4},{12,8},{16,12},{20,16},{24,20},{28,24},{32,28}... | collective-permute-start | bytes 13256 | tf_op jit(solution)/shard_map/ppermute | solution.py:532
  42.8 2.5 %collective-permute-start.7 = (bf16[32,69]{1,0:T(8,128)(2,1)}, bf16[32,69]{1,0:T(8,128)(2,1)S(1)}, u32[]{:S(2)}, u32[]{:S(2)}) collective-permute-start(bf16[32,69]{1,0:T(8,128)(2,1)} %get-tuple-element.41), channel_id=1, source_target_pairs={{0,127},{1,124},{2,125},{3,126},{4,3},{5,0},{6,1},{7,2},{8,7},{9,4... | collective-permute-start | bytes 13256 | tf_op jit(solution)/shard_map/ppermute | solution.py:538
  45.3 0.0 collective-permute-start.8
  45.4 4.8 %all-to-all-start.1 = ((f32[128,1,8]{2,1,0:T(1,128)}), f32[128,1,8]{2,1,0:T(1,128)S(1)}, u32[]{:S(2)}, u32[]{:S(2)}) async-start(f32[128,1,8]{2,1,0:T(1,128)} %bitcast.27), calls=%async_computation.1 | async-start | bytes 131072 | tf_op jit(solution)/shard_map/all_to_all | solution.py:653
  50.2 0.0 collective-permute-done.6.lon_hbm
  50.2 0.0 copy-start.3
  50.2 0.0 collective-permute-done.7.far_hbm
  50.2 0.0 collective-permute-done.8.lat_hbm
  50.3 0.5 copy-done.3
  50.8 0.0 copy-done.4
  50.8 0.0 copy-done.5
  50.8 8.6 %adjoint.1 = (bf16[32,69]{1,0:T(8,128)(2,1)}, bf16[32,69]{1,0:T(8,128)(2,1)}, bf16[32,69]{1,0:T(8,128)(2,1)}, bf16[32,69]{1,0:T(8,128)(2,1)}) custom-call(bf16[32,69]{1,0:T(8,128)(2,1)} %get-tuple-element.39.own_hbm, bf16[32,69]{1,0:T(8,128)(2,1)} %copy-done.3, bf16[32,69]{1,0:T(8,128)(2,1)} %copy-done.4, bf16[32,69]{1,0:T(8,128)(2,1)} %copy-done.5, ...), custom_call_target="tpu_custom_call" | custom-call | flops 1500000000 | bytes 10000000 | tf_op jit(solution)/shard_map/adjoint/pallas_call | solution.py:588
  59.5 0.3 all-to-all-done.1
  59.7 1.3 %collective-permute-start.9 = (bf16[32,69]{1,0:T(8,128)(2,1)}, bf16[32,69]{1,0:T(8,128)(2,1)S(1)}, u32[]{:S(2)}, u32[]{:S(2)}) collective-permute-start(bf16[32,69]{1,0:T(8,128)(2,1)} %get-tuple-element.52), channel_id=1, source_target_pairs={{0,4},{4,8},{8,12},{12,16},{16,20},{20,24},{24,28},{28,32},{32,36}... | collective-permute-start | bytes 13256 | tf_op jit(solution)/shard_map/ppermute | solution.py:532
  61.1 2.9 %collective-permute-start.10 = (bf16[32,69]{1,0:T(8,128)(2,1)}, bf16[32,69]{1,0:T(8,128)(2,1)S(1)}, u32[]{:S(2)}, u32[]{:S(2)}) collective-permute-start(bf16[32,69]{1,0:T(8,128)(2,1)} %get-tuple-element.53), channel_id=1, source_target_pairs={{0,5},{1,6},{2,7},{3,4},{4,9},{5,10},{6,11},{7,8},{8,13},{9,14},{1... | collective-permute-start | bytes 13256 | tf_op jit(solution)/shard_map/ppermute | solution.py:538
  64.0 0.0 collective-permute-start.11
  64.0 0.0 copy-done.1
  64.0 1.6 %unpack.1 = f32[1,512]{1,0:T(1,128)} custom-call(s32[1,512]{1,0:T(1,128)} %bitcast.29, f32[1,512]{1,0:T(1,128)} %get-tuple-element.56.slots_ref, f32[128,8]{1,0:T(8,128)} %bitcast.23), custom_call_target="tpu_custom_call" | custom-call | tf_op jit(solution)/shard_map/unpack/pallas_call | solution.py:671
  65.6 3.2 %collective-permute-done.9 = bf16[32,69]{1,0:T(8,128)(2,1)S(1)} collective-permute-done((bf16[32,69]{1,0:T(8,128)(2,1)}, bf16[32,69]{1,0:T(8,128)(2,1)S(1)}, u32[]{:S(2)}, u32[]{:S(2)}) %collective-permute-start.9) | collective-permute-done | bytes 4448 | tf_op jit(solution)/shard_map/ppermute | solution.py:532
  68.8 1.3 %collective-permute-done.10 = bf16[32,69]{1,0:T(8,128)(2,1)S(1)} collective-permute-done((bf16[32,69]{1,0:T(8,128)(2,1)}, bf16[32,69]{1,0:T(8,128)(2,1)S(1)}, u32[]{:S(2)}, u32[]{:S(2)}) %collective-permute-start.10) | collective-permute-done | bytes 4448 | tf_op jit(solution)/shard_map/ppermute | solution.py:538
  70.1 0.0 collective-permute-done.11
  70.1 1.3 %convert_add_fusion = f32[8,16,69]{2,1,0:T(8,128)} fusion(f32[8,16,69]{2,1,0:T(8,128)S(1)} %copy-done.2, bf16[4,8,69]{2,1,0:T(8,128)(2,1)} %bitcast.31, bf16[4,8,69]{2,1,0:T(8,128)(2,1)S(1)} %bitcast.34, bf16[4,8,69]{2,1,0:T(8,128)(2,1)S(1)} %bitcast.33, bf16[4,8,69]{2,1,0:T(8,128)(2,1)S(1)} %bitcast.32), kind=kLoop, calls=%fused_computation | loop fusion | flops 70656 | bytes 88320 | tf_op jit(solution)/shard_map/add | solution.py:670
  (10 shorter events, 0.0 us)
Async XLA Ops:
  2.7 15.1 %collective-permute-start = (bf16[64,69]{1,0:T(8,128)(2,1)}, bf16[64,69]{1,0:T(8,128)(2,1)S(1)}, u32[]{:S(2)}, u32[]{:S(2)}) collective-permute-start(bf16[64,69]{1,0:T(8,128)(2,1)} %get-tuple-element.30), channel_id=1, source_target_pairs={{0,124},{4,0},{8,4},{12,8},{16,12},{20,16},{24,20},{28,24},{32,28}... | collective-permute-start | bytes 26504 | tf_op jit(solution)/shard_map/ppermute | solution.py:532
  12.2 5.6 %collective-permute-start.1 = (bf16[64,69]{1,0:T(8,128)(2,1)}, bf16[64,69]{1,0:T(8,128)(2,1)S(1)}, u32[]{:S(2)}, u32[]{:S(2)}) collective-permute-start(bf16[64,69]{1,0:T(8,128)(2,1)} %get-tuple-element.31), channel_id=1, source_target_pairs={{0,127},{1,124},{2,125},{3,126},{4,3},{5,0},{6,1},{7,2},{8,7},{9,4... | collective-permute-start | bytes 26504 | tf_op jit(solution)/shard_map/ppermute | solution.py:538
  13.1 4.7 %collective-permute-start.2 = (bf16[64,69]{1,0:T(8,128)(2,1)}, bf16[64,69]{1,0:T(8,128)(2,1)S(1)}, u32[]{:S(2)}, u32[]{:S(2)}) collective-permute-start(bf16[64,69]{1,0:T(8,128)(2,1)} %get-tuple-element.32), channel_id=1, source_target_pairs={{0,3},{1,0},{2,1},{3,2},{4,7},{5,4},{6,5},{7,6},{8,11},{9,8},{10,9... | collective-permute-start | bytes 26504 | tf_op jit(solution)/shard_map/ppermute | solution.py:531
  13.1 25.1 %all-to-all-start = ((f32[128,1,64]{2,1,0:T(1,128)}), f32[128,1,64]{2,1,0:T(1,128)S(1)}, u32[]{:S(2)}, u32[]{:S(2)}) async-start(f32[128,1,64]{2,1,0:T(1,128)} %bitcast.26), calls=%async_computation | async-start | bytes 131072 | tf_op jit(solution)/shard_map/all_to_all | solution.py:642
  17.8 0.6 copy-start.9
  17.8 0.6 copy-start.10
  17.8 0.6 copy-start.11
  27.6 9.3 %collective-permute-start.3 = (bf16[32,69]{1,0:T(8,128)(2,1)}, bf16[32,69]{1,0:T(8,128)(2,1)S(1)}, u32[]{:S(2)}, u32[]{:S(2)}) collective-permute-start(bf16[32,69]{1,0:T(8,128)(2,1)} %get-tuple-element.34), channel_id=1, source_target_pairs={{0,4},{4,8},{8,12},{12,16},{16,20},{20,24},{24,28},{28,32},{32,36}... | collective-permute-start | bytes 13256 | tf_op jit(solution)/shard_map/ppermute | solution.py:532
  29.2 9.0 %collective-permute-start.4 = (bf16[32,69]{1,0:T(8,128)(2,1)}, bf16[32,69]{1,0:T(8,128)(2,1)S(1)}, u32[]{:S(2)}, u32[]{:S(2)}) collective-permute-start(bf16[32,69]{1,0:T(8,128)(2,1)} %get-tuple-element.35), channel_id=1, source_target_pairs={{0,5},{1,6},{2,7},{3,4},{4,9},{5,10},{6,11},{7,8},{8,13},{9,14},{1... | collective-permute-start | bytes 13256 | tf_op jit(solution)/shard_map/ppermute | solution.py:538
  32.1 6.1 %collective-permute-start.5 = (bf16[32,69]{1,0:T(8,128)(2,1)}, bf16[32,69]{1,0:T(8,128)(2,1)S(1)}, u32[]{:S(2)}, u32[]{:S(2)}) collective-permute-start(bf16[32,69]{1,0:T(8,128)(2,1)} %get-tuple-element.36), channel_id=1, source_target_pairs={{0,1},{1,2},{2,3},{3,0},{4,5},{5,6},{6,7},{7,4},{8,9},{9,10},{10,1... | collective-permute-start | bytes 13256 | tf_op jit(solution)/shard_map/ppermute | solution.py:531
  37.0 1.3 %copy-start.6 = (bf16[32,69]{1,0:T(8,128)(2,1)}, bf16[32,69]{1,0:T(8,128)(2,1)S(1)}, u32[]{:S(2)}) copy-start(bf16[32,69]{1,0:T(8,128)(2,1)S(1)} %collective-permute-done.3.lon_piece) | copy-start | bytes 13252
  38.2 0.6 copy-start.7
  38.2 0.6 copy-start.8
  38.2 0.6 copy-start
  41.3 28.7 %copy-start.2 = (f32[8,16,69]{2,1,0:T(8,128)S(1)}, f32[8,16,69]{2,1,0:T(8,128)}, u32[]{:S(2)}) copy-start(f32[8,16,69]{2,1,0:T(8,128)} %get-tuple-element.38) | copy-start | bytes 105988
  41.3 8.9 %collective-permute-start.6 = (bf16[32,69]{1,0:T(8,128)(2,1)}, bf16[32,69]{1,0:T(8,128)(2,1)S(1)}, u32[]{:S(2)}, u32[]{:S(2)}) collective-permute-start(bf16[32,69]{1,0:T(8,128)(2,1)} %get-tuple-element.40), channel_id=1, source_target_pairs={{0,124},{4,0},{8,4},{12,8},{16,12},{20,16},{24,20},{28,24},{32,28}... | collective-permute-start | bytes 13256 | tf_op jit(solution)/shard_map/ppermute | solution.py:532
  42.8 7.4 %collective-permute-start.7 = (bf16[32,69]{1,0:T(8,128)(2,1)}, bf16[32,69]{1,0:T(8,128)(2,1)S(1)}, u32[]{:S(2)}, u32[]{:S(2)}) collective-permute-start(bf16[32,69]{1,0:T(8,128)(2,1)} %get-tuple-element.41), channel_id=1, source_target_pairs={{0,127},{1,124},{2,125},{3,126},{4,3},{5,0},{6,1},{7,2},{8,7},{9,4... | collective-permute-start | bytes 13256 | tf_op jit(solution)/shard_map/ppermute | solution.py:538
  45.3 4.9 %collective-permute-start.8 = (bf16[32,69]{1,0:T(8,128)(2,1)}, bf16[32,69]{1,0:T(8,128)(2,1)S(1)}, u32[]{:S(2)}, u32[]{:S(2)}) collective-permute-start(bf16[32,69]{1,0:T(8,128)(2,1)} %get-tuple-element.42), channel_id=1, source_target_pairs={{0,3},{1,0},{2,1},{3,2},{4,7},{5,4},{6,5},{7,6},{8,11},{9,8},{10,9... | collective-permute-start | bytes 13256 | tf_op jit(solution)/shard_map/ppermute | solution.py:531
  45.4 14.4 %all-to-all-start.1 = ((f32[128,1,8]{2,1,0:T(1,128)}), f32[128,1,8]{2,1,0:T(1,128)S(1)}, u32[]{:S(2)}, u32[]{:S(2)}) async-start(f32[128,1,8]{2,1,0:T(1,128)} %bitcast.27), calls=%async_computation.1 | async-start | bytes 131072 | tf_op jit(solution)/shard_map/all_to_all | solution.py:653
  50.2 0.6 copy-start.3
  50.2 0.6 copy-start.4
  50.2 0.6 copy-start.5
  59.7 4.3 %copy-start.1 = (f32[128,1,8]{2,1,0:T(1,128)}, f32[128,1,8]{2,1,0:T(1,128)S(1)}, u32[]{:S(2)}) copy-start(f32[128,1,8]{2,1,0:T(1,128)S(1)} %all-to-all-done.1) | copy-start | bytes 12292
  59.7 9.1 %collective-permute-start.9 = (bf16[32,69]{1,0:T(8,128)(2,1)}, bf16[32,69]{1,0:T(8,128)(2,1)S(1)}, u32[]{:S(2)}, u32[]{:S(2)}) collective-permute-start(bf16[32,69]{1,0:T(8,128)(2,1)} %get-tuple-element.52), channel_id=1, source_target_pairs={{0,4},{4,8},{8,12},{12,16},{16,20},{20,24},{24,28},{28,32},{32,36}... | collective-permute-start | bytes 13256 | tf_op jit(solution)/shard_map/ppermute | solution.py:532
  61.1 9.0 %collective-permute-start.10 = (bf16[32,69]{1,0:T(8,128)(2,1)}, bf16[32,69]{1,0:T(8,128)(2,1)S(1)}, u32[]{:S(2)}, u32[]{:S(2)}) collective-permute-start(bf16[32,69]{1,0:T(8,128)(2,1)} %get-tuple-element.53), channel_id=1, source_target_pairs={{0,5},{1,6},{2,7},{3,4},{4,9},{5,10},{6,11},{7,8},{8,13},{9,14},{1... | collective-permute-start | bytes 13256 | tf_op jit(solution)/shard_map/ppermute | solution.py:538
  64.0 6.1 %collective-permute-start.11 = (bf16[32,69]{1,0:T(8,128)(2,1)}, bf16[32,69]{1,0:T(8,128)(2,1)S(1)}, u32[]{:S(2)}, u32[]{:S(2)}) collective-permute-start(bf16[32,69]{1,0:T(8,128)(2,1)} %get-tuple-element.54), channel_id=1, source_target_pairs={{0,1},{1,2},{2,3},{3,0},{4,5},{5,6},{6,7},{7,4},{8,9},{9,10},{10,1... | collective-permute-start | bytes 13256 | tf_op jit(solution)/shard_map/ppermute | solution.py:531

commit v5 on v4

--- a/solution.py
+++ b/solution.py
@@ -655,7 +655,7 @@
     own_piece, lat_piece, lon_piece, far_piece = run_adjoint(
         logit_scale, (own_piece, lon_piece, far_piece, lat_piece), embed_weight, gain, decode_gain, decode_rows, kept, qkv_weight, out_weight
     )
-    lat_piece, lon_piece, far_piece, returned = lax.optimization_barrier((lat_piece, lon_piece, far_piece, returned))
+    own_piece, returned = lax.optimization_barrier((own_piece, returned))
     lat_piece, lon_piece, far_piece = exchanged(lat_piece, lon_piece, far_piece, 1)
 
     hvp = adjoint_field

time: 71.8 us -> 71.8 us (level)
  waiting for transfers between devices: 10.8 us -> 9.9 us
  transfers between devices with their start and end apart: 14 -> 14, of which waited for: 5 -> 4; matrix products, arithmetic and copies ran while one was open for 0% -> 0% of each run, Pallas kernels for 27% -> 27%
where the time goes in v5:
time: 71.8 us; the launch traced here: 71.4 us
  starting transfers between devices  33 us (46%)
  Pallas kernels  24 us (33%)
  waiting for transfers between devices  9.9 us (14%)
  local copies, waits for them, and re-layouts  2.44 us (3%)
  other arithmetic  1.34 us (2%)
  between operations  0.8 us (1%)
    ppermute x4, starting transfers between devices, exchanged(): lax.ppermute(lon_piece, 'lon', [(i, (i + steps) % lon_count) for i in ran...  14.1 us
    ppermute x4, starting transfers between devices, exchanged(): far_piece = lax.ppermute(far_piece, ('lon', 'lat'), pairs)  9.29 us
    pallas_call x1, Pallas kernels, run_forward(): pl.pallas_call(forward_kernel, out_shape=[quarter] * 4 + kept, in_specs=[...  9.18 us
    pallas_call x1, Pallas kernels, run_adjoint(): pl.pallas_call(adjoint_kernel, out_shape=[shape(pieces[0].shape, bf16)] *...  8.62 us
    ppermute x4, waiting for transfers between devices, exchanged(): lax.ppermute(lon_piece, 'lon', [(i, (i + steps) % lon_count) for i in ran...  7.36 us
    all_to_all x1, starting transfers between devices, per_device(): lax.all_to_all(at_obs, ('lon', 'lat'), split_axis=0, concat_axis=0, tiled...  4.83 us
    all_to_all x1, starting transfers between devices, per_device(): lax.all_to_all(outgoing, ('lon', 'lat'), split_axis=0, concat_axis=0, til...  4.64 us
    ppermute x4, waiting for transfers between devices, exchanged(): far_piece = lax.ppermute(far_piece, ('lon', 'lat'), pairs)  2.53 us
  transfers between devices with their start and end apart: 14, of which 4 were waited for; matrix products, arithmetic and copies ran while one was open for 0% of the time, Pallas kernels for 27%

profile of v5, /device:TPU:1, one launch (start us, length us, event | category | flops | bytes accessed | tf_op | source)
XLA Modules:
  0.0 71.4 jit_solution(7292776445747044806)
XLA Ops:
  0.6 2.0 %prepare.1 = (bf16[64,69]{1,0:T(8,128)(2,1)}, bf16[64,69]{1,0:T(8,128)(2,1)}, bf16[64,69]{1,0:T(8,128)(2,1)}, f32[128,64]{1,0:T(8,128)}, f32[1,512]{1,0:T(1,128)}) custom-call(f32[8,16,69]{2,1,0:T(8,128)} %background_hbm.1, f32[8,16,69]{2,1,0:T(8,128)} %direction_ref.3, s32[1,512]{1,0:T(1,128)} %bitcast.28, s32[1,512]{1,0:T(1,128)} %bitcast.39, ...), custom_call_target="tpu_custom_call" | custom-call | tf_op jit(solution)/shard_map/prepare/pallas_call | solution.py:626
  2.7 9.5 %collective-permute-start = (bf16[64,69]{1,0:T(8,128)(2,1)}, bf16[64,69]{1,0:T(8,128)(2,1)S(1)}, u32[]{:S(2)}, u32[]{:S(2)}) collective-permute-start(bf16[64,69]{1,0:T(8,128)(2,1)} %get-tuple-element.28), channel_id=1, source_target_pairs={{0,124},{4,0},{8,4},{12,8},{16,12},{20,16},{24,20},{28,24},{32,28}... | collective-permute-start | bytes 26504 | tf_op jit(solution)/shard_map/ppermute | solution.py:532
  12.2 1.0 %collective-permute-start.1 = (bf16[64,69]{1,0:T(8,128)(2,1)}, bf16[64,69]{1,0:T(8,128)(2,1)S(1)}, u32[]{:S(2)}, u32[]{:S(2)}) collective-permute-start(bf16[64,69]{1,0:T(8,128)(2,1)} %get-tuple-element.29), channel_id=1, source_target_pairs={{0,127},{1,124},{2,125},{3,126},{4,3},{5,0},{6,1},{7,2},{8,7},{9,4... | collective-permute-start | bytes 26504 | tf_op jit(solution)/shard_map/ppermute | solution.py:538
  13.1 0.0 collective-permute-start.2
  13.1 4.6 %all-to-all-start = ((f32[128,1,64]{2,1,0:T(1,128)}), f32[128,1,64]{2,1,0:T(1,128)S(1)}, u32[]{:S(2)}, u32[]{:S(2)}) async-start(f32[128,1,64]{2,1,0:T(1,128)} %bitcast.26), calls=%async_computation | async-start | bytes 131072 | tf_op jit(solution)/shard_map/all_to_all | solution.py:642
  17.8 0.0 collective-permute-done.lon_hbm
  17.8 0.0 copy-start.9
  17.8 0.0 collective-permute-done.1.far_hbm
  17.8 0.0 collective-permute-done.2.lat_hbm
  17.8 0.0 copy-start.11
  17.9 0.5 copy-done.9
  18.4 0.0 copy-done.10
  18.4 0.0 copy-done.11
  18.4 9.2 %forward.1 = (bf16[32,69]{1,0:T(8,128)(2,1)}, bf16[32,69]{1,0:T(8,128)(2,1)}, bf16[32,69]{1,0:T(8,128)(2,1)}, bf16[32,69]{1,0:T(8,128)(2,1)}, bf16[128,1024]{1,0...) custom-call(f32[1,1]{1,0:T(1,128)} %bitcast.band_hbm, ...), custom_call_target="tpu_custom_call" | custom-call | flops 2500000000 | bytes 10000000 | tf_op jit(solution)/shard_map/forward/pallas_call | solution.py:557
  27.6 1.6 %collective-permute-start.3 = (bf16[32,69]{1,0:T(8,128)(2,1)}, bf16[32,69]{1,0:T(8,128)(2,1)S(1)}, u32[]{:S(2)}, u32[]{:S(2)}) collective-permute-start(bf16[32,69]{1,0:T(8,128)(2,1)} %get-tuple-element.32), channel_id=1, source_target_pairs={{0,4},{4,8},{8,12},{12,16},{16,20},{20,24},{24,28},{28,32},{32,36}... | collective-permute-start | bytes 13256 | tf_op jit(solution)/shard_map/ppermute | solution.py:532
  29.2 2.9 %collective-permute-start.4 = (bf16[32,69]{1,0:T(8,128)(2,1)}, bf16[32,69]{1,0:T(8,128)(2,1)S(1)}, u32[]{:S(2)}, u32[]{:S(2)}) collective-permute-start(bf16[32,69]{1,0:T(8,128)(2,1)} %get-tuple-element.33), channel_id=1, source_target_pairs={{0,5},{1,6},{2,7},{3,4},{4,9},{5,10},{6,11},{7,8},{8,13},{9,14},{1... | collective-permute-start | bytes 13256 | tf_op jit(solution)/shard_map/ppermute | solution.py:538
  32.1 0.0 collective-permute-start.5
  32.1 4.8 %collective-permute-done.3.lon_piece = bf16[32,69]{1,0:T(8,128)(2,1)S(1)} collective-permute-done((bf16[32,69]{1,0:T(8,128)(2,1)}, bf16[32,69]{1,0:T(8,128)(2,1)S(1)}, u32[]{:S(2)}, u32[]{:S(2)}) %collective-permute-start.3) | collective-permute-done | bytes 4448 | tf_op jit(solution)/shard_map/ppermute | solution.py:532
  37.0 1.3 %collective-permute-done.4.far_piece = bf16[32,69]{1,0:T(8,128)(2,1)S(1)} collective-permute-done((bf16[32,69]{1,0:T(8,128)(2,1)}, bf16[32,69]{1,0:T(8,128)(2,1)S(1)}, u32[]{:S(2)}, u32[]{:S(2)}) %collective-permute-start.4) | collective-permute-done | bytes 4448 | tf_op jit(solution)/shard_map/ppermute | solution.py:538
  38.2 0.0 collective-permute-done.5.lat_piece
  38.2 0.0 all-to-all-done
  38.2 0.0 copy-start
  38.3 0.6 copy-done.7
  38.8 0.0 copy-done.8
  38.8 0.0 copy-done
  38.9 2.5 %observe.1 = (f32[128,8]{1,0:T(8,128)}, f32[8,16,69]{2,1,0:T(8,128)}, bf16[32,69]{1,0:T(8,128)(2,1)}, bf16[32,69]{1,0:T(8,128)(2,1)}, bf16[32,69]{1,0:T(8,128)(2,1)}, /*index=5*/bf16[32,69]{1,0:T(8,128)(2,1)}) custom-call(f32[8,16,69]{2,1,0:T(8,128)} %direction_ref.3, bf16[32,69]{1,0:T(8,128)(2,1)} %get-tuple-element.31.own_piece, bf16[32,69]{1,0:T(8,128)(2,1)} %copy-done.6, ...), custom_call_target="tpu_custom_call" | custom-call | tf_op jit(solution)/shard_map/observe/pallas_call | solution.py:574
  41.3 1.5 %collective-permute-start.6 = (bf16[32,69]{1,0:T(8,128)(2,1)}, bf16[32,69]{1,0:T(8,128)(2,1)S(1)}, u32[]{:S(2)}, u32[]{:S(2)}) collective-permute-start(bf16[32,69]{1,0:T(8,128)(2,1)} %get-tuple-element.38), channel_id=1, source_target_pairs={{0,124},{4,0},{8,4},{12,8},{16,12},{20,16},{24,20},{28,24},{32,28}... | collective-permute-start | bytes 13256 | tf_op jit(solution)/shard_map/ppermute | solution.py:532
  42.8 2.5 %collective-permute-start.7 = (bf16[32,69]{1,0:T(8,128)(2,1)}, bf16[32,69]{1,0:T(8,128)(2,1)S(1)}, u32[]{:S(2)}, u32[]{:S(2)}) collective-permute-start(bf16[32,69]{1,0:T(8,128)(2,1)} %get-tuple-element.39), channel_id=1, source_target_pairs={{0,127},{1,124},{2,125},{3,126},{4,3},{5,0},{6,1},{7,2},{8,7},{9,4... | collective-permute-start | bytes 13256 | tf_op jit(solution)/shard_map/ppermute | solution.py:538
  45.3 0.0 collective-permute-start.8
  45.4 4.8 %all-to-all-start.1 = ((f32[128,1,8]{2,1,0:T(1,128)}), f32[128,1,8]{2,1,0:T(1,128)S(1)}, u32[]{:S(2)}, u32[]{:S(2)}) async-start(f32[128,1,8]{2,1,0:T(1,128)} %bitcast.27), calls=%async_computation.1 | async-start | bytes 131072 | tf_op jit(solution)/shard_map/all_to_all | solution.py:653
  50.2 0.0 collective-permute-done.6.lon_hbm
  50.2 0.0 copy-start.3
  50.2 0.0 collective-permute-done.7.far_hbm
  50.2 0.0 collective-permute-done.8.lat_hbm
  50.3 0.5 copy-done.3
  50.8 0.0 copy-done.4
  50.8 0.0 copy-done.5
  50.8 8.6 %adjoint.1 = (bf16[32,69]{1,0:T(8,128)(2,1)}, bf16[32,69]{1,0:T(8,128)(2,1)}, bf16[32,69]{1,0:T(8,128)(2,1)}, bf16[32,69]{1,0:T(8,128)(2,1)}) custom-call(bf16[32,69]{1,0:T(8,128)(2,1)} %get-tuple-element.37.own_hbm, bf16[32,69]{1,0:T(8,128)(2,1)} %copy-done.3, bf16[32,69]{1,0:T(8,128)(2,1)} %copy-done.4, bf16[32,69]{1,0:T(8,128)(2,1)} %copy-done.5, ...), custom_call_target="tpu_custom_call" | custom-call | flops 1500000000 | bytes 10000000 | tf_op jit(solution)/shard_map/adjoint/pallas_call | solution.py:588
  59.5 1.6 %collective-permute-start.9 = (bf16[32,69]{1,0:T(8,128)(2,1)}, bf16[32,69]{1,0:T(8,128)(2,1)S(1)}, u32[]{:S(2)}, u32[]{:S(2)}) collective-permute-start(bf16[32,69]{1,0:T(8,128)(2,1)} %get-tuple-element.46), channel_id=1, source_target_pairs={{0,4},{4,8},{8,12},{12,16},{16,20},{20,24},{24,28},{28,32},{32,36}... | collective-permute-start | bytes 13256 | tf_op jit(solution)/shard_map/ppermute | solution.py:532
  61.0 2.9 %collective-permute-start.10 = (bf16[32,69]{1,0:T(8,128)(2,1)}, bf16[32,69]{1,0:T(8,128)(2,1)S(1)}, u32[]{:S(2)}, u32[]{:S(2)}) collective-permute-start(bf16[32,69]{1,0:T(8,128)(2,1)} %get-tuple-element.47), channel_id=1, source_target_pairs={{0,5},{1,6},{2,7},{3,4},{4,9},{5,10},{6,11},{7,8},{8,13},{9,14},{1... | collective-permute-start | bytes 13256 | tf_op jit(solution)/shard_map/ppermute | solution.py:538
  63.9 0.0 collective-permute-start.11
  64.0 0.0 all-to-all-done.1
  64.0 0.6 copy-done.1
  64.6 1.6 %unpack.1 = f32[1,512]{1,0:T(1,128)} custom-call(s32[1,512]{1,0:T(1,128)} %bitcast.29, f32[1,512]{1,0:T(1,128)} %get-tuple-element.52.slots_ref, f32[128,8]{1,0:T(8,128)} %bitcast.23), custom_call_target="tpu_custom_call" | custom-call | tf_op jit(solution)/shard_map/unpack/pallas_call | solution.py:671
  66.3 2.5 %collective-permute-done.9 = bf16[32,69]{1,0:T(8,128)(2,1)S(1)} collective-permute-done((bf16[32,69]{1,0:T(8,128)(2,1)}, bf16[32,69]{1,0:T(8,128)(2,1)S(1)}, u32[]{:S(2)}, u32[]{:S(2)}) %collective-permute-start.9) | collective-permute-done | bytes 4448 | tf_op jit(solution)/shard_map/ppermute | solution.py:532
  68.8 1.3 %collective-permute-done.10 = bf16[32,69]{1,0:T(8,128)(2,1)S(1)} collective-permute-done((bf16[32,69]{1,0:T(8,128)(2,1)}, bf16[32,69]{1,0:T(8,128)(2,1)S(1)}, u32[]{:S(2)}, u32[]{:S(2)}) %collective-permute-start.10) | collective-permute-done | bytes 4448 | tf_op jit(solution)/shard_map/ppermute | solution.py:538
  70.1 0.0 collective-permute-done.11
  70.1 1.3 %convert_add_fusion = f32[8,16,69]{2,1,0:T(8,128)} fusion(f32[8,16,69]{2,1,0:T(8,128)S(1)} %copy-done.2, bf16[4,8,69]{2,1,0:T(8,128)(2,1)} %bitcast.31, bf16[4,8,69]{2,1,0:T(8,128)(2,1)S(1)} %bitcast.34, bf16[4,8,69]{2,1,0:T(8,128)(2,1)S(1)} %bitcast.33, bf16[4,8,69]{2,1,0:T(8,128)(2,1)S(1)} %bitcast.32), kind=kLoop, calls=%fused_computation | loop fusion | flops 70656 | bytes 88320 | tf_op jit(solution)/shard_map/add | solution.py:670
  (10 shorter events, 0.0 us)
Async XLA Ops:
  2.7 15.1 %collective-permute-start = (bf16[64,69]{1,0:T(8,128)(2,1)}, bf16[64,69]{1,0:T(8,128)(2,1)S(1)}, u32[]{:S(2)}, u32[]{:S(2)}) collective-permute-start(bf16[64,69]{1,0:T(8,128)(2,1)} %get-tuple-element.28), channel_id=1, source_target_pairs={{0,124},{4,0},{8,4},{12,8},{16,12},{20,16},{24,20},{28,24},{32,28}... | collective-permute-start | bytes 26504 | tf_op jit(solution)/shard_map/ppermute | solution.py:532
  12.2 5.6 %collective-permute-start.1 = (bf16[64,69]{1,0:T(8,128)(2,1)}, bf16[64,69]{1,0:T(8,128)(2,1)S(1)}, u32[]{:S(2)}, u32[]{:S(2)}) collective-permute-start(bf16[64,69]{1,0:T(8,128)(2,1)} %get-tuple-element.29), channel_id=1, source_target_pairs={{0,127},{1,124},{2,125},{3,126},{4,3},{5,0},{6,1},{7,2},{8,7},{9,4... | collective-permute-start | bytes 26504 | tf_op jit(solution)/shard_map/ppermute | solution.py:538
  13.1 4.7 %collective-permute-start.2 = (bf16[64,69]{1,0:T(8,128)(2,1)}, bf16[64,69]{1,0:T(8,128)(2,1)S(1)}, u32[]{:S(2)}, u32[]{:S(2)}) collective-permute-start(bf16[64,69]{1,0:T(8,128)(2,1)} %get-tuple-element.30), channel_id=1, source_target_pairs={{0,3},{1,0},{2,1},{3,2},{4,7},{5,4},{6,5},{7,6},{8,11},{9,8},{10,9... | collective-permute-start | bytes 26504 | tf_op jit(solution)/shard_map/ppermute | solution.py:531
  13.1 25.1 %all-to-all-start = ((f32[128,1,64]{2,1,0:T(1,128)}), f32[128,1,64]{2,1,0:T(1,128)S(1)}, u32[]{:S(2)}, u32[]{:S(2)}) async-start(f32[128,1,64]{2,1,0:T(1,128)} %bitcast.26), calls=%async_computation | async-start | bytes 131072 | tf_op jit(solution)/shard_map/all_to_all | solution.py:642
  17.8 0.6 copy-start.9
  17.8 0.6 copy-start.10
  17.8 0.6 copy-start.11
  27.6 9.3 %collective-permute-start.3 = (bf16[32,69]{1,0:T(8,128)(2,1)}, bf16[32,69]{1,0:T(8,128)(2,1)S(1)}, u32[]{:S(2)}, u32[]{:S(2)}) collective-permute-start(bf16[32,69]{1,0:T(8,128)(2,1)} %get-tuple-element.32), channel_id=1, source_target_pairs={{0,4},{4,8},{8,12},{12,16},{16,20},{20,24},{24,28},{28,32},{32,36}... | collective-permute-start | bytes 13256 | tf_op jit(solution)/shard_map/ppermute | solution.py:532
  29.2 9.0 %collective-permute-start.4 = (bf16[32,69]{1,0:T(8,128)(2,1)}, bf16[32,69]{1,0:T(8,128)(2,1)S(1)}, u32[]{:S(2)}, u32[]{:S(2)}) collective-permute-start(bf16[32,69]{1,0:T(8,128)(2,1)} %get-tuple-element.33), channel_id=1, source_target_pairs={{0,5},{1,6},{2,7},{3,4},{4,9},{5,10},{6,11},{7,8},{8,13},{9,14},{1... | collective-permute-start | bytes 13256 | tf_op jit(solution)/shard_map/ppermute | solution.py:538
  32.1 6.1 %collective-permute-start.5 = (bf16[32,69]{1,0:T(8,128)(2,1)}, bf16[32,69]{1,0:T(8,128)(2,1)S(1)}, u32[]{:S(2)}, u32[]{:S(2)}) collective-permute-start(bf16[32,69]{1,0:T(8,128)(2,1)} %get-tuple-element.34), channel_id=1, source_target_pairs={{0,1},{1,2},{2,3},{3,0},{4,5},{5,6},{6,7},{7,4},{8,9},{9,10},{10,1... | collective-permute-start | bytes 13256 | tf_op jit(solution)/shard_map/ppermute | solution.py:531
  37.0 1.3 %copy-start.6 = (bf16[32,69]{1,0:T(8,128)(2,1)}, bf16[32,69]{1,0:T(8,128)(2,1)S(1)}, u32[]{:S(2)}) copy-start(bf16[32,69]{1,0:T(8,128)(2,1)S(1)} %collective-permute-done.3.lon_piece) | copy-start | bytes 13252
  38.2 0.6 copy-start.7
  38.2 0.6 copy-start.8
  38.2 0.6 copy-start
  41.3 28.7 %copy-start.2 = (f32[8,16,69]{2,1,0:T(8,128)S(1)}, f32[8,16,69]{2,1,0:T(8,128)}, u32[]{:S(2)}) copy-start(f32[8,16,69]{2,1,0:T(8,128)} %get-tuple-element.36) | copy-start | bytes 105988
  41.3 8.9 %collective-permute-start.6 = (bf16[32,69]{1,0:T(8,128)(2,1)}, bf16[32,69]{1,0:T(8,128)(2,1)S(1)}, u32[]{:S(2)}, u32[]{:S(2)}) collective-permute-start(bf16[32,69]{1,0:T(8,128)(2,1)} %get-tuple-element.38), channel_id=1, source_target_pairs={{0,124},{4,0},{8,4},{12,8},{16,12},{20,16},{24,20},{28,24},{32,28}... | collective-permute-start | bytes 13256 | tf_op jit(solution)/shard_map/ppermute | solution.py:532
  42.8 7.4 %collective-permute-start.7 = (bf16[32,69]{1,0:T(8,128)(2,1)}, bf16[32,69]{1,0:T(8,128)(2,1)S(1)}, u32[]{:S(2)}, u32[]{:S(2)}) collective-permute-start(bf16[32,69]{1,0:T(8,128)(2,1)} %get-tuple-element.39), channel_id=1, source_target_pairs={{0,127},{1,124},{2,125},{3,126},{4,3},{5,0},{6,1},{7,2},{8,7},{9,4... | collective-permute-start | bytes 13256 | tf_op jit(solution)/shard_map/ppermute | solution.py:538
  45.3 4.9 %collective-permute-start.8 = (bf16[32,69]{1,0:T(8,128)(2,1)}, bf16[32,69]{1,0:T(8,128)(2,1)S(1)}, u32[]{:S(2)}, u32[]{:S(2)}) collective-permute-start(bf16[32,69]{1,0:T(8,128)(2,1)} %get-tuple-element.40), channel_id=1, source_target_pairs={{0,3},{1,0},{2,1},{3,2},{4,7},{5,4},{6,5},{7,6},{8,11},{9,8},{10,9... | collective-permute-start | bytes 13256 | tf_op jit(solution)/shard_map/ppermute | solution.py:531
  45.4 18.6 %all-to-all-start.1 = ((f32[128,1,8]{2,1,0:T(1,128)}), f32[128,1,8]{2,1,0:T(1,128)S(1)}, u32[]{:S(2)}, u32[]{:S(2)}) async-start(f32[128,1,8]{2,1,0:T(1,128)} %bitcast.27), calls=%async_computation.1 | async-start | bytes 131072 | tf_op jit(solution)/shard_map/all_to_all | solution.py:653
  50.2 0.6 copy-start.3
  50.2 0.6 copy-start.4
  50.2 0.6 copy-start.5
  59.5 9.3 %collective-permute-start.9 = (bf16[32,69]{1,0:T(8,128)(2,1)}, bf16[32,69]{1,0:T(8,128)(2,1)S(1)}, u32[]{:S(2)}, u32[]{:S(2)}) collective-permute-start(bf16[32,69]{1,0:T(8,128)(2,1)} %get-tuple-element.46), channel_id=1, source_target_pairs={{0,4},{4,8},{8,12},{12,16},{16,20},{20,24},{24,28},{28,32},{32,36}... | collective-permute-start | bytes 13256 | tf_op jit(solution)/shard_map/ppermute | solution.py:532
  61.0 9.0 %collective-permute-start.10 = (bf16[32,69]{1,0:T(8,128)(2,1)}, bf16[32,69]{1,0:T(8,128)(2,1)S(1)}, u32[]{:S(2)}, u32[]{:S(2)}) collective-permute-start(bf16[32,69]{1,0:T(8,128)(2,1)} %get-tuple-element.47), channel_id=1, source_target_pairs={{0,5},{1,6},{2,7},{3,4},{4,9},{5,10},{6,11},{7,8},{8,13},{9,14},{1... | collective-permute-start | bytes 13256 | tf_op jit(solution)/shard_map/ppermute | solution.py:538
  63.9 6.1 %collective-permute-start.11 = (bf16[32,69]{1,0:T(8,128)(2,1)}, bf16[32,69]{1,0:T(8,128)(2,1)S(1)}, u32[]{:S(2)}, u32[]{:S(2)}) collective-permute-start(bf16[32,69]{1,0:T(8,128)(2,1)} %get-tuple-element.48), channel_id=1, source_target_pairs={{0,1},{1,2},{2,3},{3,0},{4,5},{5,6},{6,7},{7,4},{8,9},{9,10},{10,1... | collective-permute-start | bytes 13256 | tf_op jit(solution)/shard_map/ppermute | solution.py:531
  64.0 0.6 copy-start.1

commit v6 on v5

--- a/solution.py
+++ b/solution.py
@@ -552,11 +552,11 @@
         shape((2 * CELLS, width), f32),
         shape((HEADS // 2, CELLS, 2 * CELLS), bf16),
     ]
-    inputs = (last_band, logit_scale, background, direction, strips[1], strips[2], strips[0], embed_weight, gain, decode_gain, decode_rows, qkv_weight, out_weight)
+    inputs = (last_band, logit_scale, background, direction, *(pltpu.with_memory_space_constraint(strips[i], pltpu.VMEM) for i in (1, 2, 0)), embed_weight, gain, decode_gain, decode_rows, qkv_weight, out_weight)
     both = pltpu.VMEM((2 * CELLS, width), bf16)
     return pl.pallas_call(
         forward_kernel,
-        out_shape=[quarter] * 4 + kept,
+        out_shape=[pltpu.VMEM(quarter.shape, bf16)] * 4 + kept,
         in_specs=[ANY] * 13,
         out_specs=[VMEM] * 4 + [ANY] * 5,
         scratch_shapes=[pltpu.VMEM(item.shape, item.dtype) for item in inputs]
@@ -573,21 +573,23 @@
     devices = arrived.shape[0]
     return pl.pallas_call(
         observe_kernel,
-        out_shape=[shape((devices, SLOTS), f32), shape(direction.shape, f32)] + [quarter] * 4,
+        out_shape=[pltpu.VMEM((devices, SLOTS), f32), shape(direction.shape, f32)] + [pltpu.VMEM(quarter.shape, bf16)] * 4,
         in_specs=[VMEM] * 6,
         out_specs=[VMEM] * 6,
+        compiler_params=pltpu.CompilerParams(vmem_limit_bytes=2 * 1024 * 1024),
         name="observe",
-    )(direction, *pieces, arrived)
+    )(direction, pltpu.with_memory_space_constraint(pieces[0], pltpu.VMEM), *pieces[1:], arrived)
 
 
 def run_adjoint(logit_scale, pieces, embed_weight, gain, decode_gain, decode_rows, kept, qkv_weight, out_weight):
     hidden, block, units, scales, probs = kept
     width = embed_weight.shape[1]
+    pieces = [pltpu.with_memory_space_constraint(piece, pltpu.VMEM) for piece in pieces]
     inputs = (*pieces, block, decode_rows, decode_gain, logit_scale, out_weight, units, probs, scales)
     inputs = (*inputs, hidden, gain, embed_weight, qkv_weight)
     return pl.pallas_call(
         adjoint_kernel,
-        out_shape=[shape(pieces[0].shape, bf16)] * 4,
+        out_shape=[pltpu.VMEM(pieces[0].shape, bf16)] * 4,
         in_specs=[ANY] * len(inputs),
         out_specs=[VMEM] * 4,
         scratch_shapes=[pltpu.VMEM(item.shape, item.dtype) for item in inputs]
@@ -625,8 +627,8 @@
     owners = obs_owner.reshape(1, obs_rows)
     *strips, outgoing, slots = pl.pallas_call(
         prepare_kernel,
-        out_shape=[shape((2 * QUARTER, var_count), bf16)] * 3
-        + [shape((devices, SLOTS * 8), f32), shape((1, obs_rows), f32)],
+        out_shape=[pltpu.VMEM((2 * QUARTER, var_count), bf16)] * 3
+        + [pltpu.VMEM((devices, SLOTS * 8), f32), shape((1, obs_rows), f32)],
         in_specs=[VMEM] * 6,
         out_specs=[VMEM] * 5,
         name="prepare",

time: 71.8 us -> 66.4 us (0.925)
  Pallas kernels: 24 us -> 21.8 us
  local copies, waits for them, and re-layouts: 2.44 us -> 0.64 us
    pallas_call x4, Pallas kernels: 22.3 us -> 20.1 us  [the longest x1 8.62 us: run_forward(): pl.pallas_call(forward_kernel, out_shape=[pltpu.VMEM(quarter.shape, bf16)...]
    unnamed x24 -> x4, local copies, waits for them, and re-layouts: 2.44 us -> 0.64 us
  transfers between devices with their start and end apart: 14 -> 14, of which waited for: 4 -> 4; matrix products, arithmetic and copies ran while one was open for 0% -> 0% of each run, Pallas kernels for 27% -> 28%
where the time goes in v6:
time: 66.4 us; the launch traced here: 66.1 us
  starting transfers between devices  32.9 us (50%)
  Pallas kernels  21.8 us (33%)
  waiting for transfers between devices  9.45 us (14%)
  between operations  0.74 us (1%)
    ppermute x4, starting transfers between devices, exchanged(): lax.ppermute(lon_piece, 'lon', [(i, (i + steps) % lon_count) for i in ran...  14 us
    ppermute x4, starting transfers between devices, exchanged(): far_piece = lax.ppermute(far_piece, ('lon', 'lat'), pairs)  9.31 us
    pallas_call x1, Pallas kernels, run_forward(): pl.pallas_call(forward_kernel, out_shape=[pltpu.VMEM(quarter.shape, bf16)...  8.62 us
    pallas_call x1, Pallas kernels, run_adjoint(): pl.pallas_call(adjoint_kernel, out_shape=[pltpu.VMEM(pieces[0].shape, bf1...  8.03 us
    ppermute x4, waiting for transfers between devices, exchanged(): lax.ppermute(lon_piece, 'lon', [(i, (i + steps) % lon_count) for i in ran...  6.91 us
    all_to_all x1, starting transfers between devices, per_device(): lax.all_to_all(at_obs, ('lon', 'lat'), split_axis=0, concat_axis=0, tiled...  4.84 us
    all_to_all x1, starting transfers between devices, per_device(): lax.all_to_all(outgoing, ('lon', 'lat'), split_axis=0, concat_axis=0, til...  4.64 us
    ppermute x4, waiting for transfers between devices, exchanged(): far_piece = lax.ppermute(far_piece, ('lon', 'lat'), pairs)  2.52 us
  transfers between devices with their start and end apart: 14, of which 4 were waited for; matrix products, arithmetic and copies ran while one was open for 0% of the time, Pallas kernels for 28%

profile of v6, /device:TPU:1, one launch (start us, length us, event | category | flops | bytes accessed | tf_op | source)
XLA Modules:
  0.0 66.1 jit_solution(10452270786306423026)
XLA Ops:
  0.6 0.0 copy-start
  0.6 2.1 %prepare.1 = (bf16[64,69]{1,0:T(8,128)(2,1)S(1)}, bf16[64,69]{1,0:T(8,128)(2,1)S(1)}, bf16[64,69]{1,0:T(8,128)(2,1)S(1)}, f32[128,64]{1,0:T(8,128)}, f32[1,512]{1,0:T(1,128)}) custom-call(f32[8,16,69]{2,1,0:T(8,128)} %background_hbm.1, f32[8,16,69]{2,1,0:T(8,128)} %direction_ref.3, s32[1,512]{1,0:T(1,128)} %bitcast.27, s32[1,512]{1,0:T(1,128)} %bitcast.37, ...), custom_call_target="tpu_custom_call" | custom-call | tf_op jit(solution)/shard_map/prepare/pallas_call | solution.py:628
  2.7 9.5 %collective-permute-start = (bf16[64,69]{1,0:T(8,128)(2,1)S(1)}, bf16[64,69]{1,0:T(8,128)(2,1)S(1)}, u32[]{:S(2)}, u32[]{:S(2)}) collective-permute-start(bf16[64,69]{1,0:T(8,128)(2,1)S(1)} %get-tuple-element.28), channel_id=1, source_target_pairs={{0,124},{4,0},{8,4},{12,8},{16,12},{20,16},{24,20},{28,24},{32,28}... | collective-permute-start | bytes 26504 | tf_op jit(solution)/shard_map/ppermute | solution.py:532
  12.2 1.0 %collective-permute-start.1 = (bf16[64,69]{1,0:T(8,128)(2,1)S(1)}, bf16[64,69]{1,0:T(8,128)(2,1)S(1)}, u32[]{:S(2)}, u32[]{:S(2)}) collective-permute-start(bf16[64,69]{1,0:T(8,128)(2,1)S(1)} %get-tuple-element.29), channel_id=1, source_target_pairs={{0,127},{1,124},{2,125},{3,126},{4,3},{5,0},{6,1},{7,2},{8,7},{9,4... | collective-permute-start | bytes 26504 | tf_op jit(solution)/shard_map/ppermute | solution.py:538
  13.2 0.0 collective-permute-start.2
  13.2 4.6 %all-to-all-start = ((f32[128,1,64]{2,1,0:T(1,128)}), f32[128,1,64]{2,1,0:T(1,128)S(1)}, u32[]{:S(2)}, u32[]{:S(2)}) async-start(f32[128,1,64]{2,1,0:T(1,128)} %bitcast.10), calls=%async_computation | async-start | bytes 131072 | tf_op jit(solution)/shard_map/all_to_all | solution.py:644
  17.8 0.0 collective-permute-done.lon_hbm
  17.8 0.0 collective-permute-done.1.far_hbm
  17.9 0.0 collective-permute-done.2.lat_hbm
  17.9 8.6 %forward.1 = (bf16[32,69]{1,0:T(8,128)(2,1)S(1)}, bf16[32,69]{1,0:T(8,128)(2,1)S(1)}, bf16[32,69]{1,0:T(8,128)(2,1)S(1)}, bf16[32,69]{1,0:T(8,128)(2,1)S(1)}, bf...) custom-call(f32[1,1]{1,0:T(1,128)} %bitcast.band_hbm, ...), custom_call_target="tpu_custom_call" | custom-call | flops 2500000000 | bytes 10000000 | tf_op jit(solution)/shard_map/forward/pallas_call | solution.py:557
  26.5 1.6 %collective-permute-start.3 = (bf16[32,69]{1,0:T(8,128)(2,1)S(1)}, bf16[32,69]{1,0:T(8,128)(2,1)S(1)}, u32[]{:S(2)}, u32[]{:S(2)}) collective-permute-start(bf16[32,69]{1,0:T(8,128)(2,1)S(1)} %get-tuple-element.32), channel_id=1, source_target_pairs={{0,4},{4,8},{8,12},{12,16},{16,20},{20,24},{24,28},{28,32},{32,36}... | collective-permute-start | bytes 13256 | tf_op jit(solution)/shard_map/ppermute | solution.py:532
  28.0 2.9 %collective-permute-start.4 = (bf16[32,69]{1,0:T(8,128)(2,1)S(1)}, bf16[32,69]{1,0:T(8,128)(2,1)S(1)}, u32[]{:S(2)}, u32[]{:S(2)}) collective-permute-start(bf16[32,69]{1,0:T(8,128)(2,1)S(1)} %get-tuple-element.33), channel_id=1, source_target_pairs={{0,5},{1,6},{2,7},{3,4},{4,9},{5,10},{6,11},{7,8},{8,13},{9,14},{1... | collective-permute-start | bytes 13256 | tf_op jit(solution)/shard_map/ppermute | solution.py:538
  31.0 0.0 collective-permute-start.5
  31.0 4.6 %collective-permute-done.3.lon_piece = bf16[32,69]{1,0:T(8,128)(2,1)S(1)} collective-permute-done((bf16[32,69]{1,0:T(8,128)(2,1)S(1)}, bf16[32,69]{1,0:T(8,128)(2,1)S(1)}, u32[]{:S(2)}, u32[]{:S(2)}) %collective-permute-start.3) | collective-permute-done | bytes 4448 | tf_op jit(solution)/shard_map/ppermute | solution.py:532
  35.6 1.3 %collective-permute-done.4.far_piece = bf16[32,69]{1,0:T(8,128)(2,1)S(1)} collective-permute-done((bf16[32,69]{1,0:T(8,128)(2,1)S(1)}, bf16[32,69]{1,0:T(8,128)(2,1)S(1)}, u32[]{:S(2)}, u32[]{:S(2)}) %collective-permute-start.4) | collective-permute-done | bytes 4448 | tf_op jit(solution)/shard_map/ppermute | solution.py:538
  36.8 0.0 collective-permute-done.5.lat_piece
  36.9 0.0 all-to-all-done
  36.9 0.0 copy-done
  36.9 1.4 %observe.1 = (f32[128,8]{1,0:T(8,128)}, f32[8,16,69]{2,1,0:T(8,128)S(1)}, bf16[32,69]{1,0:T(8,128)(2,1)S(1)}, bf16[32,69]{1,0:T(8,128)(2,1)S(1)}, bf16[32,69]{1,...) custom-call(f32[8,16,69]{2,1,0:T(8,128)S(1)} %copy-done, bf16[32,69]{1,0:T(8,128)(2,1)S(1)} %get-tuple-element.31.own_piece, ...), custom_call_target="tpu_custom_call" | custom-call | tf_op jit(solution)/shard_map/observe/pallas_call | solution.py:574
  38.3 1.4 %collective-permute-start.6 = (bf16[32,69]{1,0:T(8,128)(2,1)S(1)}, bf16[32,69]{1,0:T(8,128)(2,1)S(1)}, u32[]{:S(2)}, u32[]{:S(2)}) collective-permute-start(bf16[32,69]{1,0:T(8,128)(2,1)S(1)} %get-tuple-element.38), channel_id=1, source_target_pairs={{0,124},{4,0},{8,4},{12,8},{16,12},{20,16},{24,20},{28,24},{32,28}... | collective-permute-start | bytes 13256 | tf_op jit(solution)/shard_map/ppermute | solution.py:532
  39.7 2.5 %collective-permute-start.7 = (bf16[32,69]{1,0:T(8,128)(2,1)S(1)}, bf16[32,69]{1,0:T(8,128)(2,1)S(1)}, u32[]{:S(2)}, u32[]{:S(2)}) collective-permute-start(bf16[32,69]{1,0:T(8,128)(2,1)S(1)} %get-tuple-element.39), channel_id=1, source_target_pairs={{0,127},{1,124},{2,125},{3,126},{4,3},{5,0},{6,1},{7,2},{8,7},{9,4... | collective-permute-start | bytes 13256 | tf_op jit(solution)/shard_map/ppermute | solution.py:538
  42.2 0.0 collective-permute-start.8
  42.2 4.8 %all-to-all-start.1 = ((f32[128,1,8]{2,1,0:T(1,128)}), f32[128,1,8]{2,1,0:T(1,128)S(1)}, u32[]{:S(2)}, u32[]{:S(2)}) async-start(f32[128,1,8]{2,1,0:T(1,128)} %bitcast.16), calls=%async_computation.1 | async-start | bytes 131072 | tf_op jit(solution)/shard_map/all_to_all | solution.py:655
  47.1 0.0 collective-permute-done.6.lon_hbm
  47.1 0.0 collective-permute-done.7.far_hbm
  47.1 0.0 collective-permute-done.8.lat_hbm
  47.1 8.0 %adjoint.1 = (bf16[32,69]{1,0:T(8,128)(2,1)S(1)}, bf16[32,69]{1,0:T(8,128)(2,1)S(1)}, bf16[32,69]{1,0:T(8,128)(2,1)S(1)}, bf16[32,69]{1,0:T(8,128)(2,1)S(1)}) custom-call(bf16[32,69]{1,0:T(8,128)(2,1)S(1)} %get-tuple-element.37.own_hbm, bf16[32,69]{1,0:T(8,128)(2,1)S(1)} %collective-permute-done.6.lon_hbm, ...), custom_call_target="tpu_custom_call" | custom-call | flops 1500000000 | bytes 10000000 | tf_op jit(solution)/shard_map/adjoint/pallas_call | solution.py:590
  55.1 1.6 %collective-permute-start.9 = (bf16[32,69]{1,0:T(8,128)(2,1)S(1)}, bf16[32,69]{1,0:T(8,128)(2,1)S(1)}, u32[]{:S(2)}, u32[]{:S(2)}) collective-permute-start(bf16[32,69]{1,0:T(8,128)(2,1)S(1)} %get-tuple-element.46), channel_id=1, source_target_pairs={{0,4},{4,8},{8,12},{12,16},{16,20},{20,24},{24,28},{28,32},{32,36}... | collective-permute-start | bytes 13256 | tf_op jit(solution)/shard_map/ppermute | solution.py:532
  56.7 2.9 %collective-permute-start.10 = (bf16[32,69]{1,0:T(8,128)(2,1)S(1)}, bf16[32,69]{1,0:T(8,128)(2,1)S(1)}, u32[]{:S(2)}, u32[]{:S(2)}) collective-permute-start(bf16[32,69]{1,0:T(8,128)(2,1)S(1)} %get-tuple-element.47), channel_id=1, source_target_pairs={{0,5},{1,6},{2,7},{3,4},{4,9},{5,10},{6,11},{7,8},{8,13},{9,14},{1... | collective-permute-start | bytes 13256 | tf_op jit(solution)/shard_map/ppermute | solution.py:538
  59.6 0.0 collective-permute-start.11
  59.6 0.0 all-to-all-done.1
  59.6 0.0 copy-start.1
  59.6 0.6 copy-done.1
  60.3 1.6 %unpack.1 = f32[1,512]{1,0:T(1,128)} custom-call(s32[1,512]{1,0:T(1,128)} %bitcast.28, f32[1,512]{1,0:T(1,128)} %get-tuple-element.52.slots_ref, f32[128,8]{1,0:T(8,128)} %bitcast.24), custom_call_target="tpu_custom_call" | custom-call | tf_op jit(solution)/shard_map/unpack/pallas_call | solution.py:673
  61.9 2.3 %collective-permute-done.9 = bf16[32,69]{1,0:T(8,128)(2,1)S(1)} collective-permute-done((bf16[32,69]{1,0:T(8,128)(2,1)S(1)}, bf16[32,69]{1,0:T(8,128)(2,1)S(1)}, u32[]{:S(2)}, u32[]{:S(2)}) %collective-permute-start.9) | collective-permute-done | bytes 4448 | tf_op jit(solution)/shard_map/ppermute | solution.py:532
  64.2 1.3 %collective-permute-done.10 = bf16[32,69]{1,0:T(8,128)(2,1)S(1)} collective-permute-done((bf16[32,69]{1,0:T(8,128)(2,1)S(1)}, bf16[32,69]{1,0:T(8,128)(2,1)S(1)}, u32[]{:S(2)}, u32[]{:S(2)}) %collective-permute-start.10) | collective-permute-done | bytes 4448 | tf_op jit(solution)/shard_map/ppermute | solution.py:538
  65.5 0.0 collective-permute-done.11
  65.5 0.6 convert_add_fusion
Async XLA Ops:
  0.6 36.2 %copy-start = (f32[8,16,69]{2,1,0:T(8,128)S(1)}, f32[8,16,69]{2,1,0:T(8,128)}, u32[]{:S(2)}) copy-start(f32[8,16,69]{2,1,0:T(8,128)} %direction_ref.3) | copy-start | bytes 105988
  2.7 15.1 %collective-permute-start = (bf16[64,69]{1,0:T(8,128)(2,1)S(1)}, bf16[64,69]{1,0:T(8,128)(2,1)S(1)}, u32[]{:S(2)}, u32[]{:S(2)}) collective-permute-start(bf16[64,69]{1,0:T(8,128)(2,1)S(1)} %get-tuple-element.28), channel_id=1, source_target_pairs={{0,124},{4,0},{8,4},{12,8},{16,12},{20,16},{24,20},{28,24},{32,28}... | collective-permute-start | bytes 26504 | tf_op jit(solution)/shard_map/ppermute | solution.py:532
  12.2 5.6 %collective-permute-start.1 = (bf16[64,69]{1,0:T(8,128)(2,1)S(1)}, bf16[64,69]{1,0:T(8,128)(2,1)S(1)}, u32[]{:S(2)}, u32[]{:S(2)}) collective-permute-start(bf16[64,69]{1,0:T(8,128)(2,1)S(1)} %get-tuple-element.29), channel_id=1, source_target_pairs={{0,127},{1,124},{2,125},{3,126},{4,3},{5,0},{6,1},{7,2},{8,7},{9,4... | collective-permute-start | bytes 26504 | tf_op jit(solution)/shard_map/ppermute | solution.py:538
  13.2 4.7 %collective-permute-start.2 = (bf16[64,69]{1,0:T(8,128)(2,1)S(1)}, bf16[64,69]{1,0:T(8,128)(2,1)S(1)}, u32[]{:S(2)}, u32[]{:S(2)}) collective-permute-start(bf16[64,69]{1,0:T(8,128)(2,1)S(1)} %get-tuple-element.30), channel_id=1, source_target_pairs={{0,3},{1,0},{2,1},{3,2},{4,7},{5,4},{6,5},{7,6},{8,11},{9,8},{10,9... | collective-permute-start | bytes 26504 | tf_op jit(solution)/shard_map/ppermute | solution.py:531
  13.2 23.7 %all-to-all-start = ((f32[128,1,64]{2,1,0:T(1,128)}), f32[128,1,64]{2,1,0:T(1,128)S(1)}, u32[]{:S(2)}, u32[]{:S(2)}) async-start(f32[128,1,64]{2,1,0:T(1,128)} %bitcast.10), calls=%async_computation | async-start | bytes 131072 | tf_op jit(solution)/shard_map/all_to_all | solution.py:644
  26.5 9.1 %collective-permute-start.3 = (bf16[32,69]{1,0:T(8,128)(2,1)S(1)}, bf16[32,69]{1,0:T(8,128)(2,1)S(1)}, u32[]{:S(2)}, u32[]{:S(2)}) collective-permute-start(bf16[32,69]{1,0:T(8,128)(2,1)S(1)} %get-tuple-element.32), channel_id=1, source_target_pairs={{0,4},{4,8},{8,12},{12,16},{16,20},{20,24},{24,28},{28,32},{32,36}... | collective-permute-start | bytes 13256 | tf_op jit(solution)/shard_map/ppermute | solution.py:532
  28.0 8.8 %collective-permute-start.4 = (bf16[32,69]{1,0:T(8,128)(2,1)S(1)}, bf16[32,69]{1,0:T(8,128)(2,1)S(1)}, u32[]{:S(2)}, u32[]{:S(2)}) collective-permute-start(bf16[32,69]{1,0:T(8,128)(2,1)S(1)} %get-tuple-element.33), channel_id=1, source_target_pairs={{0,5},{1,6},{2,7},{3,4},{4,9},{5,10},{6,11},{7,8},{8,13},{9,14},{1... | collective-permute-start | bytes 13256 | tf_op jit(solution)/shard_map/ppermute | solution.py:538
  31.0 5.9 %collective-permute-start.5 = (bf16[32,69]{1,0:T(8,128)(2,1)S(1)}, bf16[32,69]{1,0:T(8,128)(2,1)S(1)}, u32[]{:S(2)}, u32[]{:S(2)}) collective-permute-start(bf16[32,69]{1,0:T(8,128)(2,1)S(1)} %get-tuple-element.34), channel_id=1, source_target_pairs={{0,1},{1,2},{2,3},{3,0},{4,5},{5,6},{6,7},{7,4},{8,9},{9,10},{10,1... | collective-permute-start | bytes 13256 | tf_op jit(solution)/shard_map/ppermute | solution.py:531
  38.3 8.8 %collective-permute-start.6 = (bf16[32,69]{1,0:T(8,128)(2,1)S(1)}, bf16[32,69]{1,0:T(8,128)(2,1)S(1)}, u32[]{:S(2)}, u32[]{:S(2)}) collective-permute-start(bf16[32,69]{1,0:T(8,128)(2,1)S(1)} %get-tuple-element.38), channel_id=1, source_target_pairs={{0,124},{4,0},{8,4},{12,8},{16,12},{20,16},{24,20},{28,24},{32,28}... | collective-permute-start | bytes 13256 | tf_op jit(solution)/shard_map/ppermute | solution.py:532
  39.7 7.4 %collective-permute-start.7 = (bf16[32,69]{1,0:T(8,128)(2,1)S(1)}, bf16[32,69]{1,0:T(8,128)(2,1)S(1)}, u32[]{:S(2)}, u32[]{:S(2)}) collective-permute-start(bf16[32,69]{1,0:T(8,128)(2,1)S(1)} %get-tuple-element.39), channel_id=1, source_target_pairs={{0,127},{1,124},{2,125},{3,126},{4,3},{5,0},{6,1},{7,2},{8,7},{9,4... | collective-permute-start | bytes 13256 | tf_op jit(solution)/shard_map/ppermute | solution.py:538
  42.2 4.9 %collective-permute-start.8 = (bf16[32,69]{1,0:T(8,128)(2,1)S(1)}, bf16[32,69]{1,0:T(8,128)(2,1)S(1)}, u32[]{:S(2)}, u32[]{:S(2)}) collective-permute-start(bf16[32,69]{1,0:T(8,128)(2,1)S(1)} %get-tuple-element.40), channel_id=1, source_target_pairs={{0,3},{1,0},{2,1},{3,2},{4,7},{5,4},{6,5},{7,6},{8,11},{9,8},{10,9... | collective-permute-start | bytes 13256 | tf_op jit(solution)/shard_map/ppermute | solution.py:531
  42.2 17.4 %all-to-all-start.1 = ((f32[128,1,8]{2,1,0:T(1,128)}), f32[128,1,8]{2,1,0:T(1,128)S(1)}, u32[]{:S(2)}, u32[]{:S(2)}) async-start(f32[128,1,8]{2,1,0:T(1,128)} %bitcast.16), calls=%async_computation.1 | async-start | bytes 131072 | tf_op jit(solution)/shard_map/all_to_all | solution.py:655
  55.1 9.1 %collective-permute-start.9 = (bf16[32,69]{1,0:T(8,128)(2,1)S(1)}, bf16[32,69]{1,0:T(8,128)(2,1)S(1)}, u32[]{:S(2)}, u32[]{:S(2)}) collective-permute-start(bf16[32,69]{1,0:T(8,128)(2,1)S(1)} %get-tuple-element.46), channel_id=1, source_target_pairs={{0,4},{4,8},{8,12},{12,16},{16,20},{20,24},{24,28},{28,32},{32,36}... | collective-permute-start | bytes 13256 | tf_op jit(solution)/shard_map/ppermute | solution.py:532
  56.7 8.8 %collective-permute-start.10 = (bf16[32,69]{1,0:T(8,128)(2,1)S(1)}, bf16[32,69]{1,0:T(8,128)(2,1)S(1)}, u32[]{:S(2)}, u32[]{:S(2)}) collective-permute-start(bf16[32,69]{1,0:T(8,128)(2,1)S(1)} %get-tuple-element.47), channel_id=1, source_target_pairs={{0,5},{1,6},{2,7},{3,4},{4,9},{5,10},{6,11},{7,8},{8,13},{9,14},{1... | collective-permute-start | bytes 13256 | tf_op jit(solution)/shard_map/ppermute | solution.py:538
  59.6 5.9 %collective-permute-start.11 = (bf16[32,69]{1,0:T(8,128)(2,1)S(1)}, bf16[32,69]{1,0:T(8,128)(2,1)S(1)}, u32[]{:S(2)}, u32[]{:S(2)}) collective-permute-start(bf16[32,69]{1,0:T(8,128)(2,1)S(1)} %get-tuple-element.48), channel_id=1, source_target_pairs={{0,1},{1,2},{2,3},{3,0},{4,5},{5,6},{6,7},{7,4},{8,9},{9,10},{10,1... | collective-permute-start | bytes 13256 | tf_op jit(solution)/shard_map/ppermute | solution.py:531
  59.6 0.6 copy-start.1

commit v7 on v6

--- a/solution.py
+++ b/solution.py
@@ -154,9 +154,9 @@
     logit_hbm,
     background_hbm,
     direction_hbm,
-    lon_hbm,
-    far_hbm,
-    lat_hbm,
+    lon_piece,
+    far_piece,
+    lat_piece,
     embed_hbm,
     gain_hbm,
     decode_gain_hbm,
@@ -176,9 +176,6 @@
     logit_ref,
     background_ref,
     direction_ref,
-    lon_piece,
-    far_piece,
-    lat_piece,
     embed_ref,
     gain_ref,
     decode_gain_ref,
@@ -208,9 +205,6 @@
     first_needed = [
         fetch(*pair)
         for pair in (
-            (lat_hbm, lat_piece),
-            (lon_hbm, lon_piece),
-            (far_hbm, far_piece),
             (background_hbm, background_ref),
             (direction_hbm, direction_ref),
             (embed_hbm, embed_ref),
@@ -399,14 +393,14 @@
 
 
 def adjoint_kernel(
-    own_hbm,
-    lon_hbm,
-    far_hbm,
-    lat_hbm,
+    own_piece,
+    lon_piece,
+    far_piece,
+    lat_piece,
+    decode_ref,
+    decode_gain_ref,
+    logit_ref,
     block_hbm,
-    decode_hbm,
-    decode_gain_hbm,
-    logit_hbm,
     outw_hbm,
     units_hbm,
     probs_hbm,
@@ -419,14 +413,7 @@
     lat_out,
     lon_out,
     far_out,
-    own_piece,
-    lon_piece,
-    far_piece,
-    lat_piece,
     block_ref,
-    decode_ref,
-    decode_gain_ref,
-    logit_ref,
     outw_ref,
     units_ref,
     probs_ref,
@@ -448,14 +435,7 @@
         fetched.append(copy)
 
     for source, target in (
-        (own_hbm, own_piece),
-        (lon_hbm, lon_piece),
-        (far_hbm, far_piece),
-        (lat_hbm, lat_piece),
         (block_hbm, block_ref),
-        (decode_hbm, decode_ref),
-        (decode_gain_hbm, decode_gain_ref),
-        (logit_hbm, logit_ref),
         (outw_hbm, outw_ref),
         (units_hbm, units_ref),
         (probs_hbm, probs_ref),
@@ -471,19 +451,19 @@
         for copy in fetched[start:stop]:
             copy.wait()
 
-    wait(0, 8)
+    wait(0, 1)
     change = quadrants(*[piece[...].astype(f32) for piece in (own_piece, lat_piece, lon_piece, far_piece)])
     unit, scale = normed_rows(block_ref[...].astype(f32))
     normed_ct = product(change.astype(bf16), decode_ref[...], NN).astype(bf16).astype(f32) * decode_gain_ref[...]
     block_ct = norm_tangent(unit, scale, normed_ct).astype(bf16)
-    wait(8, 9)
+    wait(1, 2)
     mixed_ct = product(block_ct, outw_ref[...], NT).astype(bf16)
 
     lane = lax.broadcasted_iota(jnp.int32, (1, 128), 1)
     first = lane < 64
     same_head = same_head_block()
     logits = logit_ref[...]
-    wait(9, 15)
+    wait(2, 8)
     for quad in range(quads):
         cotangents = []
         for side in range(2):
@@ -512,7 +492,7 @@
         packed_ref[:, pl.ds(width + quad * QUAD, QUAD)] = raw_ct[CELLS:]
 
     unit, scale = normed_rows(hidden_ref[...].astype(f32))
-    wait(15, 16)
+    wait(8, 9)
     normed_ct = product(packed_ref[...], qkv_ref[...], NT).astype(bf16).astype(f32) * gain_ref[...]
     hidden_ct = (norm_tangent(unit, scale, normed_ct) + block_ct.astype(f32)).astype(bf16)
     state = product(hidden_ct, embed_ref[...], NT)
@@ -557,9 +537,9 @@
     return pl.pallas_call(
         forward_kernel,
         out_shape=[pltpu.VMEM(quarter.shape, bf16)] * 4 + kept,
-        in_specs=[ANY] * 13,
+        in_specs=[ANY] * 4 + [VMEM] * 3 + [ANY] * 6,
         out_specs=[VMEM] * 4 + [ANY] * 5,
-        scratch_shapes=[pltpu.VMEM(item.shape, item.dtype) for item in inputs]
+        scratch_shapes=[pltpu.VMEM(item.shape, item.dtype) for item in (*inputs[:4], *inputs[7:])]
         + [both, both]
         + [pltpu.VMEM(item.shape, item.dtype) for item in kept[2:]]
         + [both, pltpu.SemaphoreType.DMA((18,)), pltpu.SemaphoreType.DMA((5,))],
@@ -584,19 +564,21 @@
 def run_adjoint(logit_scale, pieces, embed_weight, gain, decode_gain, decode_rows, kept, qkv_weight, out_weight):
     hidden, block, units, scales, probs = kept
     width = embed_weight.shape[1]
-    pieces = [pltpu.with_memory_space_constraint(piece, pltpu.VMEM) for piece in pieces]
-    inputs = (*pieces, block, decode_rows, decode_gain, logit_scale, out_weight, units, probs, scales)
-    inputs = (*inputs, hidden, gain, embed_weight, qkv_weight)
+    near = [
+        pltpu.with_memory_space_constraint(item, pltpu.VMEM)
+        for item in (*pieces, decode_rows, decode_gain, logit_scale)
+    ]
+    late = (block, out_weight, units, probs, scales, hidden, gain, embed_weight, qkv_weight)
     return pl.pallas_call(
         adjoint_kernel,
         out_shape=[pltpu.VMEM(pieces[0].shape, bf16)] * 4,
-        in_specs=[ANY] * len(inputs),
+        in_specs=[VMEM] * len(near) + [ANY] * len(late),
         out_specs=[VMEM] * 4,
-        scratch_shapes=[pltpu.VMEM(item.shape, item.dtype) for item in inputs]
-        + [pltpu.VMEM((CELLS, 3 * width), bf16), pltpu.SemaphoreType.DMA((len(inputs),))],
+        scratch_shapes=[pltpu.VMEM(item.shape, item.dtype) for item in late]
+        + [pltpu.VMEM((CELLS, 3 * width), bf16), pltpu.SemaphoreType.DMA((len(late),))],
         cost_estimate=pl.CostEstimate(flops=1_500_000_000, bytes_accessed=10_000_000, transcendentals=300_000),
         name="adjoint",
-    )(*inputs)
+    )(*near, *late)
 
 
 def per_device(

time: 66.4 us -> 66.2 us (level)
  transfers between devices with their start and end apart: 14 -> 14, of which waited for: 4 -> 4; matrix products, arithmetic and copies ran while one was open for 0% -> 0% of each run, Pallas kernels for 28% -> 27%
where the time goes in v7:
time: 66.2 us; the launch traced here: 66 us
  starting transfers between devices  32.9 us (50%)
  Pallas kernels  21.5 us (32%)
  waiting for transfers between devices  9.48 us (14%)
  between operations  0.79 us (1%)
    ppermute x4, starting transfers between devices, exchanged(): lax.ppermute(lon_piece, 'lon', [(i, (i + steps) % lon_count) for i in ran...  14 us
    ppermute x4, starting transfers between devices, exchanged(): far_piece = lax.ppermute(far_piece, ('lon', 'lat'), pairs)  9.3 us
    pallas_call x1, Pallas kernels, run_forward(): pl.pallas_call(forward_kernel, out_shape=[pltpu.VMEM(quarter.shape, bf16)...  8.54 us
    pallas_call x1, Pallas kernels, run_adjoint(): pl.pallas_call(adjoint_kernel, out_shape=[pltpu.VMEM(pieces[0].shape, bf1...  7.8 us
    ppermute x4, waiting for transfers between devices, exchanged(): lax.ppermute(lon_piece, 'lon', [(i, (i + steps) % lon_count) for i in ran...  6.94 us
    all_to_all x1, starting transfers between devices, per_device(): lax.all_to_all(at_obs, ('lon', 'lat'), split_axis=0, concat_axis=0, tiled...  4.83 us
    all_to_all x1, starting transfers between devices, per_device(): lax.all_to_all(outgoing, ('lon', 'lat'), split_axis=0, concat_axis=0, til...  4.64 us
    ppermute x4, waiting for transfers between devices, exchanged(): far_piece = lax.ppermute(far_piece, ('lon', 'lat'), pairs)  2.53 us
  transfers between devices with their start and end apart: 14, of which 4 were waited for; matrix products, arithmetic and copies ran while one was open for 0% of the time, Pallas kernels for 27%

profile of v7, /device:TPU:1, one launch (start us, length us, event | category | flops | bytes accessed | tf_op | source)
XLA Modules:
  0.0 66.0 jit_solution(17753520197635395931)
XLA Ops:
  0.6 0.0 copy-start
  0.6 0.0 copy-start.1
  0.7 0.0 copy-start.2
  0.7 0.0 copy-start.3
  0.7 2.1 %prepare.1 = (bf16[64,69]{1,0:T(8,128)(2,1)S(1)}, bf16[64,69]{1,0:T(8,128)(2,1)S(1)}, bf16[64,69]{1,0:T(8,128)(2,1)S(1)}, f32[128,64]{1,0:T(8,128)}, f32[1,512]{1,0:T(1,128)}) custom-call(f32[8,16,69]{2,1,0:T(8,128)} %background_hbm.1, f32[8,16,69]{2,1,0:T(8,128)} %direction_ref.3, s32[1,512]{1,0:T(1,128)} %bitcast.31, s32[1,512]{1,0:T(1,128)} %bitcast.39, ...), custom_call_target="tpu_custom_call" | custom-call | tf_op jit(solution)/shard_map/prepare/pallas_call | solution.py:610
  2.8 9.5 %collective-permute-start = (bf16[64,69]{1,0:T(8,128)(2,1)S(1)}, bf16[64,69]{1,0:T(8,128)(2,1)S(1)}, u32[]{:S(2)}, u32[]{:S(2)}) collective-permute-start(bf16[64,69]{1,0:T(8,128)(2,1)S(1)} %get-tuple-element.28), channel_id=1, source_target_pairs={{0,124},{4,0},{8,4},{12,8},{16,12},{20,16},{24,20},{28,24},{32,28}... | collective-permute-start | bytes 26504 | tf_op jit(solution)/shard_map/ppermute | solution.py:512
  12.3 1.0 %collective-permute-start.1 = (bf16[64,69]{1,0:T(8,128)(2,1)S(1)}, bf16[64,69]{1,0:T(8,128)(2,1)S(1)}, u32[]{:S(2)}, u32[]{:S(2)}) collective-permute-start(bf16[64,69]{1,0:T(8,128)(2,1)S(1)} %get-tuple-element.29), channel_id=1, source_target_pairs={{0,127},{1,124},{2,125},{3,126},{4,3},{5,0},{6,1},{7,2},{8,7},{9,4... | collective-permute-start | bytes 26504 | tf_op jit(solution)/shard_map/ppermute | solution.py:518
  13.3 0.0 collective-permute-start.2
  13.3 4.6 %all-to-all-start = ((f32[128,1,64]{2,1,0:T(1,128)}), f32[128,1,64]{2,1,0:T(1,128)S(1)}, u32[]{:S(2)}, u32[]{:S(2)}) async-start(f32[128,1,64]{2,1,0:T(1,128)} %bitcast.10), calls=%async_computation | async-start | bytes 131072 | tf_op jit(solution)/shard_map/all_to_all | solution.py:626
  17.9 0.0 collective-permute-done.lon_piece
  17.9 0.0 collective-permute-done.1.far_piece
  17.9 0.0 collective-permute-done.2.lat_piece
  18.0 8.5 %forward.1 = (bf16[32,69]{1,0:T(8,128)(2,1)S(1)}, bf16[32,69]{1,0:T(8,128)(2,1)S(1)}, bf16[32,69]{1,0:T(8,128)(2,1)S(1)}, bf16[32,69]{1,0:T(8,128)(2,1)S(1)}, bf...) custom-call(f32[1,1]{1,0:T(1,128)} %bitcast.band_hbm, ...), custom_call_target="tpu_custom_call" | custom-call | flops 2500000000 | bytes 10000000 | tf_op jit(solution)/shard_map/forward/pallas_call | solution.py:537
  26.5 1.6 %collective-permute-start.3 = (bf16[32,69]{1,0:T(8,128)(2,1)S(1)}, bf16[32,69]{1,0:T(8,128)(2,1)S(1)}, u32[]{:S(2)}, u32[]{:S(2)}) collective-permute-start(bf16[32,69]{1,0:T(8,128)(2,1)S(1)} %get-tuple-element.32), channel_id=1, source_target_pairs={{0,4},{4,8},{8,12},{12,16},{16,20},{20,24},{24,28},{28,32},{32,36}... | collective-permute-start | bytes 13256 | tf_op jit(solution)/shard_map/ppermute | solution.py:512
  28.1 2.9 %collective-permute-start.4 = (bf16[32,69]{1,0:T(8,128)(2,1)S(1)}, bf16[32,69]{1,0:T(8,128)(2,1)S(1)}, u32[]{:S(2)}, u32[]{:S(2)}) collective-permute-start(bf16[32,69]{1,0:T(8,128)(2,1)S(1)} %get-tuple-element.33), channel_id=1, source_target_pairs={{0,5},{1,6},{2,7},{3,4},{4,9},{5,10},{6,11},{7,8},{8,13},{9,14},{1... | collective-permute-start | bytes 13256 | tf_op jit(solution)/shard_map/ppermute | solution.py:518
  31.0 0.0 collective-permute-start.5
  31.0 4.6 %collective-permute-done.3.lon_piece = bf16[32,69]{1,0:T(8,128)(2,1)S(1)} collective-permute-done((bf16[32,69]{1,0:T(8,128)(2,1)S(1)}, bf16[32,69]{1,0:T(8,128)(2,1)S(1)}, u32[]{:S(2)}, u32[]{:S(2)}) %collective-permute-start.3) | collective-permute-done | bytes 4448 | tf_op jit(solution)/shard_map/ppermute | solution.py:512
  35.6 1.3 %collective-permute-done.4.far_piece = bf16[32,69]{1,0:T(8,128)(2,1)S(1)} collective-permute-done((bf16[32,69]{1,0:T(8,128)(2,1)S(1)}, bf16[32,69]{1,0:T(8,128)(2,1)S(1)}, u32[]{:S(2)}, u32[]{:S(2)}) %collective-permute-start.4) | collective-permute-done | bytes 4448 | tf_op jit(solution)/shard_map/ppermute | solution.py:518
  36.9 0.0 collective-permute-done.5.lat_piece
  36.9 0.0 all-to-all-done
  36.9 0.0 copy-done
  36.9 1.4 %observe.1 = (f32[128,8]{1,0:T(8,128)}, f32[8,16,69]{2,1,0:T(8,128)S(1)}, bf16[32,69]{1,0:T(8,128)(2,1)S(1)}, bf16[32,69]{1,0:T(8,128)(2,1)S(1)}, bf16[32,69]{1,...) custom-call(f32[8,16,69]{2,1,0:T(8,128)S(1)} %copy-done, bf16[32,69]{1,0:T(8,128)(2,1)S(1)} %get-tuple-element.31.own_piece, ...), custom_call_target="tpu_custom_call" | custom-call | tf_op jit(solution)/shard_map/observe/pallas_call | solution.py:554
  38.3 1.4 %collective-permute-start.6 = (bf16[32,69]{1,0:T(8,128)(2,1)S(1)}, bf16[32,69]{1,0:T(8,128)(2,1)S(1)}, u32[]{:S(2)}, u32[]{:S(2)}) collective-permute-start(bf16[32,69]{1,0:T(8,128)(2,1)S(1)} %get-tuple-element.38), channel_id=1, source_target_pairs={{0,124},{4,0},{8,4},{12,8},{16,12},{20,16},{24,20},{28,24},{32,28}... | collective-permute-start | bytes 13256 | tf_op jit(solution)/shard_map/ppermute | solution.py:512
  39.7 2.5 %collective-permute-start.7 = (bf16[32,69]{1,0:T(8,128)(2,1)S(1)}, bf16[32,69]{1,0:T(8,128)(2,1)S(1)}, u32[]{:S(2)}, u32[]{:S(2)}) collective-permute-start(bf16[32,69]{1,0:T(8,128)(2,1)S(1)} %get-tuple-element.39), channel_id=1, source_target_pairs={{0,127},{1,124},{2,125},{3,126},{4,3},{5,0},{6,1},{7,2},{8,7},{9,4... | collective-permute-start | bytes 13256 | tf_op jit(solution)/shard_map/ppermute | solution.py:518
  42.2 0.0 collective-permute-start.8
  42.2 4.8 %all-to-all-start.1 = ((f32[128,1,8]{2,1,0:T(1,128)}), f32[128,1,8]{2,1,0:T(1,128)S(1)}, u32[]{:S(2)}, u32[]{:S(2)}) async-start(f32[128,1,8]{2,1,0:T(1,128)} %bitcast.16), calls=%async_computation.1 | async-start | bytes 131072 | tf_op jit(solution)/shard_map/all_to_all | solution.py:637
  47.1 0.0 collective-permute-done.6.lon_piece
  47.1 0.0 collective-permute-done.7.far_piece
  47.1 0.0 collective-permute-done.8.lat_piece
  47.1 0.0 copy-done.1
  47.1 0.0 copy-done.2
  47.1 0.0 copy-done.3
  47.1 7.8 %adjoint.1 = (bf16[32,69]{1,0:T(8,128)(2,1)S(1)}, bf16[32,69]{1,0:T(8,128)(2,1)S(1)}, bf16[32,69]{1,0:T(8,128)(2,1)S(1)}, bf16[32,69]{1,0:T(8,128)(2,1)S(1)}) custom-call(bf16[32,69]{1,0:T(8,128)(2,1)S(1)} %get-tuple-element.37.own_piece, bf16[32,69]{1,0:T(8,128)(2,1)S(1)} %collective-permute-done.6.lon_piece, ...), custom_call_target="tpu_custom_call" | custom-call | flops 1500000000 | bytes 10000000 | tf_op jit(solution)/shard_map/adjoint/pallas_call | solution.py:572
  54.9 1.6 %collective-permute-start.9 = (bf16[32,69]{1,0:T(8,128)(2,1)S(1)}, bf16[32,69]{1,0:T(8,128)(2,1)S(1)}, u32[]{:S(2)}, u32[]{:S(2)}) collective-permute-start(bf16[32,69]{1,0:T(8,128)(2,1)S(1)} %get-tuple-element.46), channel_id=1, source_target_pairs={{0,4},{4,8},{8,12},{12,16},{16,20},{20,24},{24,28},{28,32},{32,36}... | collective-permute-start | bytes 13256 | tf_op jit(solution)/shard_map/ppermute | solution.py:512
  56.5 2.9 %collective-permute-start.10 = (bf16[32,69]{1,0:T(8,128)(2,1)S(1)}, bf16[32,69]{1,0:T(8,128)(2,1)S(1)}, u32[]{:S(2)}, u32[]{:S(2)}) collective-permute-start(bf16[32,69]{1,0:T(8,128)(2,1)S(1)} %get-tuple-element.47), channel_id=1, source_target_pairs={{0,5},{1,6},{2,7},{3,4},{4,9},{5,10},{6,11},{7,8},{8,13},{9,14},{1... | collective-permute-start | bytes 13256 | tf_op jit(solution)/shard_map/ppermute | solution.py:518
  59.4 0.0 collective-permute-start.11
  59.4 0.0 all-to-all-done.1
  59.4 0.0 copy-start.4
  59.4 0.6 copy-done.4
  60.1 1.6 %unpack.1 = f32[1,512]{1,0:T(1,128)} custom-call(s32[1,512]{1,0:T(1,128)} %bitcast.32, f32[1,512]{1,0:T(1,128)} %get-tuple-element.52.slots_ref, f32[128,8]{1,0:T(8,128)} %bitcast.30), custom_call_target="tpu_custom_call" | custom-call | tf_op jit(solution)/shard_map/unpack/pallas_call | solution.py:655
  61.7 2.3 %collective-permute-done.9 = bf16[32,69]{1,0:T(8,128)(2,1)S(1)} collective-permute-done((bf16[32,69]{1,0:T(8,128)(2,1)S(1)}, bf16[32,69]{1,0:T(8,128)(2,1)S(1)}, u32[]{:S(2)}, u32[]{:S(2)}) %collective-permute-start.9) | collective-permute-done | bytes 4448 | tf_op jit(solution)/shard_map/ppermute | solution.py:512
  64.0 1.3 %collective-permute-done.10 = bf16[32,69]{1,0:T(8,128)(2,1)S(1)} collective-permute-done((bf16[32,69]{1,0:T(8,128)(2,1)S(1)}, bf16[32,69]{1,0:T(8,128)(2,1)S(1)}, u32[]{:S(2)}, u32[]{:S(2)}) %collective-permute-start.10) | collective-permute-done | bytes 4448 | tf_op jit(solution)/shard_map/ppermute | solution.py:518
  65.3 0.0 collective-permute-done.11
  65.3 0.6 convert_add_fusion
Async XLA Ops:
  0.6 36.3 %copy-start = (f32[8,16,69]{2,1,0:T(8,128)S(1)}, f32[8,16,69]{2,1,0:T(8,128)}, u32[]{:S(2)}) copy-start(f32[8,16,69]{2,1,0:T(8,128)} %direction_ref.3) | copy-start | bytes 105988
  0.6 46.4 %copy-start.1 = (bf16[1024,69]{0,1:T(8,128)(2,1)S(1)}, bf16[1024,69]{0,1:T(8,128)(2,1)}, u32[]{:S(2)}) copy-start(bf16[1024,69]{0,1:T(8,128)(2,1)} %param.25) | copy-start | bytes 423940
  0.7 46.4 %copy-start.2 = (f32[1024]{0:T(1024)S(1)}, f32[1024]{0:T(1024)}, u32[]{:S(2)}) copy-start(f32[1024]{0:T(1024)} %param.24) | copy-start | bytes 12292
  0.7 46.4 %copy-start.3 = (f32[16]{0:T(128)S(1)}, f32[16]{0:T(128)}, u32[]{:S(2)}) copy-start(f32[16]{0:T(128)} %param.22) | copy-start | bytes 196
  2.8 15.1 %collective-permute-start = (bf16[64,69]{1,0:T(8,128)(2,1)S(1)}, bf16[64,69]{1,0:T(8,128)(2,1)S(1)}, u32[]{:S(2)}, u32[]{:S(2)}) collective-permute-start(bf16[64,69]{1,0:T(8,128)(2,1)S(1)} %get-tuple-element.28), channel_id=1, source_target_pairs={{0,124},{4,0},{8,4},{12,8},{16,12},{20,16},{24,20},{28,24},{32,28}... | collective-permute-start | bytes 26504 | tf_op jit(solution)/shard_map/ppermute | solution.py:512
  12.3 5.6 %collective-permute-start.1 = (bf16[64,69]{1,0:T(8,128)(2,1)S(1)}, bf16[64,69]{1,0:T(8,128)(2,1)S(1)}, u32[]{:S(2)}, u32[]{:S(2)}) collective-permute-start(bf16[64,69]{1,0:T(8,128)(2,1)S(1)} %get-tuple-element.29), channel_id=1, source_target_pairs={{0,127},{1,124},{2,125},{3,126},{4,3},{5,0},{6,1},{7,2},{8,7},{9,4... | collective-permute-start | bytes 26504 | tf_op jit(solution)/shard_map/ppermute | solution.py:518
  13.3 4.7 %collective-permute-start.2 = (bf16[64,69]{1,0:T(8,128)(2,1)S(1)}, bf16[64,69]{1,0:T(8,128)(2,1)S(1)}, u32[]{:S(2)}, u32[]{:S(2)}) collective-permute-start(bf16[64,69]{1,0:T(8,128)(2,1)S(1)} %get-tuple-element.30), channel_id=1, source_target_pairs={{0,3},{1,0},{2,1},{3,2},{4,7},{5,4},{6,5},{7,6},{8,11},{9,8},{10,9... | collective-permute-start | bytes 26504 | tf_op jit(solution)/shard_map/ppermute | solution.py:511
  13.3 23.6 %all-to-all-start = ((f32[128,1,64]{2,1,0:T(1,128)}), f32[128,1,64]{2,1,0:T(1,128)S(1)}, u32[]{:S(2)}, u32[]{:S(2)}) async-start(f32[128,1,64]{2,1,0:T(1,128)} %bitcast.10), calls=%async_computation | async-start | bytes 131072 | tf_op jit(solution)/shard_map/all_to_all | solution.py:626
  26.5 9.1 %collective-permute-start.3 = (bf16[32,69]{1,0:T(8,128)(2,1)S(1)}, bf16[32,69]{1,0:T(8,128)(2,1)S(1)}, u32[]{:S(2)}, u32[]{:S(2)}) collective-permute-start(bf16[32,69]{1,0:T(8,128)(2,1)S(1)} %get-tuple-element.32), channel_id=1, source_target_pairs={{0,4},{4,8},{8,12},{12,16},{16,20},{20,24},{24,28},{28,32},{32,36}... | collective-permute-start | bytes 13256 | tf_op jit(solution)/shard_map/ppermute | solution.py:512
  28.1 8.8 %collective-permute-start.4 = (bf16[32,69]{1,0:T(8,128)(2,1)S(1)}, bf16[32,69]{1,0:T(8,128)(2,1)S(1)}, u32[]{:S(2)}, u32[]{:S(2)}) collective-permute-start(bf16[32,69]{1,0:T(8,128)(2,1)S(1)} %get-tuple-element.33), channel_id=1, source_target_pairs={{0,5},{1,6},{2,7},{3,4},{4,9},{5,10},{6,11},{7,8},{8,13},{9,14},{1... | collective-permute-start | bytes 13256 | tf_op jit(solution)/shard_map/ppermute | solution.py:518
  31.0 5.9 %collective-permute-start.5 = (bf16[32,69]{1,0:T(8,128)(2,1)S(1)}, bf16[32,69]{1,0:T(8,128)(2,1)S(1)}, u32[]{:S(2)}, u32[]{:S(2)}) collective-permute-start(bf16[32,69]{1,0:T(8,128)(2,1)S(1)} %get-tuple-element.34), channel_id=1, source_target_pairs={{0,1},{1,2},{2,3},{3,0},{4,5},{5,6},{6,7},{7,4},{8,9},{9,10},{10,1... | collective-permute-start | bytes 13256 | tf_op jit(solution)/shard_map/ppermute | solution.py:511
  38.3 8.8 %collective-permute-start.6 = (bf16[32,69]{1,0:T(8,128)(2,1)S(1)}, bf16[32,69]{1,0:T(8,128)(2,1)S(1)}, u32[]{:S(2)}, u32[]{:S(2)}) collective-permute-start(bf16[32,69]{1,0:T(8,128)(2,1)S(1)} %get-tuple-element.38), channel_id=1, source_target_pairs={{0,124},{4,0},{8,4},{12,8},{16,12},{20,16},{24,20},{28,24},{32,28}... | collective-permute-start | bytes 13256 | tf_op jit(solution)/shard_map/ppermute | solution.py:512
  39.7 7.4 %collective-permute-start.7 = (bf16[32,69]{1,0:T(8,128)(2,1)S(1)}, bf16[32,69]{1,0:T(8,128)(2,1)S(1)}, u32[]{:S(2)}, u32[]{:S(2)}) collective-permute-start(bf16[32,69]{1,0:T(8,128)(2,1)S(1)} %get-tuple-element.39), channel_id=1, source_target_pairs={{0,127},{1,124},{2,125},{3,126},{4,3},{5,0},{6,1},{7,2},{8,7},{9,4... | collective-permute-start | bytes 13256 | tf_op jit(solution)/shard_map/ppermute | solution.py:518
  42.2 4.9 %collective-permute-start.8 = (bf16[32,69]{1,0:T(8,128)(2,1)S(1)}, bf16[32,69]{1,0:T(8,128)(2,1)S(1)}, u32[]{:S(2)}, u32[]{:S(2)}) collective-permute-start(bf16[32,69]{1,0:T(8,128)(2,1)S(1)} %get-tuple-element.40), channel_id=1, source_target_pairs={{0,3},{1,0},{2,1},{3,2},{4,7},{5,4},{6,5},{7,6},{8,11},{9,8},{10,9... | collective-permute-start | bytes 13256 | tf_op jit(solution)/shard_map/ppermute | solution.py:511
  42.2 17.2 %all-to-all-start.1 = ((f32[128,1,8]{2,1,0:T(1,128)}), f32[128,1,8]{2,1,0:T(1,128)S(1)}, u32[]{:S(2)}, u32[]{:S(2)}) async-start(f32[128,1,8]{2,1,0:T(1,128)} %bitcast.16), calls=%async_computation.1 | async-start | bytes 131072 | tf_op jit(solution)/shard_map/all_to_all | solution.py:637
  54.9 9.1 %collective-permute-start.9 = (bf16[32,69]{1,0:T(8,128)(2,1)S(1)}, bf16[32,69]{1,0:T(8,128)(2,1)S(1)}, u32[]{:S(2)}, u32[]{:S(2)}) collective-permute-start(bf16[32,69]{1,0:T(8,128)(2,1)S(1)} %get-tuple-element.46), channel_id=1, source_target_pairs={{0,4},{4,8},{8,12},{12,16},{16,20},{20,24},{24,28},{28,32},{32,36}... | collective-permute-start | bytes 13256 | tf_op jit(solution)/shard_map/ppermute | solution.py:512
  56.5 8.8 %collective-permute-start.10 = (bf16[32,69]{1,0:T(8,128)(2,1)S(1)}, bf16[32,69]{1,0:T(8,128)(2,1)S(1)}, u32[]{:S(2)}, u32[]{:S(2)}) collective-permute-start(bf16[32,69]{1,0:T(8,128)(2,1)S(1)} %get-tuple-element.47), channel_id=1, source_target_pairs={{0,5},{1,6},{2,7},{3,4},{4,9},{5,10},{6,11},{7,8},{8,13},{9,14},{1... | collective-permute-start | bytes 13256 | tf_op jit(solution)/shard_map/ppermute | solution.py:518
  59.4 5.9 %collective-permute-start.11 = (bf16[32,69]{1,0:T(8,128)(2,1)S(1)}, bf16[32,69]{1,0:T(8,128)(2,1)S(1)}, u32[]{:S(2)}, u32[]{:S(2)}) collective-permute-start(bf16[32,69]{1,0:T(8,128)(2,1)S(1)} %get-tuple-element.48), channel_id=1, source_target_pairs={{0,1},{1,2},{2,3},{3,0},{4,5},{5,6},{6,7},{7,4},{8,9},{9,10},{10,1... | collective-permute-start | bytes 13256 | tf_op jit(solution)/shard_map/ppermute | solution.py:511
  59.4 0.6 copy-start.4

commit v8 on v7

--- a/solution.py
+++ b/solution.py
@@ -96,11 +96,18 @@
 
 def slots_of(owners, rows, devices):
     owner_hot = (lax.broadcasted_iota(jnp.int32, (devices, rows), 0) == owners).astype(f32)
+    block = 128
     upper = (
-        lax.broadcasted_iota(jnp.int32, (rows, rows), 0) <= lax.broadcasted_iota(jnp.int32, (rows, rows), 1)
+        lax.broadcasted_iota(jnp.int32, (block, block), 0) <= lax.broadcasted_iota(jnp.int32, (block, block), 1)
     ).astype(bf16)
-    counted = product(owner_hot.astype(bf16), upper, NN)
-    slots = jnp.sum(counted * owner_hot, axis=0, keepdims=True) - 1.0
+    before = jnp.zeros((devices, 1), f32)
+    slots = []
+    for start in range(0, rows, block):
+        here = owner_hot[:, start : start + block]
+        counted = product(here.astype(bf16), upper, NN) + before
+        slots.append(jnp.sum(counted * here, axis=0, keepdims=True) - 1.0)
+        before = counted[:, block - 1 : block]
+    slots = jnp.concatenate(slots, axis=1)
     return owner_hot, slots
 
 
@@ -610,7 +617,7 @@
     *strips, outgoing, slots = pl.pallas_call(
         prepare_kernel,
         out_shape=[pltpu.VMEM((2 * QUARTER, var_count), bf16)] * 3
-        + [pltpu.VMEM((devices, SLOTS * 8), f32), shape((1, obs_rows), f32)],
+        + [pltpu.VMEM((devices, SLOTS * 8), f32), pltpu.VMEM((1, obs_rows), f32)],
         in_specs=[VMEM] * 6,
         out_specs=[VMEM] * 5,
         name="prepare",
@@ -658,7 +665,7 @@
         in_specs=[VMEM] * 3,
         out_specs=VMEM,
         name="unpack",
-    )(owners, slots, returned)
+    )(owners, *(pltpu.with_memory_space_constraint(item, pltpu.VMEM) for item in (slots, returned)))
     return (hvp, obs_increment.reshape(obs_rows))
 
 

time: 66.2 us -> 66.2 us (level)
  waiting for transfers between devices: 9.48 us -> 10.3 us
    ppermute x4, waiting for transfers between devices: 6.94 us -> 7.75 us  [exchanged(): lax.ppermute(lon_piece, 'lon', [(i, (i + steps) % lon_count) for i in ran...]
where the time goes in v8:
time: 66.2 us; the launch traced here: 66 us
  starting transfers between devices  32.9 us (50%)
  Pallas kernels  21.4 us (32%)
  waiting for transfers between devices  10.3 us (16%)
  between operations  0.79 us (1%)
    ppermute x4, starting transfers between devices, exchanged(): lax.ppermute(lon_piece, 'lon', [(i, (i + steps) % lon_count) for i in ran...  14.1 us
    ppermute x4, starting transfers between devices, exchanged(): far_piece = lax.ppermute(far_piece, ('lon', 'lat'), pairs)  9.3 us
    pallas_call x1, Pallas kernels, run_forward(): pl.pallas_call(forward_kernel, out_shape=[pltpu.VMEM(quarter.shape, bf16)...  8.53 us
    pallas_call x1, Pallas kernels, run_adjoint(): pl.pallas_call(adjoint_kernel, out_shape=[pltpu.VMEM(pieces[0].shape, bf1...  7.8 us
    ppermute x4, waiting for transfers between devices, exchanged(): lax.ppermute(lon_piece, 'lon', [(i, (i + steps) % lon_count) for i in ran...  7.75 us
    all_to_all x1, starting transfers between devices, per_device(): lax.all_to_all(at_obs, ('lon', 'lat'), split_axis=0, concat_axis=0, tiled...  4.83 us
    all_to_all x1, starting transfers between devices, per_device(): lax.all_to_all(outgoing, ('lon', 'lat'), split_axis=0, concat_axis=0, til...  4.64 us
    ppermute x4, waiting for transfers between devices, exchanged(): far_piece = lax.ppermute(far_piece, ('lon', 'lat'), pairs)  2.52 us
  transfers between devices with their start and end apart: 14, of which 4 were waited for; matrix products, arithmetic and copies ran while one was open for 0% of the time, Pallas kernels for 27%

profile of v8, /device:TPU:1, one launch (start us, length us, event | category | flops | bytes accessed | tf_op | source)
XLA Modules:
  0.0 66.0 jit_solution(3479597120727274103)
XLA Ops:
  0.6 0.0 copy-start
  0.6 0.0 copy-start.1
  0.7 0.0 copy-start.2
  0.7 0.0 copy-start.3
  0.7 2.2 %prepare.1 = (bf16[64,69]{1,0:T(8,128)(2,1)S(1)}, bf16[64,69]{1,0:T(8,128)(2,1)S(1)}, bf16[64,69]{1,0:T(8,128)(2,1)S(1)}, f32[128,64]{1,0:T(8,128)}, f32[1,512]{1,0:T(1,128)S(1)}) custom-call(f32[8,16,69]{2,1,0:T(8,128)} %background_hbm.1, f32[8,16,69]{2,1,0:T(8,128)} %direction_ref.3, s32[1,512]{1,0:T(1,128)} %bitcast.31, s32[1,512]{1,0:T(1,128)} %bitcast.39, ...), custom_call_target="tpu_custom_call" | custom-call | tf_op jit(solution)/shard_map/prepare/pallas_call | solution.py:617
  2.9 9.5 %collective-permute-start = (bf16[64,69]{1,0:T(8,128)(2,1)S(1)}, bf16[64,69]{1,0:T(8,128)(2,1)S(1)}, u32[]{:S(2)}, u32[]{:S(2)}) collective-permute-start(bf16[64,69]{1,0:T(8,128)(2,1)S(1)} %get-tuple-element.28), channel_id=1, source_target_pairs={{0,124},{4,0},{8,4},{12,8},{16,12},{20,16},{24,20},{28,24},{32,28}... | collective-permute-start | bytes 26504 | tf_op jit(solution)/shard_map/ppermute | solution.py:519
  12.4 1.0 %collective-permute-start.1 = (bf16[64,69]{1,0:T(8,128)(2,1)S(1)}, bf16[64,69]{1,0:T(8,128)(2,1)S(1)}, u32[]{:S(2)}, u32[]{:S(2)}) collective-permute-start(bf16[64,69]{1,0:T(8,128)(2,1)S(1)} %get-tuple-element.29), channel_id=1, source_target_pairs={{0,127},{1,124},{2,125},{3,126},{4,3},{5,0},{6,1},{7,2},{8,7},{9,4... | collective-permute-start | bytes 26504 | tf_op jit(solution)/shard_map/ppermute | solution.py:525
  13.3 0.0 collective-permute-start.2
  13.3 4.6 %all-to-all-start = ((f32[128,1,64]{2,1,0:T(1,128)}), f32[128,1,64]{2,1,0:T(1,128)S(1)}, u32[]{:S(2)}, u32[]{:S(2)}) async-start(f32[128,1,64]{2,1,0:T(1,128)} %bitcast.10), calls=%async_computation | async-start | bytes 131072 | tf_op jit(solution)/shard_map/all_to_all | solution.py:633
  18.0 0.0 collective-permute-done.lon_piece
  18.0 0.0 collective-permute-done.1.far_piece
  18.0 0.0 collective-permute-done.2.lat_piece
  18.0 8.5 %forward.1 = (bf16[32,69]{1,0:T(8,128)(2,1)S(1)}, bf16[32,69]{1,0:T(8,128)(2,1)S(1)}, bf16[32,69]{1,0:T(8,128)(2,1)S(1)}, bf16[32,69]{1,0:T(8,128)(2,1)S(1)}, bf...) custom-call(f32[1,1]{1,0:T(1,128)} %bitcast.band_hbm, ...), custom_call_target="tpu_custom_call" | custom-call | flops 2500000000 | bytes 10000000 | tf_op jit(solution)/shard_map/forward/pallas_call | solution.py:544
  26.5 1.6 %collective-permute-start.3 = (bf16[32,69]{1,0:T(8,128)(2,1)S(1)}, bf16[32,69]{1,0:T(8,128)(2,1)S(1)}, u32[]{:S(2)}, u32[]{:S(2)}) collective-permute-start(bf16[32,69]{1,0:T(8,128)(2,1)S(1)} %get-tuple-element.32), channel_id=1, source_target_pairs={{0,4},{4,8},{8,12},{12,16},{16,20},{20,24},{24,28},{28,32},{32,36}... | collective-permute-start | bytes 13256 | tf_op jit(solution)/shard_map/ppermute | solution.py:519
  28.1 2.9 %collective-permute-start.4 = (bf16[32,69]{1,0:T(8,128)(2,1)S(1)}, bf16[32,69]{1,0:T(8,128)(2,1)S(1)}, u32[]{:S(2)}, u32[]{:S(2)}) collective-permute-start(bf16[32,69]{1,0:T(8,128)(2,1)S(1)} %get-tuple-element.33), channel_id=1, source_target_pairs={{0,5},{1,6},{2,7},{3,4},{4,9},{5,10},{6,11},{7,8},{8,13},{9,14},{1... | collective-permute-start | bytes 13256 | tf_op jit(solution)/shard_map/ppermute | solution.py:525
  31.0 0.0 collective-permute-start.5
  31.1 4.6 %collective-permute-done.3.lon_piece = bf16[32,69]{1,0:T(8,128)(2,1)S(1)} collective-permute-done((bf16[32,69]{1,0:T(8,128)(2,1)S(1)}, bf16[32,69]{1,0:T(8,128)(2,1)S(1)}, u32[]{:S(2)}, u32[]{:S(2)}) %collective-permute-start.3) | collective-permute-done | bytes 4448 | tf_op jit(solution)/shard_map/ppermute | solution.py:519
  35.7 1.3 %collective-permute-done.4.far_piece = bf16[32,69]{1,0:T(8,128)(2,1)S(1)} collective-permute-done((bf16[32,69]{1,0:T(8,128)(2,1)S(1)}, bf16[32,69]{1,0:T(8,128)(2,1)S(1)}, u32[]{:S(2)}, u32[]{:S(2)}) %collective-permute-start.4) | collective-permute-done | bytes 4448 | tf_op jit(solution)/shard_map/ppermute | solution.py:525
  36.9 0.0 collective-permute-done.5.lat_piece
  36.9 0.0 all-to-all-done
  36.9 0.0 copy-done
  36.9 1.4 %observe.1 = (f32[128,8]{1,0:T(8,128)}, f32[8,16,69]{2,1,0:T(8,128)S(1)}, bf16[32,69]{1,0:T(8,128)(2,1)S(1)}, bf16[32,69]{1,0:T(8,128)(2,1)S(1)}, bf16[32,69]{1,...) custom-call(f32[8,16,69]{2,1,0:T(8,128)S(1)} %copy-done, bf16[32,69]{1,0:T(8,128)(2,1)S(1)} %get-tuple-element.31.own_piece, ...), custom_call_target="tpu_custom_call" | custom-call | tf_op jit(solution)/shard_map/observe/pallas_call | solution.py:561
  38.3 1.4 %collective-permute-start.6 = (bf16[32,69]{1,0:T(8,128)(2,1)S(1)}, bf16[32,69]{1,0:T(8,128)(2,1)S(1)}, u32[]{:S(2)}, u32[]{:S(2)}) collective-permute-start(bf16[32,69]{1,0:T(8,128)(2,1)S(1)} %get-tuple-element.38), channel_id=1, source_target_pairs={{0,124},{4,0},{8,4},{12,8},{16,12},{20,16},{24,20},{28,24},{32,28}... | collective-permute-start | bytes 13256 | tf_op jit(solution)/shard_map/ppermute | solution.py:519
  39.7 2.5 %collective-permute-start.7 = (bf16[32,69]{1,0:T(8,128)(2,1)S(1)}, bf16[32,69]{1,0:T(8,128)(2,1)S(1)}, u32[]{:S(2)}, u32[]{:S(2)}) collective-permute-start(bf16[32,69]{1,0:T(8,128)(2,1)S(1)} %get-tuple-element.39), channel_id=1, source_target_pairs={{0,127},{1,124},{2,125},{3,126},{4,3},{5,0},{6,1},{7,2},{8,7},{9,4... | collective-permute-start | bytes 13256 | tf_op jit(solution)/shard_map/ppermute | solution.py:525
  42.3 0.0 collective-permute-start.8
  42.3 4.8 %all-to-all-start.1 = ((f32[128,1,8]{2,1,0:T(1,128)}), f32[128,1,8]{2,1,0:T(1,128)S(1)}, u32[]{:S(2)}, u32[]{:S(2)}) async-start(f32[128,1,8]{2,1,0:T(1,128)} %bitcast.16), calls=%async_computation.1 | async-start | bytes 131072 | tf_op jit(solution)/shard_map/all_to_all | solution.py:644
  47.1 0.0 collective-permute-done.6.lon_piece
  47.1 0.0 collective-permute-done.7.far_piece
  47.1 0.0 collective-permute-done.8.lat_piece
  47.2 0.0 copy-done.1
  47.2 0.0 copy-done.2
  47.2 0.0 copy-done.3
  47.2 7.8 %adjoint.1 = (bf16[32,69]{1,0:T(8,128)(2,1)S(1)}, bf16[32,69]{1,0:T(8,128)(2,1)S(1)}, bf16[32,69]{1,0:T(8,128)(2,1)S(1)}, bf16[32,69]{1,0:T(8,128)(2,1)S(1)}) custom-call(bf16[32,69]{1,0:T(8,128)(2,1)S(1)} %get-tuple-element.37.own_piece, bf16[32,69]{1,0:T(8,128)(2,1)S(1)} %collective-permute-done.6.lon_piece, ...), custom_call_target="tpu_custom_call" | custom-call | flops 1500000000 | bytes 10000000 | tf_op jit(solution)/shard_map/adjoint/pallas_call | solution.py:579
  55.0 1.6 %collective-permute-start.9 = (bf16[32,69]{1,0:T(8,128)(2,1)S(1)}, bf16[32,69]{1,0:T(8,128)(2,1)S(1)}, u32[]{:S(2)}, u32[]{:S(2)}) collective-permute-start(bf16[32,69]{1,0:T(8,128)(2,1)S(1)} %get-tuple-element.46), channel_id=1, source_target_pairs={{0,4},{4,8},{8,12},{12,16},{16,20},{20,24},{24,28},{28,32},{32,36}... | collective-permute-start | bytes 13256 | tf_op jit(solution)/shard_map/ppermute | solution.py:519
  56.6 2.9 %collective-permute-start.10 = (bf16[32,69]{1,0:T(8,128)(2,1)S(1)}, bf16[32,69]{1,0:T(8,128)(2,1)S(1)}, u32[]{:S(2)}, u32[]{:S(2)}) collective-permute-start(bf16[32,69]{1,0:T(8,128)(2,1)S(1)} %get-tuple-element.47), channel_id=1, source_target_pairs={{0,5},{1,6},{2,7},{3,4},{4,9},{5,10},{6,11},{7,8},{8,13},{9,14},{1... | collective-permute-start | bytes 13256 | tf_op jit(solution)/shard_map/ppermute | solution.py:525
  59.5 0.0 collective-permute-start.11
  59.5 0.0 all-to-all-done.1
  59.5 1.5 %unpack.1 = f32[1,512]{1,0:T(1,128)} custom-call(s32[1,512]{1,0:T(1,128)} %bitcast.32, f32[1,512]{1,0:T(1,128)S(1)} %get-tuple-element.52.slots_ref, f32[128,8]{1,0:T(8,128)S(1)} %bitcast.23), custom_call_target="tpu_custom_call" | custom-call | tf_op jit(solution)/shard_map/unpack/pallas_call | solution.py:662
  61.0 3.1 %collective-permute-done.9 = bf16[32,69]{1,0:T(8,128)(2,1)S(1)} collective-permute-done((bf16[32,69]{1,0:T(8,128)(2,1)S(1)}, bf16[32,69]{1,0:T(8,128)(2,1)S(1)}, u32[]{:S(2)}, u32[]{:S(2)}) %collective-permute-start.9) | collective-permute-done | bytes 4448 | tf_op jit(solution)/shard_map/ppermute | solution.py:519
  64.1 1.3 %collective-permute-done.10 = bf16[32,69]{1,0:T(8,128)(2,1)S(1)} collective-permute-done((bf16[32,69]{1,0:T(8,128)(2,1)S(1)}, bf16[32,69]{1,0:T(8,128)(2,1)S(1)}, u32[]{:S(2)}, u32[]{:S(2)}) %collective-permute-start.10) | collective-permute-done | bytes 4448 | tf_op jit(solution)/shard_map/ppermute | solution.py:525
  65.4 0.0 collective-permute-done.11
  65.4 0.6 convert_add_fusion
Async XLA Ops:
  0.6 36.3 %copy-start = (f32[8,16,69]{2,1,0:T(8,128)S(1)}, f32[8,16,69]{2,1,0:T(8,128)}, u32[]{:S(2)}) copy-start(f32[8,16,69]{2,1,0:T(8,128)} %direction_ref.3) | copy-start | bytes 105988
  0.6 46.5 %copy-start.1 = (bf16[1024,69]{0,1:T(8,128)(2,1)S(1)}, bf16[1024,69]{0,1:T(8,128)(2,1)}, u32[]{:S(2)}) copy-start(bf16[1024,69]{0,1:T(8,128)(2,1)} %param.25) | copy-start | bytes 423940
  0.7 46.5 %copy-start.2 = (f32[1024]{0:T(1024)S(1)}, f32[1024]{0:T(1024)}, u32[]{:S(2)}) copy-start(f32[1024]{0:T(1024)} %param.24) | copy-start | bytes 12292
  0.7 46.5 %copy-start.3 = (f32[16]{0:T(128)S(1)}, f32[16]{0:T(128)}, u32[]{:S(2)}) copy-start(f32[16]{0:T(128)} %param.22) | copy-start | bytes 196
  2.9 15.1 %collective-permute-start = (bf16[64,69]{1,0:T(8,128)(2,1)S(1)}, bf16[64,69]{1,0:T(8,128)(2,1)S(1)}, u32[]{:S(2)}, u32[]{:S(2)}) collective-permute-start(bf16[64,69]{1,0:T(8,128)(2,1)S(1)} %get-tuple-element.28), channel_id=1, source_target_pairs={{0,124},{4,0},{8,4},{12,8},{16,12},{20,16},{24,20},{28,24},{32,28}... | collective-permute-start | bytes 26504 | tf_op jit(solution)/shard_map/ppermute | solution.py:519
  12.4 5.6 %collective-permute-start.1 = (bf16[64,69]{1,0:T(8,128)(2,1)S(1)}, bf16[64,69]{1,0:T(8,128)(2,1)S(1)}, u32[]{:S(2)}, u32[]{:S(2)}) collective-permute-start(bf16[64,69]{1,0:T(8,128)(2,1)S(1)} %get-tuple-element.29), channel_id=1, source_target_pairs={{0,127},{1,124},{2,125},{3,126},{4,3},{5,0},{6,1},{7,2},{8,7},{9,4... | collective-permute-start | bytes 26504 | tf_op jit(solution)/shard_map/ppermute | solution.py:525
  13.3 4.7 %collective-permute-start.2 = (bf16[64,69]{1,0:T(8,128)(2,1)S(1)}, bf16[64,69]{1,0:T(8,128)(2,1)S(1)}, u32[]{:S(2)}, u32[]{:S(2)}) collective-permute-start(bf16[64,69]{1,0:T(8,128)(2,1)S(1)} %get-tuple-element.30), channel_id=1, source_target_pairs={{0,3},{1,0},{2,1},{3,2},{4,7},{5,4},{6,5},{7,6},{8,11},{9,8},{10,9... | collective-permute-start | bytes 26504 | tf_op jit(solution)/shard_map/ppermute | solution.py:518
  13.3 23.6 %all-to-all-start = ((f32[128,1,64]{2,1,0:T(1,128)}), f32[128,1,64]{2,1,0:T(1,128)S(1)}, u32[]{:S(2)}, u32[]{:S(2)}) async-start(f32[128,1,64]{2,1,0:T(1,128)} %bitcast.10), calls=%async_computation | async-start | bytes 131072 | tf_op jit(solution)/shard_map/all_to_all | solution.py:633
  26.5 9.1 %collective-permute-start.3 = (bf16[32,69]{1,0:T(8,128)(2,1)S(1)}, bf16[32,69]{1,0:T(8,128)(2,1)S(1)}, u32[]{:S(2)}, u32[]{:S(2)}) collective-permute-start(bf16[32,69]{1,0:T(8,128)(2,1)S(1)} %get-tuple-element.32), channel_id=1, source_target_pairs={{0,4},{4,8},{8,12},{12,16},{16,20},{20,24},{24,28},{28,32},{32,36}... | collective-permute-start | bytes 13256 | tf_op jit(solution)/shard_map/ppermute | solution.py:519
  28.1 8.8 %collective-permute-start.4 = (bf16[32,69]{1,0:T(8,128)(2,1)S(1)}, bf16[32,69]{1,0:T(8,128)(2,1)S(1)}, u32[]{:S(2)}, u32[]{:S(2)}) collective-permute-start(bf16[32,69]{1,0:T(8,128)(2,1)S(1)} %get-tuple-element.33), channel_id=1, source_target_pairs={{0,5},{1,6},{2,7},{3,4},{4,9},{5,10},{6,11},{7,8},{8,13},{9,14},{1... | collective-permute-start | bytes 13256 | tf_op jit(solution)/shard_map/ppermute | solution.py:525
  31.0 5.9 %collective-permute-start.5 = (bf16[32,69]{1,0:T(8,128)(2,1)S(1)}, bf16[32,69]{1,0:T(8,128)(2,1)S(1)}, u32[]{:S(2)}, u32[]{:S(2)}) collective-permute-start(bf16[32,69]{1,0:T(8,128)(2,1)S(1)} %get-tuple-element.34), channel_id=1, source_target_pairs={{0,1},{1,2},{2,3},{3,0},{4,5},{5,6},{6,7},{7,4},{8,9},{9,10},{10,1... | collective-permute-start | bytes 13256 | tf_op jit(solution)/shard_map/ppermute | solution.py:518
  38.3 8.8 %collective-permute-start.6 = (bf16[32,69]{1,0:T(8,128)(2,1)S(1)}, bf16[32,69]{1,0:T(8,128)(2,1)S(1)}, u32[]{:S(2)}, u32[]{:S(2)}) collective-permute-start(bf16[32,69]{1,0:T(8,128)(2,1)S(1)} %get-tuple-element.38), channel_id=1, source_target_pairs={{0,124},{4,0},{8,4},{12,8},{16,12},{20,16},{24,20},{28,24},{32,28}... | collective-permute-start | bytes 13256 | tf_op jit(solution)/shard_map/ppermute | solution.py:519
  39.7 7.4 %collective-permute-start.7 = (bf16[32,69]{1,0:T(8,128)(2,1)S(1)}, bf16[32,69]{1,0:T(8,128)(2,1)S(1)}, u32[]{:S(2)}, u32[]{:S(2)}) collective-permute-start(bf16[32,69]{1,0:T(8,128)(2,1)S(1)} %get-tuple-element.39), channel_id=1, source_target_pairs={{0,127},{1,124},{2,125},{3,126},{4,3},{5,0},{6,1},{7,2},{8,7},{9,4... | collective-permute-start | bytes 13256 | tf_op jit(solution)/shard_map/ppermute | solution.py:525
  42.3 4.9 %collective-permute-start.8 = (bf16[32,69]{1,0:T(8,128)(2,1)S(1)}, bf16[32,69]{1,0:T(8,128)(2,1)S(1)}, u32[]{:S(2)}, u32[]{:S(2)}) collective-permute-start(bf16[32,69]{1,0:T(8,128)(2,1)S(1)} %get-tuple-element.40), channel_id=1, source_target_pairs={{0,3},{1,0},{2,1},{3,2},{4,7},{5,4},{6,5},{7,6},{8,11},{9,8},{10,9... | collective-permute-start | bytes 13256 | tf_op jit(solution)/shard_map/ppermute | solution.py:518
  42.3 17.2 %all-to-all-start.1 = ((f32[128,1,8]{2,1,0:T(1,128)}), f32[128,1,8]{2,1,0:T(1,128)S(1)}, u32[]{:S(2)}, u32[]{:S(2)}) async-start(f32[128,1,8]{2,1,0:T(1,128)} %bitcast.16), calls=%async_computation.1 | async-start | bytes 131072 | tf_op jit(solution)/shard_map/all_to_all | solution.py:644
  55.0 9.1 %collective-permute-start.9 = (bf16[32,69]{1,0:T(8,128)(2,1)S(1)}, bf16[32,69]{1,0:T(8,128)(2,1)S(1)}, u32[]{:S(2)}, u32[]{:S(2)}) collective-permute-start(bf16[32,69]{1,0:T(8,128)(2,1)S(1)} %get-tuple-element.46), channel_id=1, source_target_pairs={{0,4},{4,8},{8,12},{12,16},{16,20},{20,24},{24,28},{28,32},{32,36}... | collective-permute-start | bytes 13256 | tf_op jit(solution)/shard_map/ppermute | solution.py:519
  56.6 8.8 %collective-permute-start.10 = (bf16[32,69]{1,0:T(8,128)(2,1)S(1)}, bf16[32,69]{1,0:T(8,128)(2,1)S(1)}, u32[]{:S(2)}, u32[]{:S(2)}) collective-permute-start(bf16[32,69]{1,0:T(8,128)(2,1)S(1)} %get-tuple-element.47), channel_id=1, source_target_pairs={{0,5},{1,6},{2,7},{3,4},{4,9},{5,10},{6,11},{7,8},{8,13},{9,14},{1... | collective-permute-start | bytes 13256 | tf_op jit(solution)/shard_map/ppermute | solution.py:525
  59.5 5.9 %collective-permute-start.11 = (bf16[32,69]{1,0:T(8,128)(2,1)S(1)}, bf16[32,69]{1,0:T(8,128)(2,1)S(1)}, u32[]{:S(2)}, u32[]{:S(2)}) collective-permute-start(bf16[32,69]{1,0:T(8,128)(2,1)S(1)} %get-tuple-element.48), channel_id=1, source_target_pairs={{0,1},{1,2},{2,3},{3,0},{4,5},{5,6},{6,7},{7,4},{8,9},{9,10},{10,1... | collective-permute-start | bytes 13256 | tf_op jit(solution)/shard_map/ppermute | solution.py:518
